TPU v7x, 32 devices: a whole 2x2x4 slice. The times are simulated.
32 devices in a mesh: dp: 2 (over x), batch: 4 (over z), head: 4 (over y, core).
Axes of the slice: x: 2, y: 2, z: 4, core: 2. Of those that a mesh axis runs over, the one named last changes fastest.
Arguments:
- block_in: bfloat16 [32768, 768], P(('dp', 'batch', 'head')), may hold values from -6 to 6
- cotangent: bfloat16 [32768, 768], P(('dp', 'batch', 'head')), may hold values from -6 to 6
- seq_len: int32 [8, 2], P(('dp', 'batch')), may hold values from 1024 to 2048, as said below
- w_qkv: float32 [768, 3, 768], P(('dp', 'batch'), None, 'head'), may hold values from -0.21875 to 0.21875
- w_out: float32 [768, 768], P('head', ('dp', 'batch')), may hold values from -6 to 6
- w_feat: float32 [2, 12, 4096], P(None, 'head', ('dp', 'batch')), may hold values from -1.5 to 1.5
- w_fc: float32 [768, 3072], P(None, ('dp', 'batch', 'head')), may hold values from -0.36084392 to 0.36084392
- w_proj: float32 [3072, 768], P(('dp', 'batch', 'head')), may hold values from -0.109375 to 0.109375
- norm_params: float32 [4, 768], replicated, may hold values from -0.6 to 1.8, as said below
- first_qkv: float32 [768, 3, 768], P(('dp', 'batch'), None, 'head'), may hold values from -0.00024414062 to 0.00024414062
- second_qkv: float32 [768, 3, 768], P(('dp', 'batch'), None, 'head'), may hold values from 7.326656e-09 to 2.9320555e-08
- first_out: float32 [768, 768], P('head', ('dp', 'batch')), may hold values from -0.00024414062 to 0.00024414062
- second_out: float32 [768, 768], P('head', ('dp', 'batch')), may hold values from 1.7689836e-10 to 7.0759343e-10
- first_feat: float32 [2, 12, 4096], P(None, 'head', ('dp', 'batch')), may hold values from -0.00024414062 to 0.00024414062
- second_feat: float32 [2, 12, 4096], P(None, 'head', ('dp', 'batch')), may hold values from 7.326656e-09 to 2.9320555e-08
- first_fc: float32 [768, 3072], P(None, ('dp', 'batch', 'head')), may hold values from -0.00024414062 to 0.00024414062
- second_fc: float32 [768, 3072], P(None, ('dp', 'batch', 'head')), may hold values from 8.176326e-10 to 3.273316e-09
- first_proj: float32 [3072, 768], P(('dp', 'batch', 'head')), may hold values from -0.00024414062 to 0.00024414062
- second_proj: float32 [3072, 768], P(('dp', 'batch', 'head')), may hold values from 7.326656e-09 to 2.9320555e-08
- first_norms: float32 [4, 768], replicated, may hold values from -0.00024414062 to 0.00024414062
- second_norms: float32 [4, 768], replicated, may hold values from 7.326656e-09 to 2.9320555e-08
Outputs:
- grad_norm: float32 [], replicated
- block_out: bfloat16 [32768, 768], P(('dp', 'batch', 'head'))
- block_in_grad: float32 [32768, 768], P(('dp', 'batch', 'head'))
- new_qkv: float32 [768, 3, 768], P(('dp', 'batch'), None, 'head')
- new_out: float32 [768, 768], P('head', ('dp', 'batch'))
- new_feat: float32 [2, 12, 4096], P(None, 'head', ('dp', 'batch'))
- new_fc: float32 [768, 3072], P(None, ('dp', 'batch', 'head'))
- new_proj: float32 [3072, 768], P(('dp', 'batch', 'head'))
- new_norms: float32 [4, 768], replicated
- new_first_qkv: float32 [768, 3, 768], P(('dp', 'batch'), None, 'head')
- new_first_out: float32 [768, 768], P('head', ('dp', 'batch'))
- new_first_feat: float32 [2, 12, 4096], P(None, 'head', ('dp', 'batch'))
- new_first_fc: float32 [768, 3072], P(None, ('dp', 'batch', 'head'))
- new_first_proj: float32 [3072, 768], P(('dp', 'batch', 'head'))
- new_first_norms: float32 [4, 768], replicated
- new_second_qkv: float32 [768, 3, 768], P(('dp', 'batch'), None, 'head')
- new_second_out: float32 [768, 768], P('head', ('dp', 'batch'))
- new_second_feat: float32 [2, 12, 4096], P(None, 'head', ('dp', 'batch'))
- new_second_fc: float32 [768, 3072], P(None, ('dp', 'batch', 'head'))
- new_second_proj: float32 [3072, 768], P(('dp', 'batch', 'head'))
- new_second_norms: float32 [2, 768], replicated
- new_second_late_norm: float32 [2, 768], replicated
- copy_qkv: bfloat16 [768, 3, 768], P(('dp', 'batch'), None, 'head')
- copy_out: bfloat16 [768, 768], P('head', ('dp', 'batch'))
- copy_feat: bfloat16 [2, 12, 4096], P(None, 'head', ('dp', 'batch'))
- copy_fc: bfloat16 [768, 3072], P(None, ('dp', 'batch', 'head'))
- copy_proj: bfloat16 [3072, 768], P(('dp', 'batch', 'head'))
- copy_norms: bfloat16 [4, 768], replicated
Inputs may be any that keep to these rules, and one draw needn't show every extreme that they name: `seq_len`: every length is a multiple of 64; a group's two lengths together are at most 4096. `norm_params`: rows 0 and 2 are positive gains, rows 1 and 3 shifts.
All inputs are finite; a program needn't handle non-finite values.
Results may differ from a plain program's by a relative error of at most 0.02.
Values may be sent and summed in bfloat16 or wider, within the bound.
A program may use at most 256 MiB of HBM per device.

v0:
```python
import jax
import jax.numpy as jnp
from jax import lax
from jax.sharding import PartitionSpec as P

HD = 64
BLOCK = 64
SLOTS = 2
STEP = 8


norm_eps = 1e-05
beta_one = 0.9
beta_two = 0.95
adam_eps = 1e-08
clip_limit = 1.0
highest = lax.Precision.HIGHEST


def rounded(values):
    return lax.optimization_barrier(values.astype(jnp.bfloat16)).astype(jnp.float32)


def contract_rows(left, right):
    return lax.dot_general(
        left, right, (((0,), (0,)), ((), ())), preferred_element_type=jnp.float32
    )


def against(left, right):
    return lax.dot_general(
        left, right, (((1,), (1,)), ((), ())), preferred_element_type=jnp.float32
    )


def layer_norm(values, gain_row, shifts):
    center = values - jnp.mean(values, axis=-1, keepdims=True)
    spread = jnp.mean(center * center, axis=-1, keepdims=True)
    return center * lax.rsqrt(spread + norm_eps) * gain_row + shifts


def gelu_tanh(values):
    return jax.nn.gelu(values, approximate=True)


def feature_softmax(scaled):
    return jnp.concatenate(
        [jax.nn.softmax(scaled, axis=-1), jax.nn.softmax(-scaled, axis=-1)], axis=-1
    )


def block_layout(lengths, total_rows):
    blocks = total_rows // BLOCK
    begins = jnp.arange(blocks, dtype=jnp.int32) * BLOCK
    endings = jnp.cumsum(lengths)
    doc_index = jnp.sum((begins[:, None] >= endings[None, :]).astype(jnp.int32), axis=1)
    earlier = (
        (doc_index[:, None] == doc_index[None, :])
        & (begins[None, :] < begins[:, None])
        & (doc_index[:, None] < SLOTS)
    )
    live_rows = (jnp.arange(total_rows, dtype=jnp.int32) < endings[-1]).astype(jnp.float32)
    return (earlier.astype(jnp.float32), live_rows)


def linear_core(queries, key_rows, values, earlier, live_rows):
    total_rows, heads, feat = queries.shape
    blocks = total_rows // BLOCK
    query_blocks = queries.reshape(blocks, BLOCK, heads, feat)
    key_blocks = key_rows.reshape(blocks, BLOCK, heads, feat)
    value_blocks = values.reshape(blocks, BLOCK, heads, -1)
    causal = jnp.tril(jnp.ones((BLOCK, BLOCK), jnp.float32))
    scores = jnp.einsum("nihf,njhf->nhij", query_blocks, key_blocks, precision=highest) * causal
    numerator = jnp.einsum("nhij,njhd->nihd", scores, value_blocks, precision=highest)
    denominator = jnp.einsum("nhij->nih", scores)
    states = jnp.einsum("njhf,njhd->nhfd", key_blocks, value_blocks, precision=highest)
    totals = jnp.sum(key_blocks, axis=1)
    prior_state = jnp.einsum("nm,mhfd->nhfd", earlier, states, precision=highest)
    prior_sum = jnp.einsum("nm,mhf->nhf", earlier, totals, precision=highest)
    numerator = numerator + jnp.einsum(
        "nihf,nhfd->nihd", query_blocks, prior_state, precision=highest
    )
    denominator = denominator + jnp.einsum(
        "nihf,nhf->nih", query_blocks, prior_sum, precision=highest
    )
    denominator = denominator + (1.0 - live_rows.reshape(blocks, BLOCK, 1))
    return (numerator / denominator[..., None]).reshape(total_rows, heads, -1)


def adamw_update(master, first_mom, second_mom, grad_in, factor, step_rate, decay_rate):
    clipped = grad_in * factor
    first_new = beta_one * first_mom + (1.0 - beta_one) * clipped
    second_new = beta_two * second_mom + (1.0 - beta_two) * clipped * clipped
    direction = (
        first_new
        / (1.0 - beta_one**STEP)
        / (jnp.sqrt(second_new / (1.0 - beta_two**STEP)) + adam_eps)
    )
    master_new = master - step_rate * (direction + decay_rate * master)
    return (master_new, first_new, second_new)


def on_device(
    block_in,
    cotangent,
    seq_len,
    w_qkv,
    w_out,
    w_feat,
    w_fc,
    w_proj,
    norm_params,
    first_qkv,
    second_qkv,
    first_out,
    second_out,
    first_feat,
    second_feat,
    first_fc,
    second_fc,
    first_proj,
    second_proj,
    first_norms,
    second_norms,
):
    model_width = block_in.shape[1]
    heads_here = w_feat.shape[1]
    norm_low = rounded(norm_params)
    qkv_full, out_full, feat_full, fc_part, proj_part = (
        lax.all_gather(w_qkv.astype(jnp.bfloat16), ("dp", "batch"), axis=0, tiled=True),
        lax.all_gather(w_out.astype(jnp.bfloat16), ("dp", "batch"), axis=1, tiled=True),
        lax.all_gather(w_feat.astype(jnp.bfloat16), ("dp", "batch"), axis=2, tiled=True),
        lax.all_gather(w_fc.astype(jnp.bfloat16), ("dp", "batch"), axis=1, tiled=True),
        lax.all_gather(w_proj.astype(jnp.bfloat16), ("dp", "batch"), axis=0, tiled=True),
    )
    qkv_matrix = qkv_full.reshape(model_width, -1)
    feat_lowp = feat_full.reshape(2, heads_here, HD, HD)
    feat_maps = feat_lowp.astype(jnp.float32)
    inputs_f = block_in.astype(jnp.float32)
    normed, first_back = jax.vjp(layer_norm, inputs_f, norm_low[0], norm_low[1])
    normed_b = normed.astype(jnp.bfloat16)
    normed_all = lax.all_gather(normed_b, "head", axis=0, tiled=True)
    group_rows = normed_all.shape[0]
    earlier, live_rows = block_layout(seq_len[0], group_rows)
    qkv_rows = jnp.dot(normed_all, qkv_matrix, preferred_element_type=jnp.float32).astype(
        jnp.bfloat16
    )
    qkv_heads = qkv_rows.reshape(group_rows, 3, heads_here, HD)
    qkv_split = qkv_heads.astype(jnp.float32)
    scaled_q = jnp.einsum(
        "rhd,hde->rhe", qkv_heads[:, 0], feat_lowp[0], preferred_element_type=jnp.float32
    )
    scaled_k = jnp.einsum(
        "rhd,hde->rhe", qkv_heads[:, 1], feat_lowp[1], preferred_element_type=jnp.float32
    )

    def feature_pair(query_scaled, key_scaled):
        live_col = live_rows[:, None, None]
        return (feature_softmax(query_scaled) * live_col, feature_softmax(key_scaled) * live_col)

    (query_feat, key_feat), feature_back = jax.vjp(feature_pair, scaled_q, scaled_k)

    def attend(queries, key_rows, values):
        return linear_core(queries, key_rows, values, earlier, live_rows)

    attn_mixed, attend_back = jax.vjp(
        attend, rounded(query_feat), rounded(key_feat), qkv_split[:, 2]
    )
    mixed_b = attn_mixed.reshape(group_rows, -1).astype(jnp.bfloat16)
    attended = lax.psum_scatter(
        jnp.dot(mixed_b, out_full, preferred_element_type=jnp.float32).astype(jnp.bfloat16),
        "head",
        scatter_dimension=0,
        tiled=True,
    ).astype(jnp.float32)
    middle = inputs_f + attended
    hidden, second_back = jax.vjp(layer_norm, middle, norm_low[2], norm_low[3])
    hidden_b = hidden.astype(jnp.bfloat16)
    fc_whole, proj_whole = (
        lax.all_gather(fc_part, "head", axis=1, tiled=True),
        lax.all_gather(proj_part, "head", axis=0, tiled=True),
    )
    pre_act = jnp.dot(hidden_b, fc_whole, preferred_element_type=jnp.float32)
    active, active_back = jax.vjp(gelu_tanh, pre_act)
    active_b = active.astype(jnp.bfloat16)
    branch = jnp.dot(active_b, proj_whole, preferred_element_type=jnp.float32)
    grad_proj_whole = contract_rows(active_b, cotangent)
    d_pre = active_back(against(cotangent, proj_whole))[0].astype(jnp.bfloat16)
    grad_fc_whole = contract_rows(hidden_b, d_pre)
    d_hidden = against(d_pre, fc_whole)
    grad_fc, grad_proj = (
        lax.psum_scatter(
            grad_fc_whole.astype(jnp.bfloat16), "head", scatter_dimension=1, tiled=True
        ).astype(jnp.float32),
        lax.psum_scatter(
            grad_proj_whole.astype(jnp.bfloat16), "head", scatter_dimension=0, tiled=True
        ).astype(jnp.float32),
    )
    block_out = (middle + branch).astype(jnp.bfloat16)
    d_middle_norm, gain_two, shift_two = second_back(d_hidden)
    d_middle = cotangent.astype(jnp.float32) + d_middle_norm
    d_attended = lax.all_gather(d_middle.astype(jnp.bfloat16), "head", axis=0, tiled=True)
    grad_out = contract_rows(mixed_b, d_attended)
    d_mixed = rounded(against(d_attended, out_full))
    d_query, d_key, d_value = attend_back(d_mixed.reshape(group_rows, heads_here, HD))
    d_query_scaled, d_key_scaled = feature_back((rounded(d_query), rounded(d_key)))
    d_qin = jnp.einsum("rhe,hde->rhd", d_query_scaled, feat_maps[0], precision=highest)
    d_kin = jnp.einsum("rhe,hde->rhd", d_key_scaled, feat_maps[1], precision=highest)
    grad_feat = jnp.stack(
        [
            jnp.einsum("rhd,rhe->hde", qkv_split[:, 0], d_query_scaled, precision=highest),
            jnp.einsum("rhd,rhe->hde", qkv_split[:, 1], d_key_scaled, precision=highest),
        ]
    )
    d_qkv = jnp.stack([d_qin, d_kin, d_value], axis=1).reshape(group_rows, -1).astype(jnp.bfloat16)
    grad_qkv = contract_rows(normed_all, d_qkv).reshape(model_width, 3, -1)
    d_normed = lax.psum_scatter(
        against(d_qkv, qkv_matrix).astype(jnp.bfloat16), "head", scatter_dimension=0, tiled=True
    ).astype(jnp.float32)
    d_inputs, gain_one, shift_one = first_back(d_normed)
    block_in_grad = d_middle + d_inputs
    reduced = (
        lax.psum_scatter(
            grad_qkv.astype(jnp.bfloat16), ("dp", "batch"), scatter_dimension=0, tiled=True
        ).astype(jnp.float32),
        lax.psum_scatter(
            grad_out.astype(jnp.bfloat16), ("dp", "batch"), scatter_dimension=1, tiled=True
        ).astype(jnp.float32),
        lax.psum_scatter(
            grad_feat.reshape(2, heads_here, -1).astype(jnp.bfloat16),
            ("dp", "batch"),
            scatter_dimension=2,
            tiled=True,
        ).astype(jnp.float32),
        lax.psum_scatter(
            grad_fc.astype(jnp.bfloat16), ("dp", "batch"), scatter_dimension=1, tiled=True
        ).astype(jnp.float32),
        lax.psum_scatter(
            grad_proj.astype(jnp.bfloat16), ("dp", "batch"), scatter_dimension=0, tiled=True
        ).astype(jnp.float32),
    )
    partial_sq = jnp.float32(0.0)
    for member in reduced:
        partial_sq = partial_sq + jnp.sum(member * member)
    norm_terms = jnp.stack([gain_one, shift_one, gain_two, shift_two])
    norm_grads, squares = lax.psum((norm_terms, partial_sq), ("dp", "batch", "head"))
    grad_norm = jnp.sqrt(squares + jnp.sum(norm_grads * norm_grads))
    factor = clip_limit / jnp.maximum(grad_norm, clip_limit)
    up_qkv = adamw_update(w_qkv, first_qkv, second_qkv, reduced[0], factor, 0.02, 0.1)
    up_out = adamw_update(w_out, first_out, second_out, reduced[1], factor, 0.4, 0.1)
    up_feat = adamw_update(w_feat, first_feat, second_feat, reduced[2], factor, 0.15, 0.1)
    up_fc = adamw_update(w_fc, first_fc, second_fc, reduced[3], factor, 0.02, 0.1)
    up_proj = adamw_update(w_proj, first_proj, second_proj, reduced[4], factor, 0.01, 0.1)
    up_norms = adamw_update(norm_params, first_norms, second_norms, norm_grads, factor, 0.3, 0.0)
    return (
        grad_norm,
        block_out,
        block_in_grad,
        up_qkv[0],
        up_out[0],
        up_feat[0],
        up_fc[0],
        up_proj[0],
        up_norms[0],
        up_qkv[1],
        up_out[1],
        up_feat[1],
        up_fc[1],
        up_proj[1],
        up_norms[1],
        up_qkv[2],
        up_out[2],
        up_feat[2],
        up_fc[2],
        up_proj[2],
        up_norms[2][:2],
        up_norms[2][2:],
        up_qkv[0].astype(jnp.bfloat16),
        up_out[0].astype(jnp.bfloat16),
        up_feat[0].astype(jnp.bfloat16),
        up_fc[0].astype(jnp.bfloat16),
        up_proj[0].astype(jnp.bfloat16),
        up_norms[0].astype(jnp.bfloat16),
    )


def solution(mesh):
    in_specs = (
        P(("dp", "batch", "head"), None),
        P(("dp", "batch", "head"), None),
        P(("dp", "batch"), None),
        P(("dp", "batch"), None, "head"),
        P("head", ("dp", "batch")),
        P(None, "head", ("dp", "batch")),
        P(None, ("dp", "batch", "head")),
        P(("dp", "batch", "head"), None),
        P(),
        P(("dp", "batch"), None, "head"),
        P(("dp", "batch"), None, "head"),
        P("head", ("dp", "batch")),
        P("head", ("dp", "batch")),
        P(None, "head", ("dp", "batch")),
        P(None, "head", ("dp", "batch")),
        P(None, ("dp", "batch", "head")),
        P(None, ("dp", "batch", "head")),
        P(("dp", "batch", "head"), None),
        P(("dp", "batch", "head"), None),
        P(),
        P(),
    )
    out_specs = (
        P(),
        P(("dp", "batch", "head"), None),
        P(("dp", "batch", "head"), None),
        P(("dp", "batch"), None, "head"),
        P("head", ("dp", "batch")),
        P(None, "head", ("dp", "batch")),
        P(None, ("dp", "batch", "head")),
        P(("dp", "batch", "head"), None),
        P(),
        P(("dp", "batch"), None, "head"),
        P("head", ("dp", "batch")),
        P(None, "head", ("dp", "batch")),
        P(None, ("dp", "batch", "head")),
        P(("dp", "batch", "head"), None),
        P(),
        P(("dp", "batch"), None, "head"),
        P("head", ("dp", "batch")),
        P(None, "head", ("dp", "batch")),
        P(None, ("dp", "batch", "head")),
        P(("dp", "batch", "head"), None),
        P(),
        P(),
        P(("dp", "batch"), None, "head"),
        P("head", ("dp", "batch")),
        P(None, "head", ("dp", "batch")),
        P(None, ("dp", "batch", "head")),
        P(("dp", "batch", "head"), None),
        P(),
    )
    return jax.shard_map(
        on_device, mesh=mesh, in_specs=in_specs, out_specs=out_specs, check_vma=False
    )
```

profile of v0, /device:TPU:0, one launch (start us, length us, event | category | flops | bytes accessed | tf_op | source)
XLA Modules:
  0.0 1131.8 jit_solution(8184118383744627510)
XLA Ops:
  20.4 28.7 %all_gather.31 = bf16[2,3,4096]{2,0,1:T(2,128)(2,1)S(1)} all-gather(bf16[2,3,512]{2,0,1:T(2,128)(2,1)S(1)} %convert_element_type.190), channel_id=1, replica_groups=mesh['dp'=2,'batch'=4,'head'=4] {'dp','batch'}, dimensions={2}, use_global_device_ids=true | all-gather | bytes 55296 | tf_op jit(solution)/shard_map/all_gather | solution.py:132
  51.0 32.3 %all_gather.32 = bf16[192,768]{0,1:T(8,128)(2,1)S(1)} all-gather(bf16[192,96]{0,1:T(8,128)(2,1)S(1)} %copy.266), channel_id=1, replica_groups=mesh['dp'=2,'batch'=4,'head'=4] {'dp','batch'}, dimensions={1}, use_global_device_ids=true | all-gather | bytes 331776 | tf_op jit(solution)/shard_map/all_gather | solution.py:131
  83.3 46.7 %all_gather.30 = bf16[768,3,192]{2,1,0:T(4,128)(2,1)S(1)} all-gather(bf16[96,3,192]{2,1,0:T(4,128)(2,1)S(1)} %copy.247), channel_id=1, replica_groups=mesh['dp'=2,'batch'=4,'head'=4] {'dp','batch'}, dimensions={0}, use_global_device_ids=true | all-gather | bytes 995328 | tf_op jit(solution)/shard_map/all_gather | solution.py:130
  196.4 10.6 fusion.28
  207.0 11.8 %fusion.35 = f32[64,3,64,64]{3,2,1,0:T(8,128)S(1)} fusion(f32[64,3,128,64]{2,0,3,1:T(8,128)} %fusion.28, bf16[64,64,3,128]{3,1,0,2:T(8,128)(2,1)S(1)} %bitcast.204), kind=kOutput, calls=%fused_computation.54 | convolution fusion | flops 1207959552 | bytes 12582912 | tf_op jit(solution)/shard_map/jvp(nihf,nhfd->nihd)/dot_general | solution.py:80
  229.2 9.1 fusion.22
  253.9 57.9 %reduce-scatter.16.cloned.1.call-done = bf16[1024,768]{1,0:T(8,128)(2,1)} async-done(((bf16[4096,768]{1,0:T(8,128)(2,1)}), bf16[1024,768]{1,0:T(8,128)(2,1)}) %reduce-scatter.16.cloned.1.call-update) | async-done | bytes 1572880 | tf_op jit(solution)/shard_map/reduce_scatter | solution.py:170
  315.2 35.6 %all-gather.15.cloned.1.call-done = bf16[768,3072]{0,1:T(8,128)(2,1)} async-done(((bf16[768,768]{0,1:T(8,128)(2,1)}), bf16[768,3072]{0,1:T(8,128)(2,1)}) %all-gather.15.cloned.1.call-update) | async-done | bytes 4718608 | tf_op jit(solution)/shard_map/all_gather | solution.py:180
  350.8 11.6 %fusion.137 = f32[1024,3072]{1,0:T(8,128)} fusion(bf16[768,3072]{0,1:T(8,128)(2,1)} %all-gather.15.cloned.1.call-done, bf16[1024,768]{1,0:T(8,128)(2,1)S(1)} %copy-done.24, bf16[1024,768]{1,0:T(8,128)(2,1)S(1)} %copy-done, f32[768]{0:T(1024)} %get-tuple-element.181, f32[768]{0:T(1024)} %get-tuple-element.180, f32[1024]{0:T(1024)} %fusion.135, ...), kind=kOutput, calls=%fused_computation.244 | convolution fusion | flops 4838129664 | bytes 20461568 | tf_op jit(solution)/shard_map/dot_general | solution.py:183
  362.5 27.4 %all-gather.11.cloned.1.call-done = bf16[3072,768]{1,0:T(8,128)(2,1)} async-done(((bf16[768,768]{1,0:T(8,128)(2,1)}), bf16[3072,768]{1,0:T(8,128)(2,1)}) %all-gather.11.cloned.1.call-update) | async-done | bytes 4718608 | tf_op jit(solution)/shard_map/all_gather | solution.py:181
  389.8 15.5 %fusion.10 = bf16[1024,3072]{1,0:T(8,128)(2,1)S(1)} fusion(f32[1024,3072]{1,0:T(8,128)} %fusion.137, bf16[1024,768]{1,0:T(8,128)(2,1)} %param.22, bf16[3072,768]{1,0:T(8,128)(2,1)} %all-gather.11.cloned.1.call-done), kind=kOutput, calls=%fused_computation.12 | convolution fusion | flops 4894752768 | bytes 25165824 | tf_op jit(solution)/shard_map/dot_general | solution.py:31
  416.8 10.3 convolution_convert_fusion.4
  430.1 11.6 %convolution_convert_fusion.3 = bf16[3072,768]{1,0:T(8,128)(2,1)} fusion(bf16[1024,768]{1,0:T(8,128)(2,1)S(1)} %copy-done.28, f32[1024,3072]{1,0:T(8,128)} %fusion.137), kind=kOutput, calls=%fused_computation.74 | convolution fusion | flops 4862509056 | bytes 18874368 | tf_op jit(solution)/shard_map/dot_general | solution.py:25
  441.8 21.5 %all-gather.17.cloned.1.call-done = bf16[4096,768]{1,0:T(8,128)(2,1)} async-done(((bf16[1024,768]{1,0:T(8,128)(2,1)}), bf16[4096,768]{1,0:T(8,128)(2,1)}) %all-gather.17.cloned.1.call-update) | async-done | bytes 6291472 | tf_op jit(solution)/shard_map/all_gather | solution.py:202
  472.6 25.7 %fusion.20 = f32[64,3,64,128]{3,2,1,0:T(8,128)} fusion(f32[64,3,128,64]{2,0,3,1:T(8,128)} %fusion.28, f32[64,64,3,64]{1,0,3,2:T(8,128)} %reshape.288, f32[64,64,3]{1,2,0:T(4,128)S(1)} %copy-done.76), kind=kOutput, calls=%fused_computation.29 | convolution fusion | flops 1208745984 | bytes 15777792 | tf_op jit(solution)/shard_map/transpose(jvp(nihf,nhfd->nihd))/dot_general | solution.py:80
  498.4 10.8 fusion.18
  509.1 11.0 fusion.16
  520.2 12.0 %fusion.23 = f32[64,64,3]{1,2,0:T(4,128)S(1)} fusion(f32[64,64,3,64]{1,0,3,2:T(8,128)} %reshape.288, f32[64,64,3]{1,2,0:T(4,128)S(1)} %copy-done.55, f32[64,3,64,64]{3,2,1,0:T(8,128)} %get-tuple-element.233, f32[64,3,64,64]{3,2,1,0:T(8,128)S(1)} %bitcast.211), kind=kLoop, calls=%fused_computation.34 | loop fusion | flops 3133440 | bytes 9535488 | tf_op jit(solution)/shard_map/transpose(jvp())/reduce_sum | solution.py:87
  535.2 10.4 fusion.26
  551.5 11.9 %fusion.13 = bf16[64,64,3,128]{3,1,2,0:T(8,128)(2,1)S(1)} fusion(f32[64,3,64,128]{3,2,1,0:T(8,128)} %fusion.41, f32[64,3,128]{2,1,0:T(4,128)S(1)} %copy.279, bf16[64,64,3,64]{3,1,2,0:T(8,128)(2,1)} %copy.273, f32[64,3,128,64]{2,0,3,1:T(8,128)S(1)} %fusion.26), kind=kOutput, calls=%fused_computation.22 | convolution fusion | flops 1212678144 | bytes 17399808 | tf_op jit(solution)/shard_map/transpose(jvp(njhf,njhd->nhfd))/dot_general | solution.py:76
  570.8 9.6 fusion.61
  636.8 19.5 %fusion.14 = f32[64,3,64,64]{3,2,1,0:T(8,128)} fusion(f32[64,3,64,64]{2,3,1,0:T(8,128)} %get-tuple-element.231, f32[64,64]{0,1:T(8,128)S(1)} %copy-done.53, f32[64,64,3,64]{1,0,3,2:T(8,128)} %reshape.288, f32[64,64,3]{1,2,0:T(4,128)S(1)} %copy-done.77), kind=kOutput, calls=%fused_computation.23 | convolution fusion | flops 605552640 | bytes 9502720 | tf_op jit(solution)/shard_map/transpose(jvp(nhij,njhd->nihd))/dot_general | solution.py:74
  656.3 13.4 %add_bitcast_fusion = bf16[64,64,3,64]{1,3,2,0:T(8,128)(2,1)} fusion(f32[64,3,64,64]{3,2,1,0:T(8,128)} %fusion.14, f32[64,3,128,64]{2,0,3,1:T(8,128)S(1)} %bitcast.203, bf16[64,64,3,128]{3,1,0,2:T(8,128)(2,1)S(1)} %bitcast.201), kind=kOutput, calls=%fused_computation.41 | convolution fusion | flops 1209532416 | bytes 14155776 | tf_op jit(solution)/shard_map/transpose(jvp(njhf,njhd->nhfd))/dot_general | solution.py:76
  690.9 8.2 fusion.84
  702.4 9.5 convolution_convert_fusion
  717.6 12.7 %add_convert_fusion.1 = bf16[1024,768]{1,0:T(8,128)(2,1)} fusion(bf16[1024,768]{1,0:T(8,128)(2,1)S(1)} %copy-done.25, bf16[1024,768]{1,0:T(8,128)(2,1)S(1)} %copy-done.1, bf16[3072,768]{1,0:T(8,128)(2,1)} %all-gather.11.cloned.1.call-done, f32[1024,3072]{1,0:T(8,128)} %fusion.137), kind=kOutput, calls=%fused_computation.98 | convolution fusion | flops 4864081920 | bytes 22020096 | tf_op jit(solution)/shard_map/dot_general | solution.py:186
  735.7 61.4 %reduce-scatter.28.cloned.1.call-done = bf16[96,192]{1,0:T(8,128)(2,1)} async-done(((bf16[768,192]{1,0:T(8,128)(2,1)}), bf16[96,192]{1,0:T(8,128)(2,1)}) %reduce-scatter.28.cloned.1.call-update) | async-done | bytes 36880
  798.6 65.3 %reduce-scatter.18.cloned.1.call-done = bf16[96,3,192]{2,0,1:T(8,128)(2,1)} async-done(((bf16[768,3,192]{2,0,1:T(8,128)(2,1)}), bf16[96,3,192]{2,0,1:T(8,128)(2,1)}) %reduce-scatter.18.cloned.1.call-update) | async-done | bytes 110608 | tf_op jit(solution)/shard_map/reduce_scatter | solution.py:223
  867.5 62.8 %reduce-scatter.32.cloned.1.call-done = bf16[96,768]{1,0:T(8,128)(2,1)} async-done(((bf16[768,768]{1,0:T(8,128)(2,1)}), bf16[96,768]{1,0:T(8,128)(2,1)}) %reduce-scatter.32.cloned.1.call-update) | async-done | bytes 147472
  932.8 63.8 %reduce-scatter.24.cloned.1.call-done = bf16[96,768]{1,0:T(8,128)(2,1)} async-done(((bf16[768,768]{1,0:T(8,128)(2,1)}), bf16[96,768]{1,0:T(8,128)(2,1)}) %reduce-scatter.24.cloned.1.call-update) | async-done | bytes 147472 | tf_op jit(solution)/shard_map/reduce_scatter | solution.py:238
  998.8 57.5 %reduce-scatter.26.cloned.1.call-done = bf16[1024,768]{1,0:T(8,128)(2,1)} async-done(((bf16[4096,768]{1,0:T(8,128)(2,1)}), bf16[1024,768]{1,0:T(8,128)(2,1)}) %reduce-scatter.26.cloned.1.call-update) | async-done | bytes 1572880 | tf_op jit(solution)/shard_map/reduce_scatter | solution.py:217
  1061.2 39.8 %all-reduce = (f32[]{:T(128)}, f32[4,768]{1,0:T(4,128)S(1)}) all-reduce(f32[]{:T(128)S(6)} %add.232, f32[4,768]{1,0:T(4,128)S(1)} %pad_maximum_fusion.1), channel_id=1, replica_groups=mesh['dp'=2,'batch'=4,'head'=4] {'dp','batch','head'}, use_global_device_ids=true, to_apply=%region_36.37 | all-reduce | flops 3073 | bytes 24584 | tf_op jit(solution)/shard_map/psum | solution.py:246
  (389 shorter events, 274.5 us)
Async XLA Ops:
  7.2 124.8 %all-gather.7.cloned.1.call-start = ((), (), s32[]{:S(2)}) async-start(), calls=%async_computation.9 | async-start | bytes 7864320 | tf_op jit(solution)/shard_map/all_gather | solution.py:142
  13.0 37.8 %copy-start.57 = (f32[192,96]{1,0:T(8,128)S(1)}, f32[192,96]{1,0:T(8,128)}, u32[]{:S(2)}) copy-start(f32[192,96]{1,0:T(8,128)} %param.25) | copy-start | bytes 221188
  13.0 37.9 %copy-start.33 = (f32[96,3,192]{2,0,1:T(8,128)S(1)}, f32[96,3,192]{2,0,1:T(8,128)}, u32[]{:S(2)}) copy-start(f32[96,3,192]{2,0,1:T(8,128)} %param.24) | copy-start | bytes 663556
  14.8 237.9 %all-gather.13.cloned.1.call-start = ((), (), s32[]{:S(2)}) async-start(), calls=%async_computation.13 | async-start | bytes 1327104 | tf_op jit(solution)/shard_map/all_gather | solution.py:133
  15.6 237.8 %all-gather.9.cloned.1.call-start = ((), (), s32[]{:S(2)}) async-start(), calls=%async_computation.10 | async-start | bytes 1327104 | tf_op jit(solution)/shard_map/all_gather | solution.py:134
  16.3 295.5 %reduce-scatter.16.cloned.1.call-start = ((), (), s32[]{:S(2)}) async-start(), calls=%async_computation.12 | async-start | bytes 7864320 | tf_op jit(solution)/shard_map/reduce_scatter | solution.py:170
  17.8 158.6 %copy-start.72 = (f32[4096]{0:T(1024)}, f32[4096]{0:T(1024)S(1)}, u32[]{:S(2)}) copy-start(f32[4096]{0:T(1024)S(1)} %fusion.128) | copy-start | bytes 49156
  193.2 30.2 %copy-start.58 = (f32[64,3,128]{2,0,1:T(8,128)}, f32[64,3,128]{2,0,1:T(8,128)S(1)}, u32[]{:S(2)}) copy-start(f32[64,3,128]{2,0,1:T(8,128)S(1)} %fusion.124) | copy-start | bytes 294916
  252.7 98.2 %all-gather.15.cloned.1.call-start = ((), (), s32[]{:S(2)}) async-start(), calls=%async_computation.14 | async-start | bytes 5898240 | tf_op jit(solution)/shard_map/all_gather | solution.py:180
  253.3 136.6 %all-gather.11.cloned.1.call-start = ((), (), s32[]{:S(2)}) async-start(), calls=%async_computation.11 | async-start | bytes 5898240 | tf_op jit(solution)/shard_map/all_gather | solution.py:181
  253.8 209.4 %all-gather.17.cloned.1.call-start = ((), (), s32[]{:S(2)}) async-start(), calls=%async_computation.15 | async-start | bytes 7864320 | tf_op jit(solution)/shard_map/all_gather | solution.py:202
  389.8 15.5 %copy-start.96 = (f32[1024]{0:T(1024)S(1)}, f32[1024]{0:T(1024)}, u32[]{:S(2)}) copy-start(f32[1024]{0:T(1024)} %fusion.135) | copy-start | bytes 12292
  389.8 15.5 %copy-start.101 = (bf16[768,3072]{0,1:T(8,128)(2,1)S(1)}, bf16[768,3072]{0,1:T(8,128)(2,1)}, u32[]{:S(2)}) copy-start(bf16[768,3072]{0,1:T(8,128)(2,1)} %all-gather.15.cloned.1.call-done) | copy-start | bytes 14155780
  416.7 282.5 %reduce-scatter.20.cloned.1.call-start = ((), (), s32[]{:S(2)}) async-start(), calls=%async_computation.17 | async-start | bytes 5898240 | tf_op jit(solution)/shard_map/reduce_scatter | solution.py:192
  427.1 274.7 %reduce-scatter.22.cloned.1.call-start = ((), (), s32[]{:S(2)}) async-start(), calls=%async_computation.18 | async-start | bytes 5898240 | tf_op jit(solution)/shard_map/reduce_scatter | solution.py:195
  441.7 291.6 %reduce-scatter.30.cloned.1.call-start = ((), (), s32[]{:S(2)}) async-start(), calls=%async_computation.22 | async-start | bytes 1179648
  472.6 25.7 %copy-start.9 = (bf16[64,64,3,64]{3,1,2,0:T(8,128)(2,1)S(1)}, bf16[64,64,3,64]{3,1,2,0:T(8,128)(2,1)}, u32[]{:S(2)}) copy-start(bf16[64,64,3,64]{3,1,2,0:T(8,128)(2,1)} %copy.273) | copy-start | bytes 4718596
  472.6 25.7 %copy-start.22 = (f32[64,64,3,64]{1,0,3,2:T(8,128)S(1)}, f32[64,64,3,64]{1,0,3,2:T(8,128)}, u32[]{:S(2)}) copy-start(f32[64,64,3,64]{1,0,3,2:T(8,128)} %reshape.288) | copy-start | bytes 9437188
  498.4 21.8 %slice-start.2 = ((s8[6291456]{0:T(1024)(128)(4,1)}), s8[4194304]{0:T(1024)(128)(4,1)S(1)}, s32[]{:S(2)}) async-start(s8[6291456]{0:T(1024)(128)(4,1)} %bitcast.210), calls=%async_computation.26 | async-start | bytes 8388608
  631.7 24.5 %slice-start = ((s8[6291456]{0:T(1024)(128)(4,1)}), s8[4194304]{0:T(1024)(128)(4,1)S(1)}, s32[]{:S(2)}) async-start(s8[6291456]{0:T(1024)(128)(4,1)} %bitcast.202), calls=%async_computation.24 | async-start | bytes 8388608
  636.8 19.5 %slice-start.1 = ((s8[6291456]{0:T(1024)(128)(4,1)}), s8[2097152]{0:T(1024)(128)(4,1)S(1)}, s32[]{:S(2)}) async-start(s8[6291456]{0:T(1024)(128)(4,1)} %bitcast.202), calls=%async_computation.25 | async-start | bytes 4194304
  669.7 127.3 %reduce-scatter.28.cloned.1.call-start = ((), (), s32[]{:S(2)}) async-start(), calls=%async_computation.21 | async-start | bytes 442368
  685.9 178.0 %reduce-scatter.18.cloned.1.call-start = ((), (), s32[]{:S(2)}) async-start(), calls=%async_computation.16 | async-start | bytes 1327104 | tf_op jit(solution)/shard_map/reduce_scatter | solution.py:223
  699.2 231.2 %reduce-scatter.32.cloned.1.call-start = ((), (), s32[]{:S(2)}) async-start(), calls=%async_computation.23 | async-start | bytes 1327104
  701.7 294.8 %reduce-scatter.24.cloned.1.call-start = ((), (), s32[]{:S(2)}) async-start(), calls=%async_computation.19 | async-start | bytes 1327104 | tf_op jit(solution)/shard_map/reduce_scatter | solution.py:238
  702.3 354.0 %reduce-scatter.26.cloned.1.call-start = ((), (), s32[]{:S(2)}) async-start(), calls=%async_computation.20 | async-start | bytes 7864320 | tf_op jit(solution)/shard_map/reduce_scatter | solution.py:217
  717.6 338.8 %copy-start.71 = (f32[1024]{0:T(1024)S(1)}, f32[1024]{0:T(1024)}, u32[]{:S(2)}) copy-start(f32[1024]{0:T(1024)} %copy-done.70) | copy-start | bytes 12292
  717.6 338.8 %copy-start.79 = (f32[768]{0:T(1024)S(1)}, f32[768]{0:T(1024)}, u32[]{:S(2)}) copy-start(f32[768]{0:T(1024)} %copy-done.78) | copy-start | bytes 9220
  730.2 328.5 %copy-start.87 = (f32[1024]{0:T(1024)S(1)}, f32[1024]{0:T(1024)}, u32[]{:S(2)}) copy-start(f32[1024]{0:T(1024)} %copy-done.86) | copy-start | bytes 12292
  730.2 328.5 %copy-start.81 = (f32[1024]{0:T(1024)S(1)}, f32[1024]{0:T(1024)}, u32[]{:S(2)}) copy-start(f32[1024]{0:T(1024)} %copy-done.80) | copy-start | bytes 12292
  735.1 263.7 %copy-start.82 = (bf16[2,3,512]{2,0,1:T(2,128)(2,1)}, bf16[2,3,512]{2,0,1:T(2,128)(2,1)S(1)}, u32[]{:S(2)}) copy-start(bf16[2,3,512]{2,0,1:T(2,128)(2,1)S(1)} %copy.324) | copy-start | bytes 18436
  798.0 200.8 %copy-start.56 = (bf16[192,96]{1,0:T(8,128)(2,1)}, bf16[192,96]{1,0:T(8,128)(2,1)S(1)}, u32[]{:S(2)}) copy-start(bf16[192,96]{1,0:T(8,128)(2,1)S(1)} %copy.322) | copy-start | bytes 110596
  (93 other events, 459.2 us)
Sparse Core Ops, SparseCore 0:
  14.9 49.0 all-gather.6
  66.7 49.3 all-gather.12
  118.8 39.7 all-gather.8
  252.8 58.9 reduce-scatter.15
  313.3 37.4 all-gather.14
  352.3 37.4 all-gather.10
  416.9 46.3 all-gather.16
  466.0 47.8 reduce-scatter.19
  516.4 47.8 reduce-scatter.21
  669.8 63.4 reduce-scatter.29
  736.6 60.4 reduce-scatter.27
  800.9 63.0 reduce-scatter.17
  867.3 62.9 reduce-scatter.31
  933.6 62.9 reduce-scatter.23
  998.9 57.3 reduce-scatter.25
where the time goes:
time: 1140 us; the launch traced here: 1130 us
  waiting for transfers between devices  458 us (40%)
  matrix products  306 us (27%)
  blocking collectives  147 us (13%)
  local copies, waits for them, and re-layouts  109 us (10%)
  other arithmetic  89.4 us (8%)
  between operations  21.5 us (2%)
    unnamed x18, waiting for transfers between devices  129 us
    reduce_scatter x1, waiting for transfers between devices, on_device(): lax.psum_scatter(grad_qkv.astype(jnp.bfloat16), ('dp', 'batch'), scatter_...  65.3 us
    reduce_scatter x1, waiting for transfers between devices, on_device(): lax.psum_scatter(grad_proj.astype(jnp.bfloat16), ('dp', 'batch'), scatter...  63.8 us
    reduce_scatter x1, waiting for transfers between devices, on_device(): lax.psum_scatter(jnp.dot(mixed_b, out_full, preferred_element_type=jnp.fl...  57.9 us
    reduce_scatter x1, waiting for transfers between devices, on_device(): lax.psum_scatter(against(d_qkv, qkv_matrix).astype(jnp.bfloat16), 'head',...  57.5 us
    dot_general x3, matrix products, linear_core(): jnp.einsum('nihf,nhfd->nihd', query_blocks, prior_state, precision=highest)  48.5 us
    all_gather x1, blocking collectives, on_device(): lax.all_gather(w_qkv.astype(jnp.bfloat16), ('dp', 'batch'), axis=0, tiled...  46.7 us
    unnamed x236, local copies, waits for them, and re-layouts  45.3 us
  transfers between devices with their start and end apart: 15, of which 10 were waited for; matrix products, arithmetic and copies ran while one was open for 38% of the time, Pallas kernels for 0%

commit v1 on v0

v1 whole, which is shorter than its diff:
```python
import functools

import jax
import jax.numpy as jnp
from jax import lax
from jax.experimental import pallas as pl
from jax.experimental.pallas import tpu as pltpu
from jax.sharding import PartitionSpec as P

HD = 64
STEP = 8
CHUNK = 256
FEAT_ROWS = 32
MESH = pl.DeviceIdType.MESH
VMEM = pltpu.VMEM
F32 = jnp.float32
BF16 = jnp.bfloat16

norm_eps = 1e-05
beta_one = 0.9
beta_two = 0.95
adam_eps = 1e-08
clip_limit = 1.0


def dot(left, right):
    return lax.dot_general(left, right, (((1,), (0,)), ((), ())), preferred_element_type=F32)


def dot_nt(left, right):
    return lax.dot_general(left, right, (((1,), (1,)), ((), ())), preferred_element_type=F32)


def dot_tn(left, right):
    return lax.dot_general(left, right, (((0,), (0,)), ((), ())), preferred_element_type=F32)


def flip_bit(value, bit, on=1):
    low = 2**bit
    return value + on * (low - 2 * low * lax.rem(value // low, 2))


class Network:
    def __init__(self, sizes):
        self.X, self.Z, self.H = sizes
        self.dp, self.b, self.h = (lax.axis_index(name) for name in ("dp", "batch", "head"))
        dp_bits, head_bits = self.X.bit_length() - 1, self.H.bit_length() - 1
        if (self.X, self.H) == (2, 4):
            def first(dp, h):
                odd = lax.rem(h, 2)
                return flip_bit(dp, 0, 1 - odd), flip_bit(h, 1, odd)

            def second(dp, h):
                odd = lax.rem(h, 2)
                return flip_bit(dp, 0, odd), flip_bit(h, 1, 1 - odd)

            self.flips = [first, second, lambda dp, h: (dp, flip_bit(h, 0))]
        else:
            self.flips = [lambda dp, h, k=k: (flip_bit(dp, k), h) for k in range(dp_bits)]
            self.flips += [lambda dp, h, k=k: (dp, flip_bit(h, k)) for k in reversed(range(head_bits))]
        self.sets = [()]
        for k in range(len(self.flips)):
            self.sets += [s + (k,) for s in self.sets]
        self.index = {s: i for i, s in enumerate(self.sets)}

    def coord(self, chosen):
        dp, h = self.dp, self.h
        for k in sorted(chosen, reverse=True):
            dp, h = self.flips[k](dp, h)
        return dp, h

    def behind(self, off):
        return lax.rem(self.b + self.Z - off, self.Z)

    def ahead(self, off):
        return lax.rem(self.b + off, self.Z)

    def slot(self, chosen, off):
        dp, h = self.coord(chosen)
        return dp, self.behind(off), h

    def partner(self, k):
        dp, h = self.flips[k](self.dp, self.h)
        return {"dp": dp, "batch": self.b, "head": h}

    def along(self, b):
        return {"dp": self.dp, "batch": b, "head": self.h}

    def stages(self, chosen):
        return range(max(chosen) + 1 if chosen else 0, len(self.flips))

    def barrier(self, extra=()):
        sem = pltpu.get_barrier_semaphore()
        devices = [self.along(self.ahead(off)) for off in range(1, self.Z)]
        devices += [self.partner(k) for k in range(len(self.flips))]
        for device in devices:
            pl.semaphore_signal(sem, inc=1, device_id=device, device_id_type=MESH)
        pl.semaphore_wait(sem, len(devices))


def gather_sems(sizes):
    X, Z, H = sizes
    n = X * H - 1
    return [pltpu.SemaphoreType.DMA((n + 1, Z)), pltpu.SemaphoreType.DMA((n + 1, Z))]


class Gather:
    def __init__(self, net, shard, buf, send, recv):
        self.net, self.shard, self.buf, self.send, self.recv = net, shard, buf, send, recv

    def copy(self, chosen, off, k=None):
        net = self.net
        place = self.buf.at[net.slot(chosen, off)]
        into = net.index[chosen + (k,)]
        return pltpu.make_async_remote_copy(
            src_ref=place, dst_ref=place, send_sem=self.send.at[into, off], recv_sem=self.recv.at[into, off],
            device_id=net.partner(k), device_id_type=MESH,
        )

    def copy_along(self, off):
        net = self.net
        place = self.buf.at[net.slot((), 0)]
        return pltpu.make_async_remote_copy(
            src_ref=place, dst_ref=place, send_sem=self.send.at[0, off], recv_sem=self.recv.at[0, off],
            device_id=net.along(net.ahead(off)), device_id_type=MESH,
        )

    def arrived(self, chosen, off):
        net = self.net
        place = self.buf.at[net.slot(chosen, off)]
        into = net.index[chosen]
        pltpu.make_async_remote_copy(
            src_ref=place, dst_ref=place, send_sem=self.send.at[into, off], recv_sem=self.recv.at[into, off],
            device_id=net.partner(0), device_id_type=MESH,
        ).wait_recv()

    def begin(self):
        net = self.net
        self.buf[net.slot((), 0)] = self.shard[...]
        for off in range(1, net.Z):
            self.copy_along(off).start()
        for k in net.stages(()):
            self.copy((), 0, k).start()

    def step(self, chosen, off):
        self.arrived(chosen, off)
        for k in self.net.stages(chosen):
            self.copy(chosen, off, k).start()

    def steps(self):
        net = self.net
        order = []
        for off in range(1, net.Z):
            order.append(((), off))
        for chosen in net.sets[1:]:
            order += [(chosen, off) for off in range(net.Z)]
        return [functools.partial(self.step, *item) for item in order]

    def finish(self):
        net = self.net
        for off in range(1, net.Z):
            self.copy_along(off).wait_send()
        for chosen in net.sets:
            for k in net.stages(chosen):
                for off in range(net.Z):
                    self.copy(chosen, off, k).wait_send()


def scatter_scratch(sizes, shape):
    X, Z, H = sizes
    n = X * H
    return [
        VMEM((n // 2, Z) + shape, BF16),
        VMEM((n, Z) + shape, BF16),
        pltpu.SemaphoreType.DMA((n, Z)),
        pltpu.SemaphoreType.DMA((n, Z)),
    ]


class Scatter:
    def __init__(self, net, part, acc, inbox, send, recv):
        self.net, self.part, self.acc, self.inbox, self.send, self.recv = net, part, acc, inbox, send, recv

    def copy(self, chosen, off, k):
        net = self.net
        into = net.index[chosen + (k,)]
        last = k == len(net.flips) - 1
        source = self.part.at[net.slot(chosen + (k,), off)] if last else self.acc.at[into, off]
        return pltpu.make_async_remote_copy(
            src_ref=source, dst_ref=self.inbox.at[into, off], send_sem=self.send.at[into, off],
            recv_sem=self.recv.at[into, off], device_id=net.partner(k), device_id_type=MESH,
        )

    def copy_along(self, off):
        net = self.net
        return pltpu.make_async_remote_copy(
            src_ref=self.acc.at[0, off], dst_ref=self.inbox.at[0, off], send_sem=self.send.at[0, off],
            recv_sem=self.recv.at[0, off], device_id=net.along(net.behind(off)), device_id_type=MESH,
        )

    def begin(self):
        net = self.net
        last = len(net.flips) - 1
        for chosen in reversed(net.sets[: len(net.sets) // 2]):
            for off in range(net.Z):
                self.copy(chosen, off, last).start()

    def add(self, chosen, off, k):
        net = self.net
        into = net.index[chosen + (k,)]
        self.copy(chosen, off, k).wait_recv()
        last = k == len(net.flips) - 1
        mine = self.part[net.slot(chosen, off)] if last else self.acc[net.index[chosen], off]
        self.acc[net.index[chosen], off] = (mine.astype(F32) + self.inbox[into, off].astype(F32)).astype(BF16)

    def step(self, chosen, off):
        net = self.net
        for k in reversed(net.stages(chosen)):
            self.add(chosen, off, k)
        if chosen:
            self.copy(chosen[:-1], off, chosen[-1]).start()
        elif off:
            self.copy_along(off).start()

    def steps(self):
        net = self.net
        order = []
        for chosen in reversed(net.sets[: len(net.sets) // 2]):
            order += [(chosen, off) for off in reversed(range(net.Z))]
        return [functools.partial(self.step, *item) for item in order]

    def result(self):
        net = self.net
        total = self.acc[0, 0].astype(F32)
        for off in range(1, net.Z):
            self.copy_along(off).wait_recv()
            total = total + self.inbox[0, off].astype(F32)
        return total

    def finish(self):
        net = self.net
        for off in range(1, net.Z):
            self.copy_along(off).wait_send()
        for chosen in net.sets:
            for k in net.stages(chosen):
                for off in range(net.Z):
                    self.copy(chosen, off, k).wait_send()


def total_scratch(sizes, shape):
    X, Z, H = sizes
    bits = (X * H).bit_length() - 1
    return [
        VMEM((Z + 2 * bits,) + shape, F32),
        pltpu.SemaphoreType.DMA((Z + bits,)),
        pltpu.SemaphoreType.DMA((Z + bits,)),
    ]


def total_over_all(net, value, slots, send, recv):
    Z = net.Z
    slots[net.b] = value
    copies = []
    for off in range(1, Z):
        copies.append(
            pltpu.make_async_remote_copy(
                src_ref=slots.at[net.b], dst_ref=slots.at[net.b], send_sem=send.at[off], recv_sem=recv.at[off],
                device_id=net.along(net.ahead(off)), device_id_type=MESH,
            )
        )
    for copy in copies:
        copy.start()
    for off in range(1, Z):
        place = slots.at[net.behind(off)]
        pltpu.make_async_remote_copy(
            src_ref=place, dst_ref=place, send_sem=send.at[off], recv_sem=recv.at[off],
            device_id=net.along(net.ahead(off)), device_id_type=MESH,
        ).wait_recv()
    for copy in copies:
        copy.wait_send()
    value = slots[0]
    for off in range(1, Z):
        value = value + slots[off]
    for k in range(len(net.flips)):
        slots[Z + 2 * k] = value
        copy = pltpu.make_async_remote_copy(
            src_ref=slots.at[Z + 2 * k], dst_ref=slots.at[Z + 2 * k + 1], send_sem=send.at[Z + k],
            recv_sem=recv.at[Z + k], device_id=net.partner(k), device_id_type=MESH,
        )
        copy.start()
        copy.wait()
        value = value + slots[Z + 2 * k + 1]
    return value


def gather_kernel(sizes, count, *refs):
    shards, bufs, sems = refs[:count], refs[count : 2 * count], refs[2 * count :]
    net = Network(sizes)
    net.barrier()
    gathers = [Gather(net, shards[i], bufs[i], sems[2 * i], sems[2 * i + 1]) for i in range(count)]
    for gather in gathers:
        gather.begin()
    for gather in gathers:
        for step in gather.steps():
            step()
    for gather in gathers:
        gather.finish()


def scatter_kernel(sizes, count, *refs):
    parts, norm_ref = refs[:count], refs[count]
    outs, norm_out, sq_out = refs[count + 1 : 2 * count + 1], refs[2 * count + 1], refs[2 * count + 2]
    scratch = refs[2 * count + 3 :]
    net = Network(sizes)
    net.barrier()
    scatters = [Scatter(net, parts[i], *scratch[4 * i : 4 * i + 4]) for i in range(count)]
    rest = scratch[4 * count :]
    for scatter in scatters:
        scatter.begin()
    for scatter in scatters:
        for step in scatter.steps():
            step()
    norm_out[...] = total_over_all(net, norm_ref[...], *rest[:3])
    square = jnp.zeros((1, 128), F32)
    for scatter, out in zip(scatters, outs):
        total = scatter.result()
        out[...] = total
        column = jnp.sum(total * total, axis=0, keepdims=True)
        for at in range(0, column.shape[1], 128):
            square = square + column[:, at : at + 128]
    first_row = lax.broadcasted_iota(jnp.int32, (8, 128), 0) == 0
    sq_out[...] = total_over_all(net, jnp.where(first_row, square, 0.0), *rest[3:])
    for scatter in scatters:
        scatter.finish()


def norm_stats(values):
    mean = jnp.mean(values, axis=-1, keepdims=True)
    center = values - mean
    spread = jnp.mean(center * center, axis=-1, keepdims=True)
    return center, lax.rsqrt(spread + norm_eps)


def norm_backward(values, gain_row, grads):
    center, scale = norm_stats(values)
    normal = center * scale
    inner = grads * gain_row
    part = jnp.mean(inner * normal, axis=-1, keepdims=True)
    back = scale * (inner - jnp.mean(inner, axis=-1, keepdims=True) - normal * part)
    return back, jnp.sum(grads * normal, axis=0, keepdims=True), jnp.sum(grads, axis=0, keepdims=True)


def low_half(shape):
    return lax.rem(lax.broadcasted_iota(jnp.int32, shape, len(shape) - 1), 128) < HD


def swap_halves(values):
    cols = values.shape[1]
    parts = [pltpu.roll(values[:, at : at + 128], HD, 1) for at in range(0, cols, 128)]
    return parts[0] if len(parts) == 1 else jnp.concatenate(parts, axis=1)


def feature_pair(scaled, live):
    low = low_half(scaled.shape)
    top = jnp.max(jnp.where(low, scaled, -jnp.inf), axis=-1, keepdims=True)
    bottom = jnp.max(jnp.where(low, -jnp.inf, scaled), axis=-1, keepdims=True)
    powers = jnp.exp(scaled - jnp.where(low, top, bottom))
    first = jnp.sum(jnp.where(low, powers, 0.0), axis=-1, keepdims=True)
    second = jnp.sum(jnp.where(low, 0.0, powers), axis=-1, keepdims=True)
    return powers * (live / jnp.where(low, first, second))


def feature_back(feature, grads):
    low = low_half(feature.shape)
    product = feature * grads
    first = jnp.sum(jnp.where(low, product, 0.0), axis=-1, keepdims=True)
    second = jnp.sum(jnp.where(low, 0.0, product), axis=-1, keepdims=True)
    return product - feature * jnp.where(low, first, second)


class Rows:
    def __init__(self, len_ref, rows, h):
        self.first_len = len_ref[0, 0]
        self.both_len = len_ref[0, 0] + len_ref[0, 1]
        self.start = h * rows
        self.rows = rows

    def second(self, row):
        return row >= self.first_len

    def column(self, chunk):
        return self.start + chunk * CHUNK + lax.broadcasted_iota(jnp.int32, (CHUNK, 1), 0)

    def live(self, chunk):
        return (self.column(chunk) < self.both_len).astype(F32)

    def second_column(self, chunk):
        return self.second(self.column(chunk))

    def masks(self, chunk):
        base = self.start + chunk * CHUNK
        down = base + lax.broadcasted_iota(jnp.int32, (CHUNK, CHUNK), 0)
        across = base + lax.broadcasted_iota(jnp.int32, (CHUNK, CHUNK), 1)
        same = (down >= self.first_len) == (across >= self.first_len)
        return same & (across <= down), same & (across >= down)

    def scalar(self, row):
        return jnp.where(self.second(row), 1.0, 0.0).astype(F32)

    def before(self):
        return self.scalar(self.start - 1)

    def first(self):
        return self.scalar(self.start)

    def last(self):
        return self.scalar(self.start + self.rows - 1)

    def after(self):
        return self.scalar(self.start + self.rows)


def with_ones(block, head, low):
    ones = jnp.ones_like(block)
    return jnp.where(low, block, ones) if head % 2 == 0 else jnp.where(low, ones, block)


def by_sequence(values, second):
    zero = jnp.zeros_like(values)
    return jnp.concatenate([jnp.where(second, zero, values), jnp.where(second, values, zero)], axis=1)


def chain(step, n, h, total_ref, pick, same, place, cin, cout, send, recv):
    begin = h == (0 if step == 1 else n - 1)
    end = h == (n - 1 if step == 1 else 0)
    neighbour = {"head": lax.rem(h + n + step, n)}
    copy = pltpu.make_async_remote_copy(
        src_ref=cout, dst_ref=cin, send_sem=send, recv_sem=recv, device_id=neighbour, device_id_type=MESH
    )

    @pl.when(begin)
    def _():
        cin[...] = jnp.zeros_like(cin)

    @pl.when(jnp.logical_not(begin))
    def _():
        copy.wait_recv()

    @pl.when(jnp.logical_not(end))
    def _():
        for i in range(cout.shape[0]):
            for j in range(cout.shape[1]):
                both = total_ref[i, j]
                mine = both[:, :128] * (1.0 - pick) + both[:, 128:] * pick
                cout[i, j] = (mine + cin[i, j].astype(F32) * same).astype(BF16)
        copy.start()
        copy.wait_send()


def chain_barrier(n, h):
    sem = pltpu.get_barrier_semaphore()
    for step in (1, n - 1):
        pl.semaphore_signal(sem, inc=1, device_id={"head": lax.rem(h + step, n)}, device_id_type=MESH)
    pl.semaphore_wait(sem, 2)


def equal(a, b):
    return a * b + (1.0 - a) * (1.0 - b)


def attention_forward(
    groups, heads, len_ref, x_ref, w_ref, feat_ref, norm_ref,
    normed_ref, qkv_ref, fq_ref, fk_ref, state_ref, mixed_ref, rden_ref, wo_ref, maps_ref, middle_ref, hidden_ref,
    total_ref, cin, cout, send, recv,
):
    h = lax.axis_index("head")
    rows = x_ref.shape[0]
    chunks = rows // CHUNK
    width = x_ref.shape[1]
    seq = Rows(len_ref, rows, h)
    chain_barrier(groups, h)
    low = low_half((CHUNK, 128))

    maps_ref[...] = jnp.zeros_like(maps_ref)
    low64 = low_half((HD, 128))
    for g in range(groups):
        for j in range(heads):
            pair = feat_ref[g * heads + j]
            swapped = pltpu.roll(pair, HD, 1)
            at = slice(HD * j, HD * j + HD), slice(128 * j, 128 * j + 128)
            maps_ref[0, g, at[0], at[1]] = jnp.where(low64, pair, -swapped).astype(BF16)
            maps_ref[1, g, at[0], at[1]] = jnp.where(low64, swapped, -pair).astype(BF16)

    def first_norm(c, _):
        at = pl.ds(pl.multiple_of(c * CHUNK, CHUNK), CHUNK)
        center, scale = norm_stats(x_ref[at].astype(F32))
        normed_ref[at] = (center * scale * norm_ref[0:1] + norm_ref[1:2]).astype(BF16)
        return 0

    lax.fori_loop(0, chunks, first_norm, 0)

    def project(g, _):
        weight = w_ref[:, :, g].reshape(width, width)
        lowd = low_half((width, 128))
        a = swap_halves(weight[:, 128:256].astype(F32))
        b = weight[:, 384:512].astype(F32)
        c_ = swap_halves(weight[:, 640:768].astype(F32))
        wo_ref[g, :, 0:128] = jnp.where(lowd, a, b).astype(BF16)
        wo_ref[g, :, 128:256] = jnp.where(lowd, c_, 0.0).astype(BF16)
        for j in range(heads):
            total_ref[g, j] = jnp.zeros_like(total_ref[g, j])

        def part(c, _):
            at = pl.ds(pl.multiple_of(c * CHUNK, CHUNK), CHUNK)
            live, second = seq.live(c), seq.second_column(c)
            qkv = dot(normed_ref[at], w_ref[:, :, g].reshape(width, width)).astype(BF16)
            qkv_ref[g, at] = qkv
            scaled_q = dot(qkv[:, 0:256], maps_ref[0, g])
            scaled_k = dot(qkv[:, 256:512], maps_ref[1, g])
            for j in range(heads):
                lanes = slice(128 * j, 128 * j + 128)
                fq_ref[g, at, lanes] = feature_pair(scaled_q[:, lanes], live).astype(BF16)
                fk = feature_pair(scaled_k[:, lanes], live).astype(BF16)
                fk_ref[g, at, lanes] = fk
                block = qkv[:, 512 + 128 * (j // 2) : 640 + 128 * (j // 2)]
                values = by_sequence(with_ones(block, j, low), second)
                state_ref[g, j, c] = total_ref[g, j].astype(BF16)
                total_ref[g, j] += dot_tn(fk, values)
            return 0

        lax.fori_loop(0, chunks, part, 0)
        return 0

    lax.fori_loop(0, groups, project, 0)

    before = seq.before()
    chain(1, groups, h, total_ref, seq.last(), equal(before, seq.last()), None, cin, cout, send, recv)

    def mix(g, _):
        def part(c, _):
            at = pl.ds(pl.multiple_of(c * CHUNK, CHUNK), CHUNK)
            live, second = seq.live(c), seq.second_column(c)
            lower, _ = seq.masks(c)
            found = []
            for j in range(heads):
                lanes = slice(128 * j, 128 * j + 128)
                fq, fk = fq_ref[g, at, lanes], fk_ref[g, at, lanes]
                carry = cin[g, j].astype(F32)
                prior = jnp.concatenate([carry * (1.0 - before), carry * before], axis=1)
                state = (state_ref[g, j, c].astype(F32) + prior).astype(BF16)
                state_ref[g, j, c] = state
                scores = jnp.where(lower, dot_nt(fq, fk), 0.0).astype(BF16)
                block = qkv_ref[g, at, 512 + 128 * (j // 2) : 640 + 128 * (j // 2)]
                inter = dot(fq, state)
                found.append(
                    dot(scores, with_ones(block, j, low)) + jnp.where(second, inter[:, 128:], inter[:, :128])
                )
            pair = jnp.where(low, found[0], found[1])
            rden = 1.0 / (swap_halves(jnp.where(low, found[1], found[0])) + (1.0 - live))
            mixed_ref[g, at, 0:128] = (pair * rden).astype(BF16)
            rden_ref[g, at, 0:128] = rden
            rden = jnp.where(low, 1.0 / (swap_halves(found[2]) + (1.0 - live)), 1.0)
            mixed_ref[g, at, 128:256] = jnp.where(low, found[2] * rden, 0.0).astype(BF16)
            rden_ref[g, at, 128:256] = rden
            return 0

        lax.fori_loop(0, chunks, part, 0)
        return 0

    lax.fori_loop(0, groups, mix, 0)

    def close(c, _):
        at = pl.ds(pl.multiple_of(c * CHUNK, CHUNK), CHUNK)
        attended = dot_nt(mixed_ref[0, at], wo_ref[0])
        for g in range(1, groups):
            attended = attended + dot_nt(mixed_ref[g, at], wo_ref[g])
        middle = x_ref[at].astype(F32) + attended
        middle_ref[at] = middle
        center, scale = norm_stats(middle)
        hidden_ref[at] = (center * scale * norm_ref[2:3] + norm_ref[3:4]).astype(BF16)
        return 0

    lax.fori_loop(0, chunks, close, 0)


def feed_forward(
    hidden_ref, dy_ref, fc_ref, proj_ref, middle_ref, norm_ref,
    out_ref, dmid_ref, datt_ref, gfc_ref, gproj_ref, gnorm_ref,
    branch_ref, dhid_ref, act_ref, dpre_ref,
):
    X, Z, H, part, width = fc_ref.shape
    rows = hidden_ref.shape[0]
    tile = 256
    branch_ref[...] = jnp.zeros_like(branch_ref)
    dhid_ref[...] = jnp.zeros_like(dhid_ref)

    def block(i, _):
        dp, b = i // Z, lax.rem(i, Z)

        def rowed(c, _):
            at = pl.ds(pl.multiple_of(c * tile, tile), tile)
            fc = fc_ref[dp, b].reshape(H * part, width)
            proj = proj_ref[dp, b].reshape(H * part, width)
            pre = dot_nt(hidden_ref[at], fc)
            square = pre * pre
            inner = jnp.tanh(0.7978845608 * pre * (1.0 + 0.044715 * square))
            half = 0.5 * (1.0 + inner)
            act = (pre * half).astype(BF16)
            slope = half + 0.5 * pre * (1.0 - inner * inner) * (0.7978845608 * (1.0 + 3 * 0.044715 * square))
            dpre = (dot_nt(dy_ref[at], proj) * slope).astype(BF16)
            act_ref[at] = act
            dpre_ref[at] = dpre
            branch_ref[at] += dot(act, proj)
            dhid_ref[at] += dot(dpre, fc)
            return 0

        lax.fori_loop(0, rows // tile, rowed, 0)
        gproj_ref[dp, b] = dot_tn(act_ref[...], dy_ref[...]).astype(BF16).reshape(H, part, width)
        gfc_ref[dp, b] = dot_tn(dpre_ref[...], hidden_ref[...]).astype(BF16).reshape(H, part, width)
        return 0

    lax.fori_loop(0, X * Z, block, 0)

    gnorm_ref[...] = jnp.zeros_like(gnorm_ref)

    def close(c, _):
        at = pl.ds(pl.multiple_of(c * tile, tile), tile)
        middle = middle_ref[at]
        out_ref[at] = (middle + branch_ref[at]).astype(BF16)
        back, gain, shift = norm_backward(middle, norm_ref[2:3], dhid_ref[at])
        dmid = dy_ref[at].astype(F32) + back
        dmid_ref[at] = dmid
        datt_ref[at] = dmid.astype(BF16)
        gnorm_ref[2:3] += gain
        gnorm_ref[3:4] += shift
        return 0

    lax.fori_loop(0, rows // tile, close, 0)


def attention_backward(
    groups, heads, len_ref, x_ref, normed_ref, qkv_ref, fq_ref, fk_ref, state_ref, mixed_ref, rden_ref, wo_ref,
    maps_ref, w_ref, datt_ref, dmid_ref, norm_ref, gnorm_in,
    dx_ref, gw_ref, gmap_ref, gnorm_ref,
    dne_ref, back_ref, total_ref, dqkv_ref, dnormed_ref, gsum_ref, cin, cout, send, recv,
):
    h = lax.axis_index("head")
    rows, width = x_ref.shape
    chunks = rows // CHUNK
    X, Z, H, part, _ = w_ref.shape
    seq = Rows(len_ref, rows, h)
    chain_barrier(groups, h)
    low = low_half((CHUNK, 128))
    down = lax.broadcasted_iota(jnp.int32, (256, 256), 0) // HD
    across = lax.broadcasted_iota(jnp.int32, (256, 256), 1) // HD
    other_half = ((down // 2 == across // 2) & (down != across)).astype(BF16)

    def ahead(g, _):
        for j in range(heads):
            total_ref[g, j] = jnp.zeros_like(total_ref[g, j])

        def piece(i, _):
            c = chunks - 1 - i
            at = pl.ds(pl.multiple_of(c * CHUNK, CHUNK), CHUNK)
            second = seq.second_column(c)
            dm = dot(datt_ref[at], wo_ref[g]).astype(BF16).astype(F32)
            rden = rden_ref[g, at]
            sums = dot((dm * mixed_ref[g, at].astype(F32)).astype(BF16), other_half)
            dnum = dm * rden
            dden = sums * swap_halves(rden) * (-1.0 / HD)
            for j in range(heads):
                lanes = slice(128 * (j // 2), 128 * (j // 2) + 128)
                first, other = dnum[:, lanes], dden[:, lanes]
                dne = (jnp.where(low, first, other) if j % 2 == 0 else jnp.where(low, other, first)).astype(BF16)
                dne_ref[g, j, at] = dne
                back_ref[g, j, c] = total_ref[g, j].astype(BF16)
                total_ref[g, j] += dot_tn(fq_ref[g, at, 128 * j : 128 * j + 128], by_sequence(dne, second))
            return 0

        lax.fori_loop(0, chunks, piece, 0)
        return 0

    lax.fori_loop(0, groups, ahead, 0)
    after = seq.after()
    chain(-1, groups, h, total_ref, seq.first(), equal(after, seq.first()), None, cin, cout, send, recv)

    dnormed_ref[...] = jnp.zeros_like(dnormed_ref)

    def group(g, _):
        gsum_ref[...] = jnp.zeros_like(gsum_ref)

        def piece(c, _):
            at = pl.ds(pl.multiple_of(c * CHUNK, CHUNK), CHUNK)
            second = seq.second_column(c)
            lower, upper = seq.masks(c)
            dus_q, dus_k, dvs = [], [], []
            for j in range(heads):
                lanes = slice(128 * j, 128 * j + 128)
                fq, fk, dne = fq_ref[g, at, lanes], fk_ref[g, at, lanes], dne_ref[g, j, at]
                carry = cin[g, j].astype(F32)
                later = jnp.concatenate([carry * (1.0 - after), carry * after], axis=1)
                back = (back_ref[g, j, c].astype(F32) + later).astype(BF16)
                state = state_ref[g, j, c]
                block = qkv_ref[g, at, 512 + 128 * (j // 2) : 640 + 128 * (j // 2)]
                values = with_ones(block, j, low)
                scores_t = jnp.where(upper, dot_nt(fk, fq), 0.0).astype(BF16)
                weigh = jnp.where(lower, dot_nt(dne, values), 0.0).astype(BF16)
                weigh_t = jnp.where(upper, dot_nt(values, dne), 0.0).astype(BF16)
                dfq = dot(weigh, fk) + dot_nt(by_sequence(dne, second), state)
                dfk = dot(weigh_t, fq) + dot_nt(by_sequence(values, second), back)
                inter = dot(fk, back)
                dvs.append(dot(scores_t, dne) + jnp.where(second, inter[:, 128:], inter[:, :128]))
                dus_q.append(feature_back(fq.astype(F32), dfq.astype(BF16).astype(F32)).astype(BF16))
                dus_k.append(feature_back(fk.astype(F32), dfk.astype(BF16).astype(F32)).astype(BF16))
            du_q, du_k = jnp.concatenate(dus_q, axis=1), jnp.concatenate(dus_k, axis=1)
            dq = dot_nt(du_q, maps_ref[0, g]).astype(BF16)
            dk = dot_nt(du_k, maps_ref[1, g]).astype(BF16)
            dv = jnp.concatenate([jnp.where(low, dvs[0], dvs[1]), jnp.where(low, dvs[2], 0.0)], axis=1).astype(BF16)
            gsum_ref[0] += dot_tn(qkv_ref[g, at, 0:256], du_q)
            gsum_ref[1] += dot_tn(qkv_ref[g, at, 256:512], du_k)
            dqkv = jnp.concatenate([dq, dk, dv], axis=1)
            dqkv_ref[at] = dqkv
            dnormed_ref[at] += dot_nt(dqkv, w_ref[:, :, g].reshape(width, width))
            return 0

        lax.fori_loop(0, chunks, piece, 0)
        for side in range(2):
            for j in range(heads):
                gmap_ref[side, g, j] = gsum_ref[side, HD * j : HD * j + HD, 128 * j : 128 * j + 128]
        lowd = low_half((width, 128))
        shape = (X, Z, part, 128)
        for third in range(3):
            grad = dot_tn(normed_ref[...], dqkv_ref[:, 256 * third : 256 * third + 256])
            beside = dot_tn(datt_ref[...], mixed_ref[g, :, 128 * (third // 2) : 128 * (third // 2) + 128])
            if third != 1:
                beside = swap_halves(beside)
            at = 256 * third
            gw_ref[:, :, g, :, at : at + 128] = grad[:, 0:128].astype(BF16).reshape(shape)
            gw_ref[:, :, g, :, at + 128 : at + 256] = (
                jnp.where(lowd, grad[:, 128:256], beside).astype(BF16).reshape(shape)
            )
        return 0

    lax.fori_loop(0, groups, group, 0)

    gnorm_ref[...] = gnorm_in[...]

    def close(c, _):
        at = pl.ds(pl.multiple_of(c * CHUNK, CHUNK), CHUNK)
        back, gain, shift = norm_backward(x_ref[at].astype(F32), norm_ref[0:1], dnormed_ref[at])
        dx_ref[at] = dmid_ref[at] + back
        gnorm_ref[0:1] += gain
        gnorm_ref[1:2] += shift
        return 0

    lax.fori_loop(0, chunks, close, 0)


def adamw_update(master, first_mom, second_mom, grad_in, factor, step_rate, decay_rate):
    clipped = grad_in * factor
    first_new = beta_one * first_mom + (1.0 - beta_one) * clipped
    second_new = beta_two * second_mom + (1.0 - beta_two) * clipped * clipped
    direction = (
        first_new
        / (1.0 - beta_one**STEP)
        / (jnp.sqrt(second_new / (1.0 - beta_two**STEP)) + adam_eps)
    )
    master_new = master - step_rate * (direction + decay_rate * master)
    return (master_new, first_new, second_new)


def in_vmem(count):
    return [pl.BlockSpec(memory_space=VMEM)] * count


def struct(shape, dtype):
    return jax.ShapeDtypeStruct(shape, dtype)


def call(kernel, outs, smem, operands, scratch, collective_id, name, flops, limit=63):
    specs = [pl.BlockSpec(memory_space=pltpu.SMEM)] * smem + in_vmem(len(operands) - smem)
    traffic = sum(o.size * o.dtype.itemsize for o in outs) + sum(o.size * o.dtype.itemsize for o in operands)
    extra = {} if collective_id is None else {"collective_id": collective_id, "has_side_effects": True}
    return pl.pallas_call(
        kernel,
        out_shape=tuple(outs),
        in_specs=specs,
        out_specs=tuple(in_vmem(len(outs))),
        scratch_shapes=scratch,
        compiler_params=pltpu.CompilerParams(vmem_limit_bytes=limit * 2**20, **extra),
        cost_estimate=pl.CostEstimate(flops=flops, bytes_accessed=traffic, transcendentals=0),
        name=name,
    )(*operands)


def on_device(
    sizes,
    block_in,
    cotangent,
    seq_len,
    w_qkv,
    w_out,
    w_feat,
    w_fc,
    w_proj,
    norm_params,
    first_qkv,
    second_qkv,
    first_out,
    second_out,
    first_feat,
    second_feat,
    first_fc,
    second_fc,
    first_proj,
    second_proj,
    first_norms,
    second_norms,
):
    X, Z, H = sizes
    rows, width = block_in.shape
    part, _, head_width = w_qkv.shape
    heads = w_feat.shape[1]
    depth = w_feat.shape[2] // HD
    chunks = rows // CHUNK

    norm_low = norm_params.astype(BF16).astype(F32)
    out_t = w_out.T
    pieces = []
    for j in range(3):
        pieces += [w_qkv[:, j, :], out_t[:, HD * j : HD * j + HD]]
    attn_shard = jnp.concatenate(pieces, axis=1).astype(BF16)
    fc_shard = w_fc.T.astype(BF16)
    proj_shard = w_proj.astype(BF16)
    feat_rows = w_feat.reshape(2, heads, depth, HD).transpose(1, 2, 0, 3).reshape(heads * depth, 2 * HD)
    feat_shard = jnp.pad(feat_rows.astype(BF16), ((0, FEAT_ROWS - heads * depth), (0, 0)))

    big = (X, Z, H, part, width)
    small = (X, Z, H, FEAT_ROWS, 2 * HD)
    attn_w, feat_all, fc_w, proj_w = call(
        functools.partial(gather_kernel, sizes, 4),
        [struct(big, BF16), struct(small, BF16), struct(big, BF16), struct(big, BF16)],
        0,
        [attn_shard, feat_shard, fc_shard, proj_shard],
        [sem for _ in range(4) for sem in gather_sems(sizes)],
        0,
        "gather",
        0,
    )
    feat_maps = (
        feat_all.reshape(X * Z, H, FEAT_ROWS, 2 * HD)[:, :, : heads * depth]
        .reshape(X * Z, H, heads, depth, 2 * HD)
        .transpose(1, 2, 0, 3, 4)
        .reshape(H * heads, HD, 2 * HD)
        .astype(F32)
    )

    chain_scratch = [
        VMEM((H, heads, 128, 128), BF16),
        VMEM((H, heads, 128, 128), BF16),
        pltpu.SemaphoreType.DMA,
        pltpu.SemaphoreType.DMA,
    ]
    normed, qkv, fq, fk, states, mixed, rden, wo, maps, middle, hidden = call(
        functools.partial(attention_forward, H, heads),
        [
            struct((rows, width), BF16),
            struct((H, rows, width), BF16),
            struct((H, rows, 128 * heads), BF16),
            struct((H, rows, 128 * heads), BF16),
            struct((H, heads, chunks, 128, 256), BF16),
            struct((H, rows, 256), BF16),
            struct((H, rows, 256), F32),
            struct((H, width, 256), BF16),
            struct((2, H, 256, 128 * heads), BF16),
            struct((rows, width), F32),
            struct((rows, width), BF16),
        ],
        1,
        [seq_len, block_in, attn_w, feat_maps, norm_low],
        [VMEM((H, heads, 128, 256), F32)] + chain_scratch,
        1,
        "attention_forward",
        10**10,
    )

    block_out, d_middle, d_att, g_fc_all, g_proj_all, g_norm = call(
        feed_forward,
        [
            struct((rows, width), BF16),
            struct((rows, width), F32),
            struct((rows, width), BF16),
            struct(big, BF16),
            struct(big, BF16),
            struct((8, width), F32),
        ],
        0,
        [hidden, cotangent, fc_w, proj_w, middle, norm_low],
        [
            VMEM((rows, width), F32),
            VMEM((rows, width), F32),
            VMEM((rows, H * part), BF16),
            VMEM((rows, H * part), BF16),
        ],
        None,
        "feed_forward",
        3 * 10**10,
    )

    block_in_grad, g_attn_all, g_maps, g_norm = call(
        functools.partial(attention_backward, H, heads),
        [
            struct((rows, width), F32),
            struct(big, BF16),
            struct((2, H, heads, HD, 128), F32),
            struct((8, width), F32),
        ],
        1,
        [
            seq_len, block_in, normed, qkv, fq, fk, states, mixed, rden, wo, maps, attn_w, d_att, d_middle, norm_low,
            g_norm,
        ],
        [
            VMEM((H, heads, rows, 128), BF16),
            VMEM((H, heads, chunks, 128, 256), BF16),
            VMEM((H, heads, 128, 256), F32),
            VMEM((rows, width), BF16),
            VMEM((rows, width), F32),
            VMEM((2, 256, 128 * heads), F32),
        ]
        + chain_scratch,
        2,
        "attention_backward",
        2 * 10**10,
    )

    blocks = g_maps[..., :HD] - g_maps[..., HD:]
    g_feat_all = (
        jnp.concatenate([blocks[0], blocks[1]], axis=-1)
        .reshape(H, heads, X * Z, depth, 2 * HD)
        .transpose(2, 0, 1, 3, 4)
        .reshape(X, Z, H, heads * depth, 2 * HD)
    )
    g_feat_all = jnp.pad(
        g_feat_all, ((0, 0), (0, 0), (0, 0), (0, FEAT_ROWS - heads * depth), (0, 0))
    ).astype(BF16)

    shapes = [(part, width)] * 3 + [(FEAT_ROWS, 2 * HD)]
    g_fc, g_proj, g_attn, g_feat, norm_sum, square_sum = call(
        functools.partial(scatter_kernel, sizes, 4),
        [struct(shape, F32) for shape in shapes] + [struct((8, width), F32), struct((8, 128), F32)],
        0,
        [g_fc_all, g_proj_all, g_attn_all, g_feat_all, g_norm],
        [item for shape in shapes for item in scatter_scratch(sizes, shape)]
        + total_scratch(sizes, (8, width))
        + total_scratch(sizes, (8, 128)),
        3,
        "scatter",
        0,
    )

    norm_grads = norm_sum[:4]
    grad_norm = jnp.sqrt(jnp.sum(square_sum) + jnp.sum(norm_grads * norm_grads))
    factor = clip_limit / jnp.maximum(grad_norm, clip_limit)
    reduced_qkv = jnp.stack([g_attn[:, 256 * j : 256 * j + head_width] for j in range(3)], axis=1)
    reduced_out = jnp.concatenate(
        [g_attn[:, 256 * j + head_width : 256 * j + 256] for j in range(3)], axis=1
    ).T
    reduced_feat = (
        g_feat[: heads * depth].reshape(heads, depth, 2, HD).transpose(2, 0, 1, 3).reshape(2, heads, depth * HD)
    )
    up_qkv = adamw_update(w_qkv, first_qkv, second_qkv, reduced_qkv, factor, 0.02, 0.1)
    up_out = adamw_update(w_out, first_out, second_out, reduced_out, factor, 0.4, 0.1)
    up_feat = adamw_update(w_feat, first_feat, second_feat, reduced_feat, factor, 0.15, 0.1)
    up_fc = adamw_update(w_fc, first_fc, second_fc, g_fc.T, factor, 0.02, 0.1)
    up_proj = adamw_update(w_proj, first_proj, second_proj, g_proj, factor, 0.01, 0.1)
    up_norms = adamw_update(norm_params, first_norms, second_norms, norm_grads, factor, 0.3, 0.0)
    return (
        grad_norm,
        block_out,
        block_in_grad,
        up_qkv[0],
        up_out[0],
        up_feat[0],
        up_fc[0],
        up_proj[0],
        up_norms[0],
        up_qkv[1],
        up_out[1],
        up_feat[1],
        up_fc[1],
        up_proj[1],
        up_norms[1],
        up_qkv[2],
        up_out[2],
        up_feat[2],
        up_fc[2],
        up_proj[2],
        up_norms[2][:2],
        up_norms[2][2:],
        up_qkv[0].astype(BF16),
        up_out[0].astype(BF16),
        up_feat[0].astype(BF16),
        up_fc[0].astype(BF16),
        up_proj[0].astype(BF16),
        up_norms[0].astype(BF16),
    )


def solution(mesh):
    everything = ("dp", "batch", "head")
    rows = P(everything, None)
    qkv, out, feat = P(("dp", "batch"), None, "head"), P("head", ("dp", "batch")), P(None, "head", ("dp", "batch"))
    fc, proj, whole = P(None, everything), P(everything, None), P()
    weights = (qkv, out, feat, fc, proj, whole)
    in_specs = (rows, rows, P(("dp", "batch"), None)) + weights
    for spec in weights:
        in_specs += (spec, spec)
    out_specs = (whole, rows, rows) + weights + weights + weights[:5] + (whole, whole) + weights
    sizes = (mesh.shape["dp"], mesh.shape["batch"], mesh.shape["head"])
    return jax.shard_map(
        functools.partial(on_device, sizes), mesh=mesh, in_specs=in_specs, out_specs=out_specs, check_vma=False
    )
```

time: 1140 us -> 446 us (0.39)
  waiting for transfers between devices: 458 us -> 0 us
  Pallas kernels: 0 us -> 397 us
  matrix products: 306 us -> 0 us
  blocking collectives: 147 us -> 0 us
  local copies, waits for them, and re-layouts: 109 us -> 21.9 us
  other arithmetic: 89.4 us -> 22.2 us
  between operations: 21.5 us -> 3.33 us
    pallas_call x0 -> x5, Pallas kernels: none -> 397 us  [call(): pl.pallas_call(kernel, out_shape=tuple(outs), in_specs=specs, out_specs=t...]
    dot_general x34 -> x0, matrix products: 286 us -> none  [the longest x3 48.5 us: linear_core(): jnp.einsum('nihf,nhfd->nihd', query_blocks, prior_state, precision=highest)]
    reduce_scatter x6 -> x0, waiting for transfers between devices: 245 us -> none  [the longest x1 65.3 us: on_device(): lax.psum_scatter(grad_qkv.astype(jnp.bfloat16), ('dp', 'batch'), scatter_...]
    unnamed x18 -> x0, waiting for transfers between devices: 129 us -> none
    all_gather x3 -> x0, blocking collectives: 108 us -> none  [the longest x1 46.7 us: on_device(): lax.all_gather(w_qkv.astype(jnp.bfloat16), ('dp', 'batch'), axis=0, tiled...]
    all_gather x6 -> x0, waiting for transfers between devices: 84.5 us -> none  [the longest x1 35.6 us: on_device(): lax.all_gather(fc_part, 'head', axis=1, tiled=True)]
    psum x1 -> x0, blocking collectives: 39.8 us -> none  [on_device(): lax.psum((norm_terms, partial_sq), ('dp', 'batch', 'head'))]
    reduce_sum x18 -> x2, other arithmetic: 41.3 us -> 2.63 us  [on_device(): grad_norm = jnp.sqrt(jnp.sum(square_sum) + jnp.sum(norm_grads * norm_grads))]
  transfers between devices with their start and end apart: 15 -> 0, of which waited for: 10 -> 0; matrix products, arithmetic and copies ran while one was open for 38% -> 0% of each run, Pallas kernels for 0% -> 0%
where the time goes in v1:
time: 446 us; the launch traced here: 444 us
  Pallas kernels  397 us (89%)
  other arithmetic  22.2 us (5%)
  local copies, waits for them, and re-layouts  21.9 us (5%)
    pallas_call x5, Pallas kernels, call(): pl.pallas_call(kernel, out_shape=tuple(outs), in_specs=specs, out_specs=t...  397 us
    unnamed x22, local copies, waits for them, and re-layouts  12.3 us

profile of v1, /device:TPU:0, one launch (start us, length us, event | category | flops | bytes accessed | tf_op | source)
XLA Modules:
  0.0 444.4 jit_solution(15802436013257461048)
XLA Ops:
  0.7 1.0 copy.62
  1.8 1.0 convert.34
  2.8 0.8 concatenate.16.refs_0_
  3.5 1.6 convert_bitcast_fusion.1.refs_2_
  5.2 1.6 convert_element_type.65.refs_3_
  8.3 86.0 %gather.1 = (bf16[2,4,4,96,768]{4,3,2,1,0:T(8,128)(2,1)}, bf16[2,4,4,32,128]{4,3,2,1,0:T(8,128)(2,1)}, bf16[2,4,4,96,768]{4,3,2,1,0:T(8,128)(2,1)}, bf16[2,4,4,96,768]{4,3,2,1,0:T(8,128)(2,1)}) custom-call(bf16[96,768]{1,0:T(8,128)(2,1)} %concatenate.16.refs_0_, bf16[32,128]{1,0:T(8,128)(2,1)} %pad.9.refs_1_, bf16[96,768]{1,0:T(8,128)(2,1)} %convert_bitcast_fusion.1.refs_2_, ...), custom_call_target="tpu_custom_call" | custom-call | bytes 14868480 | tf_op jit(solution)/shard_map/gather/pallas_call | solution.py:784
  94.3 1.0 convert_bitcast_fusion
  95.3 0.8 copy.64
  96.7 56.8 %attention_forward.1 = (bf16[1024,768]{1,0:T(8,128)(2,1)}, bf16[4,1024,768]{2,1,0:T(8,128)(2,1)}, bf16[4,1024,384]{2,1,0:T(8,128)(2,1)}, bf16[4,1024,384]{2,1,0:...) custom-call(s32[1,2]{1,0:T(1,128)} %len_ref.3, ...), custom_call_target="tpu_custom_call" | custom-call | flops 10000000000 | bytes 38154248 | tf_op jit(solution)/shard_map/attention_forward/pallas_call | solution.py:784
  153.5 57.5 %feed_forward.1 = (bf16[1024,768]{1,0:T(8,128)(2,1)}, f32[1024,768]{1,0:T(8,128)}, bf16[1024,768]{1,0:T(8,128)(2,1)}, bf16[2,4,4,96,768]{4,3,2,1,0:T(8,128)(2,1)...) custom-call(bf16[1024,768]{1,0:T(8,128)(2,1)} %get-tuple-element.61.hidden_ref, bf16[1024,768]{1,0:T(8,128)(2,1)} %dy_ref.1, ...), custom_call_target="tpu_custom_call" | custom-call | flops 30000001024 | bytes 31494144 | tf_op jit(solution)/shard_map/feed_forward/pallas_call | solution.py:784
  211.0 89.3 %attention_backward.1 = (f32[1024,768]{1,0:T(8,128)}, bf16[2,4,4,96,768]{4,3,2,1,0:T(8,128)(2,1)}, f32[2,4,3,64,128]{4,3,2,1,0:T(8,128)}, f32[8,768]{1,0:T(8,128)}) custom-call(s32[1,2]{1,0:T(1,128)} %len_ref.3, bf16[1024,768]{1,0:T(8,128)(2,1)} %x_ref.3, bf16[1024,768]{1,0:T(8,128)(2,1)} %get-tuple-element.67.normed_ref, ...), custom_call_target="tpu_custom_call" | custom-call | flops 20000000000 | bytes 46460936 | tf_op jit(solution)/shard_map/attention_backward/pallas_call | solution.py:784
  300.3 1.6 subtract_convert_fusion
  302.9 107.4 %scatter.1 = (f32[96,768]{1,0:T(8,128)}, f32[96,768]{1,0:T(8,128)}, f32[96,768]{1,0:T(8,128)}, f32[32,128]{1,0:T(8,128)}, f32[8,768]{1,0:T(8,128)}, /*index=5*/f32[8,128]{1,0:T(8,128)}) custom-call(bf16[2,4,4,96,768]{4,3,2,1,0:T(8,128)(2,1)} %get-tuple-element.65.refs_0_, bf16[2,4,4,96,768]{4,3,2,1,0:T(8,128)(2,1)} %get-tuple-element.66.refs_1_, ...), custom_call_target="tpu_custom_call" | custom-call | bytes 15372288 | tf_op jit(solution)/shard_map/scatter/pallas_call | solution.py:784
  410.3 1.4 multiply_reduce_fusion
  411.7 1.3 reduce_sum.18
  414.4 1.4 fusion.8
  416.4 2.2 fusion.10
  418.5 2.3 fusion.12
  421.5 1.6 copy.71
  423.1 0.8 mul.290
  423.9 1.4 fusion.15
  425.3 1.6 fusion.21
  426.9 1.6 copy.67
  428.5 1.6 copy.68
  430.2 1.9 fusion.17
  432.0 1.6 copy.72
  433.7 1.6 copy.73
  435.3 1.6 copy.74
  436.9 1.5 copy.75
  438.5 1.0 slice_bitcast_fusion.5
  439.5 2.2 fusion.19
  441.6 1.7 copy.80
  (30 shorter events, 4.5 us)
Async XLA Ops:
  0.7 95.4 %copy-start.5 = (f32[4,768]{1,0:T(4,128)S(1)}, f32[4,768]{1,0:T(4,128)}, u32[]{:S(2)}) copy-start(f32[4,768]{1,0:T(4,128)} %param.29) | copy-start | bytes 36868
  302.9 113.4 %copy-start.1 = (f32[96,768]{1,0:T(8,128)S(1)}, f32[96,768]{1,0:T(8,128)}, u32[]{:S(2)}) copy-start(f32[96,768]{1,0:T(8,128)} %param.28) | copy-start | bytes 884740
  302.9 113.4 %copy-start.4 = (f32[96,768]{1,0:T(8,128)S(1)}, f32[96,768]{1,0:T(8,128)}, u32[]{:S(2)}) copy-start(f32[96,768]{1,0:T(8,128)} %param.38) | copy-start | bytes 884740
  302.9 115.6 %copy-start.2 = (f32[768,96]{0,1:T(8,128)S(1)}, f32[768,96]{0,1:T(8,128)}, u32[]{:S(2)}) copy-start(f32[768,96]{0,1:T(8,128)} %param.27) | copy-start | bytes 884740
  414.3 6.5 %copy-start.6 = (f32[32,128]{1,0:T(8,128)S(1)}, f32[32,128]{1,0:T(8,128)}, u32[]{:S(2)}) copy-start(f32[32,128]{1,0:T(8,128)} %get-tuple-element.87) | copy-start | bytes 49156
  418.5 21.0 %copy-start.3 = (f32[96,3,192]{2,0,1:T(8,128)S(1)}, f32[96,3,192]{2,0,1:T(8,128)}, u32[]{:S(2)}) copy-start(f32[96,3,192]{2,0,1:T(8,128)} %param.24) | copy-start | bytes 663556
  420.8 20.8 %copy-start = (f32[1024,768]{1,0:T(8,128)S(1)}, f32[1024,768]{1,0:T(8,128)}, u32[]{:S(2)}) copy-start(f32[1024,768]{1,0:T(8,128)} %get-tuple-element.216) | copy-start | bytes 9437188

commit v2 on v1

v2 whole, which is shorter than its diff:
```python
import functools

import jax
import jax.numpy as jnp
from jax import lax
from jax.experimental import pallas as pl
from jax.experimental.pallas import tpu as pltpu
from jax.sharding import PartitionSpec as P

HD = 64
STEP = 8
CHUNK = 256
FEAT_ROWS = 32
MESH = pl.DeviceIdType.MESH
VMEM = pltpu.VMEM
F32 = jnp.float32
BF16 = jnp.bfloat16

norm_eps = 1e-05
beta_one = 0.9
beta_two = 0.95
adam_eps = 1e-08
clip_limit = 1.0


def dot(left, right):
    return lax.dot_general(left, right, (((1,), (0,)), ((), ())), preferred_element_type=F32)


def dot_nt(left, right):
    return lax.dot_general(left, right, (((1,), (1,)), ((), ())), preferred_element_type=F32)


def dot_tn(left, right):
    return lax.dot_general(left, right, (((0,), (0,)), ((), ())), preferred_element_type=F32)


def flip_bit(value, bit, on=1):
    low = 2**bit
    return value + on * (low - 2 * low * lax.rem(value // low, 2))


class Network:
    def __init__(self, sizes):
        self.X, self.Z, self.H = sizes
        self.dp, self.b, self.h = (lax.axis_index(name) for name in ("dp", "batch", "head"))
        dp_bits, head_bits = self.X.bit_length() - 1, self.H.bit_length() - 1
        if (self.X, self.H) == (2, 4):
            def first(dp, h):
                odd = lax.rem(h, 2)
                return flip_bit(dp, 0, 1 - odd), flip_bit(h, 1, odd)

            def second(dp, h):
                odd = lax.rem(h, 2)
                return flip_bit(dp, 0, odd), flip_bit(h, 1, 1 - odd)

            self.flips = [first, second, lambda dp, h: (dp, flip_bit(h, 0))]
        else:
            self.flips = [lambda dp, h, k=k: (flip_bit(dp, k), h) for k in range(dp_bits)]
            self.flips += [lambda dp, h, k=k: (dp, flip_bit(h, k)) for k in reversed(range(head_bits))]
        self.sets = [()]
        for k in range(len(self.flips)):
            self.sets += [s + (k,) for s in self.sets]
        self.index = {s: i for i, s in enumerate(self.sets)}

    def coord(self, chosen):
        dp, h = self.dp, self.h
        for k in sorted(chosen, reverse=True):
            dp, h = self.flips[k](dp, h)
        return dp, h

    def behind(self, off):
        return lax.rem(self.b + self.Z - off, self.Z)

    def ahead(self, off):
        return lax.rem(self.b + off, self.Z)

    def slot(self, chosen, off):
        dp, h = self.coord(chosen)
        return dp, self.behind(off), h

    def partner(self, k):
        dp, h = self.flips[k](self.dp, self.h)
        return {"dp": dp, "batch": self.b, "head": h}

    def along(self, b):
        return {"dp": self.dp, "batch": b, "head": self.h}

    def stages(self, chosen):
        return range(max(chosen) + 1 if chosen else 0, len(self.flips))

    def barrier(self, chained=False):
        sem = pltpu.get_barrier_semaphore()
        devices = [self.along(self.ahead(off)) for off in range(1, self.Z)]
        devices += [self.partner(k) for k in range(len(self.flips))]
        if chained:
            devices += [{"head": lax.rem(self.h + step, self.H)} for step in (1, self.H - 1)]
        for device in devices:
            pl.semaphore_signal(sem, inc=1, device_id=device, device_id_type=MESH)
        pl.semaphore_wait(sem, len(devices))


def gather_sems(sizes):
    X, Z, H = sizes
    n = X * H - 1
    return [pltpu.SemaphoreType.DMA((n + 1, Z)), pltpu.SemaphoreType.DMA((n + 1, Z))]


class Gather:
    def __init__(self, net, shard, buf, send, recv):
        self.net, self.shard, self.buf, self.send, self.recv = net, shard, buf, send, recv

    def source(self, chosen, off):
        return self.shard if chosen == () and off == 0 else self.buf.at[self.net.slot(chosen, off)]

    def copy(self, chosen, off, k):
        net = self.net
        into = net.index[chosen + (k,)]
        return pltpu.make_async_remote_copy(
            src_ref=self.source(chosen, off), dst_ref=self.buf.at[net.slot(chosen, off)],
            send_sem=self.send.at[into, off], recv_sem=self.recv.at[into, off],
            device_id=net.partner(k), device_id_type=MESH,
        )

    def copy_along(self, off):
        net = self.net
        return pltpu.make_async_remote_copy(
            src_ref=self.shard, dst_ref=self.buf.at[net.slot((), 0)],
            send_sem=self.send.at[0, off], recv_sem=self.recv.at[0, off],
            device_id=net.along(net.ahead(off)), device_id_type=MESH,
        )

    def copy_own(self):
        return pltpu.make_async_copy(self.shard, self.buf.at[self.net.slot((), 0)], self.send.at[0, 0])

    def arrived(self, chosen, off):
        net = self.net
        place = self.buf.at[net.slot(chosen, off)]
        into = net.index[chosen]
        pltpu.make_async_remote_copy(
            src_ref=place, dst_ref=place, send_sem=self.send.at[into, off], recv_sem=self.recv.at[into, off],
            device_id=net.partner(0), device_id_type=MESH,
        ).wait_recv()

    def begin(self):
        net = self.net
        for k in net.stages(()):
            self.copy((), 0, k).start()
        for off in range(1, net.Z):
            self.copy_along(off).start()
        self.copy_own().start()

    def step(self, chosen, off):
        self.arrived(chosen, off)
        for k in self.net.stages(chosen):
            self.copy(chosen, off, k).start()

    def steps(self):
        net = self.net
        order = [((), off) for off in range(1, net.Z)]
        for chosen in net.sets[1:]:
            order += [(chosen, off) for off in range(net.Z)]
        half = len(net.sets) // 2 * net.Z - 1
        return [functools.partial(self.step, *item) for item in order[:half]], [
            functools.partial(self.step, *item) for item in order[half:]
        ]

    def finish(self):
        net = self.net
        for off in range(1, net.Z):
            self.copy_along(off).wait_send()
        for chosen in net.sets:
            for k in net.stages(chosen):
                for off in range(net.Z):
                    self.copy(chosen, off, k).wait_send()


def scatter_scratch(sizes, shape):
    X, Z, H = sizes
    n = X * H
    return [VMEM((n, Z) + shape, BF16), pltpu.SemaphoreType.DMA((n, Z)), pltpu.SemaphoreType.DMA((n, Z))]


class Scatter:
    def __init__(self, net, part, inbox, send, recv):
        self.net, self.part, self.inbox, self.send, self.recv = net, part, inbox, send, recv
        self.last = len(net.flips) - 1

    def sum_at(self, chosen, off):
        return self.inbox.at[self.net.index[chosen + (self.last,)], off]

    def copy(self, chosen, off, k):
        net = self.net
        into = net.index[chosen + (k,)]
        first = k == self.last
        source = self.part.at[net.slot(chosen + (k,), off)] if first else self.sum_at(chosen + (k,), off)
        return pltpu.make_async_remote_copy(
            src_ref=source, dst_ref=self.inbox.at[into, off], send_sem=self.send.at[into, off],
            recv_sem=self.recv.at[into, off], device_id=net.partner(k), device_id_type=MESH,
        )

    def copy_along(self, off):
        net = self.net
        return pltpu.make_async_remote_copy(
            src_ref=self.sum_at((), off), dst_ref=self.inbox.at[0, off], send_sem=self.send.at[0, off],
            recv_sem=self.recv.at[0, off], device_id=net.along(net.behind(off)), device_id_type=MESH,
        )

    def early_sets(self):
        return self.net.sets[: len(self.net.sets) // 2]

    def begin(self, ready=None, offs=None):
        for chosen in reversed(self.early_sets()):

            def start(chosen=chosen):
                for off in range(self.net.Z) if offs is None else offs:
                    self.copy(chosen, off, self.last).start()

            if ready is None:
                start()
            else:
                pl.when(ready(*self.net.coord(chosen + (self.last,))))(start)

    def step(self, chosen, off):
        net = self.net
        total = self.part[net.slot(chosen, off)].astype(F32)
        for k in reversed(net.stages(chosen)):
            self.copy(chosen, off, k).wait_recv()
            total = total + self.inbox[net.index[chosen + (k,)], off].astype(F32)
        self.sum_at(chosen, off)[...] = total.astype(BF16)
        if chosen:
            self.copy(chosen[:-1], off, chosen[-1]).start()
        elif off:
            self.copy_along(off).start()

    def result(self):
        net = self.net
        total = self.sum_at((), 0)[...].astype(F32)
        for off in range(1, net.Z):
            self.copy_along(off).wait_recv()
            total = total + self.inbox[0, off].astype(F32)
        return total

    def finish(self):
        net = self.net
        for off in range(1, net.Z):
            self.copy_along(off).wait_send()
        for chosen in net.sets:
            for k in net.stages(chosen):
                for off in range(net.Z):
                    self.copy(chosen, off, k).wait_send()


def total_scratch(sizes, shape):
    X, Z, H = sizes
    bits = (X * H).bit_length() - 1
    return [
        VMEM((Z + 2 * bits,) + shape, F32),
        pltpu.SemaphoreType.DMA((Z + bits,)),
        pltpu.SemaphoreType.DMA((Z + bits,)),
    ]


def total_over_all(net, value, slots, send, recv):
    Z = net.Z
    slots[net.b] = value
    copies = []
    for off in range(1, Z):
        copies.append(
            pltpu.make_async_remote_copy(
                src_ref=slots.at[net.b], dst_ref=slots.at[net.b], send_sem=send.at[off], recv_sem=recv.at[off],
                device_id=net.along(net.ahead(off)), device_id_type=MESH,
            )
        )
    for copy in copies:
        copy.start()
    for off in range(1, Z):
        place = slots.at[net.behind(off)]
        pltpu.make_async_remote_copy(
            src_ref=place, dst_ref=place, send_sem=send.at[off], recv_sem=recv.at[off],
            device_id=net.along(net.ahead(off)), device_id_type=MESH,
        ).wait_recv()
    for copy in copies:
        copy.wait_send()
    value = slots[0]
    for off in range(1, Z):
        value = value + slots[off]
    for k in range(len(net.flips)):
        slots[Z + 2 * k] = value
        copy = pltpu.make_async_remote_copy(
            src_ref=slots.at[Z + 2 * k], dst_ref=slots.at[Z + 2 * k + 1], send_sem=send.at[Z + k],
            recv_sem=recv.at[Z + k], device_id=net.partner(k), device_id_type=MESH,
        )
        copy.start()
        copy.wait()
        value = value + slots[Z + 2 * k + 1]
    return value


class Mover:
    def __init__(self, sems):
        self.sems, self.used = sems, 0

    def plan(self, source, target, count=None):
        at = self.used
        self.used += 1 if count is None else count

        def make(i):
            if count is None:
                return pltpu.make_async_copy(source, target, self.sems.at[at])
            return pltpu.make_async_copy(source.at[i], target.at[i], self.sems.at[at + i])

        return make


def norm_stats(values):
    mean = jnp.mean(values, axis=-1, keepdims=True)
    center = values - mean
    spread = jnp.mean(center * center, axis=-1, keepdims=True)
    return center, lax.rsqrt(spread + norm_eps)


def norm_backward(values, gain_row, grads):
    center, scale = norm_stats(values)
    normal = center * scale
    inner = grads * gain_row
    part = jnp.mean(inner * normal, axis=-1, keepdims=True)
    back = scale * (inner - jnp.mean(inner, axis=-1, keepdims=True) - normal * part)
    return back, jnp.sum(grads * normal, axis=0, keepdims=True), jnp.sum(grads, axis=0, keepdims=True)


def low_half(shape):
    return lax.rem(lax.broadcasted_iota(jnp.int32, shape, len(shape) - 1), 128) < HD


def swap_halves(values):
    cols = values.shape[1]
    parts = [pltpu.roll(values[:, at : at + 128], HD, 1) for at in range(0, cols, 128)]
    return parts[0] if len(parts) == 1 else jnp.concatenate(parts, axis=1)


def feature_pair(scaled, live):
    low = low_half(scaled.shape)
    top = jnp.max(jnp.where(low, scaled, -jnp.inf), axis=-1, keepdims=True)
    bottom = jnp.max(jnp.where(low, -jnp.inf, scaled), axis=-1, keepdims=True)
    powers = jnp.exp(scaled - jnp.where(low, top, bottom))
    first = jnp.sum(jnp.where(low, powers, 0.0), axis=-1, keepdims=True)
    second = jnp.sum(jnp.where(low, 0.0, powers), axis=-1, keepdims=True)
    return powers * (live / jnp.where(low, first, second))


def feature_back(feature, grads):
    low = low_half(feature.shape)
    product = feature * grads
    first = jnp.sum(jnp.where(low, product, 0.0), axis=-1, keepdims=True)
    second = jnp.sum(jnp.where(low, 0.0, product), axis=-1, keepdims=True)
    return product - feature * jnp.where(low, first, second)


class Rows:
    def __init__(self, len_ref, rows, h):
        self.first_len = len_ref[0, 0]
        self.both_len = len_ref[0, 0] + len_ref[0, 1]
        self.start = h * rows
        self.rows = rows

    def second(self, row):
        return row >= self.first_len

    def column(self, chunk):
        return self.start + chunk * CHUNK + lax.broadcasted_iota(jnp.int32, (CHUNK, 1), 0)

    def live(self, chunk):
        return (self.column(chunk) < self.both_len).astype(F32)

    def second_column(self, chunk):
        return self.second(self.column(chunk))

    def masks(self, chunk):
        base = self.start + chunk * CHUNK
        down = base + lax.broadcasted_iota(jnp.int32, (CHUNK, CHUNK), 0)
        across = base + lax.broadcasted_iota(jnp.int32, (CHUNK, CHUNK), 1)
        same = (down >= self.first_len) == (across >= self.first_len)
        return same & (across <= down), same & (across >= down)

    def scalar(self, row):
        return jnp.where(self.second(row), 1.0, 0.0).astype(F32)

    def before(self):
        return self.scalar(self.start - 1)

    def first(self):
        return self.scalar(self.start)

    def last(self):
        return self.scalar(self.start + self.rows - 1)

    def after(self):
        return self.scalar(self.start + self.rows)


def with_ones(block, head, low):
    ones = jnp.ones_like(block)
    return jnp.where(low, block, ones) if head % 2 == 0 else jnp.where(low, ones, block)


def by_sequence(values, second):
    zero = jnp.zeros_like(values)
    return jnp.concatenate([jnp.where(second, zero, values), jnp.where(second, values, zero)], axis=1)


class Chain:
    def __init__(self, step, n, h, same, picked, cin, cout, send, recv):
        self.first = h == (0 if step == 1 else n - 1)
        self.final = h == (n - 1 if step == 1 else 0)
        self.neighbour = {"head": lax.rem(h + n + step, n)}
        self.same, self.picked, self.cin, self.cout, self.send, self.recv = same, picked, cin, cout, send, recv

    def copy(self, g):
        return pltpu.make_async_remote_copy(
            src_ref=self.cout.at[g], dst_ref=self.cin.at[g], send_sem=self.send.at[g], recv_sem=self.recv.at[g],
            device_id=self.neighbour, device_id_type=MESH,
        )

    def step(self, g):
        @pl.when(self.first)
        def _():
            self.cin[g] = jnp.zeros_like(self.cin[g])

        @pl.when(jnp.logical_not(self.first))
        def _():
            self.copy(g).wait_recv()

        @pl.when(jnp.logical_not(self.final))
        def _():
            self.cout[g] = (self.picked[g] + self.cin[g].astype(F32) * self.same).astype(BF16)
            self.copy(g).start()

    def finish(self, n):
        @pl.when(jnp.logical_not(self.final))
        def _():
            for g in range(n):
                self.copy(g).wait_send()


def group_at(h, i, n):
    bits = n.bit_length() - 1
    for k in range(bits):
        h = flip_bit(h, bits - 1 - k, lax.rem(i // 2**k, 2))
    return h


def run_at(slots, i, count):
    for k in range(count):
        if slots.get(k):

            @pl.when(i == k)
            def _(items=slots[k]):
                for item in items:
                    item()


def rest_of(slots, count):
    for k in sorted(slots):
        if k >= count:
            for item in slots[k]:
                item()


def equal(a, b):
    return a * b + (1.0 - a) * (1.0 - b)


def attention_forward(
    sizes, heads, depth, len_ref, x_ref, wqkv_ref, wout_ref, wfeat_ref, wfc_ref, wproj_ref, norm_in,
    normed_out, qkv_out, fq_out, fk_out, state_out, mixed_out, rden_out, wo_out, maps_out, middle_out, hidden_out,
    attn_out, fc_out, proj_out,
    normed_ref, qkv_ref, fq_ref, fk_ref, state_ref, mixed_ref, rden_ref, wo_ref, maps_ref, middle_ref, hidden_ref,
    attn_shard, feat_shard, fc_shard, proj_shard, feat_rows, norm_ref,
    w_ref, feat_ref, pairs_ref, total_ref, picked_ref, cin, cout, chain_send, chain_recv, move_sem,
    *sems,
):
    X, Z, groups = sizes
    lanes_here = heads * HD
    for j in range(3):
        attn_shard[:, 256 * j : 256 * j + 128] = wqkv_ref[j, :, 0:128].astype(BF16)
        attn_shard[:, 256 * j + 128 : 256 * j + 256] = jnp.concatenate(
            [wqkv_ref[j, :, 128:lanes_here], wout_ref[HD * j : HD * j + HD].T], axis=1
        ).astype(BF16)
    feat_rows[...] = jnp.zeros_like(feat_rows)
    low_row = low_half((1, 128))
    for j in range(heads):
        for d in range(depth):
            q, k = (wfeat_ref[j, side : side + 1, 128 * (d // 2) : 128 * (d // 2) + 128] for side in range(2))
            row = jnp.where(low_row, q, pltpu.roll(k, HD, 1)) if d % 2 == 0 else jnp.where(low_row, pltpu.roll(q, HD, 1), k)
            feat_rows[depth * j + d : depth * j + d + 1] = row
    feat_shard[...] = feat_rows[...].astype(BF16)
    fc_shard[...] = wfc_ref[...].astype(BF16)
    proj_shard[...] = wproj_ref[...].astype(BF16)
    norm_ref[...] = norm_in[...].astype(BF16).astype(F32)
    net = Network(sizes)
    h = net.h
    rows, width = x_ref.shape
    chunks = rows // CHUNK
    seq = Rows(len_ref, rows, h)
    low = low_half((CHUNK, 128))
    mover = Mover(move_sem)
    push_normed, push_wo, push_maps, push_attn = (
        mover.plan(*pair)
        for pair in ((normed_ref, normed_out), (wo_ref, wo_out), (maps_ref, maps_out), (w_ref, attn_out))
    )
    push_qkv, push_fq, push_fk, push_state, push_mixed, push_rden = (
        mover.plan(*pair, groups)
        for pair in (
            (qkv_ref, qkv_out), (fq_ref, fq_out), (fk_ref, fk_out), (state_ref, state_out), (mixed_ref, mixed_out),
            (rden_ref, rden_out),
        )
    )
    push_middle, push_hidden = mover.plan(middle_ref, middle_out), mover.plan(hidden_ref, hidden_out)

    net.barrier(chained=True)
    shards = (attn_shard, feat_shard, fc_shard, proj_shard)
    attn, feat, fc, proj = (
        Gather(net, shard, buf, sems[2 * i], sems[2 * i + 1])
        for i, (shard, buf) in enumerate(zip(shards, (w_ref, feat_ref, fc_out, proj_out)))
    )
    feat.begin()
    attn.begin()

    def first_norm(c, _):
        at = pl.ds(pl.multiple_of(c * CHUNK, CHUNK), CHUNK)
        center, scale = norm_stats(x_ref[at].astype(F32))
        normed_ref[at] = (center * scale * norm_ref[0:1] + norm_ref[1:2]).astype(BF16)
        return 0

    feat.copy_own().wait()
    attn.copy_own().wait()
    feat_on, feat_in = feat.steps()
    attn_on, attn_in = attn.steps()
    for step in feat_on[: Z - 1] + attn_on[: Z - 1]:
        step()
    lax.fori_loop(0, chunks, first_norm, 0)
    push_normed(0).start()
    late = Z if (X, groups) == (2, 4) else 0
    now = len(attn_on) - late
    for step in attn_on[Z - 1 : now] + feat_on[Z - 1 :] + feat_in:
        step()

    maps_ref[...] = jnp.zeros_like(maps_ref)
    low64 = low_half((HD, 128))
    for i in range(X * Z):
        for g in range(groups):
            block = feat_ref[i // Z, i % Z, g].astype(F32)
            for j in range(heads):
                pairs_ref[g * heads + j, depth * i : depth * i + depth] = block[depth * j : depth * j + depth]
    for g in range(groups):
        for j in range(heads):
            pair = pairs_ref[g * heads + j]
            swapped = pltpu.roll(pair, HD, 1)
            at = slice(HD * j, HD * j + HD), slice(128 * j, 128 * j + 128)
            maps_ref[0, g, at[0], at[1]] = jnp.where(low64, pair, -swapped).astype(BF16)
            maps_ref[1, g, at[0], at[1]] = jnp.where(low64, swapped, -pair).astype(BF16)
    push_maps(0).start()

    turns = groups * chunks
    slots = {}
    if late:
        for k, step in enumerate(attn_on[now:]):
            slots.setdefault(k, []).append(step)
        slots.setdefault(2 * chunks, []).extend(attn_in)
    else:
        slots[0] = list(attn_in)
    slots.setdefault(1, []).extend([fc.begin, proj.begin])
    fc_on, fc_in = fc.steps()
    proj_on, proj_in = proj.steps()
    for k, pair in enumerate(zip(fc_on, proj_on)):
        slots.setdefault(4 + k * (2 * turns - 6) // len(fc_on), []).extend(pair)
    mix_slots = {k - turns: items for k, items in slots.items() if k >= turns}
    last = seq.last()

    def project(i, _):
        g = group_at(h, i, groups)
        for j in range(heads):
            total_ref[j] = jnp.zeros_like(total_ref[j])

        def part(c, _):
            run_at(slots, i * chunks + c, turns)
            at = pl.ds(pl.multiple_of(c * CHUNK, CHUNK), CHUNK)
            live, second = seq.live(c), seq.second_column(c)
            qkv = dot(normed_ref[at], w_ref[:, :, g].reshape(width, width)).astype(BF16)
            qkv_ref[g, at] = qkv
            scaled_q = dot(qkv[:, 0:256], maps_ref[0, g])
            scaled_k = dot(qkv[:, 256:512], maps_ref[1, g])
            for j in range(heads):
                lanes = slice(128 * j, 128 * j + 128)
                fq_ref[g, at, lanes] = feature_pair(scaled_q[:, lanes], live).astype(BF16)
                fk = feature_pair(scaled_k[:, lanes], live).astype(BF16)
                fk_ref[g, at, lanes] = fk
                block = qkv[:, 512 + 128 * (j // 2) : 640 + 128 * (j // 2)]
                values = by_sequence(with_ones(block, j, low), second)
                state_ref[g, j, c] = total_ref[j].astype(BF16)
                total_ref[j] += dot_tn(fk, values)
            return 0

        lax.fori_loop(0, chunks, part, 0)
        for push in (push_qkv, push_fq, push_fk):
            push(g).start()
        for j in range(heads):
            picked_ref[g, j] = total_ref[j, :, :128] * (1.0 - last) + total_ref[j, :, 128:] * last
        weight = w_ref[:, :, g].reshape(width, width)
        lowd = low_half((width, 128))
        a = swap_halves(weight[:, 128:256].astype(F32))
        b = weight[:, 384:512].astype(F32)
        c_ = swap_halves(weight[:, 640:768].astype(F32))
        wo_ref[g, :, 0:128] = jnp.where(lowd, a, b).astype(BF16)
        wo_ref[g, :, 128:256] = jnp.where(lowd, c_, 0.0).astype(BF16)
        return 0

    lax.fori_loop(0, groups, project, 0)
    push_wo(0).start()
    push_attn(0).start()

    before = seq.before()
    chain = Chain(1, groups, h, equal(before, last), picked_ref, cin, cout, chain_send, chain_recv)

    def mix(g, _):
        chain.step(g)

        def part(c, _):
            run_at(mix_slots, g * chunks + c, turns)
            at = pl.ds(pl.multiple_of(c * CHUNK, CHUNK), CHUNK)
            live, second = seq.live(c), seq.second_column(c)
            lower, _ = seq.masks(c)
            found = []
            for j in range(heads):
                lanes = slice(128 * j, 128 * j + 128)
                fq, fk = fq_ref[g, at, lanes], fk_ref[g, at, lanes]
                carry = cin[g, j].astype(F32)
                prior = jnp.concatenate([carry * (1.0 - before), carry * before], axis=1)
                state = (state_ref[g, j, c].astype(F32) + prior).astype(BF16)
                state_ref[g, j, c] = state
                scores = jnp.where(lower, dot_nt(fq, fk), 0.0).astype(BF16)
                block = qkv_ref[g, at, 512 + 128 * (j // 2) : 640 + 128 * (j // 2)]
                inter = dot(fq, state)
                found.append(
                    dot(scores, with_ones(block, j, low)) + jnp.where(second, inter[:, 128:], inter[:, :128])
                )
            pair = jnp.where(low, found[0], found[1])
            rden = 1.0 / (swap_halves(jnp.where(low, found[1], found[0])) + (1.0 - live))
            mixed_ref[g, at, 0:128] = (pair * rden).astype(BF16)
            rden_ref[g, at, 0:128] = rden.astype(BF16)
            rden = jnp.where(low, 1.0 / (swap_halves(found[2]) + (1.0 - live)), 1.0)
            mixed_ref[g, at, 128:256] = jnp.where(low, found[2] * rden, 0.0).astype(BF16)
            rden_ref[g, at, 128:256] = rden.astype(BF16)
            return 0

        lax.fori_loop(0, chunks, part, 0)
        for push in (push_state, push_mixed, push_rden):
            push(g).start()
        return 0

    lax.fori_loop(0, groups, mix, 0)
    rest_of(mix_slots, turns)

    def close(c, _):
        at = pl.ds(pl.multiple_of(c * CHUNK, CHUNK), CHUNK)
        attended = dot_nt(mixed_ref[0, at], wo_ref[0])
        for g in range(1, groups):
            attended = attended + dot_nt(mixed_ref[g, at], wo_ref[g])
        middle = x_ref[at].astype(F32) + attended
        middle_ref[at] = middle
        center, scale = norm_stats(middle)
        hidden_ref[at] = (center * scale * norm_ref[2:3] + norm_ref[3:4]).astype(BF16)
        return 0

    lax.fori_loop(0, chunks, close, 0)
    push_middle(0).start()
    push_hidden(0).start()
    for step in fc_in + proj_in:
        step()
    fc.copy_own().wait()
    proj.copy_own().wait()
    chain.finish(groups)
    for gather in (attn, feat, fc, proj):
        gather.finish()
    for push in (push_normed, push_wo, push_maps, push_attn, push_middle, push_hidden):
        push(0).wait()
    for push in (push_qkv, push_fq, push_fk, push_state, push_mixed, push_rden):
        for g in range(groups):
            push(g).wait()


def feed_forward(
    sizes, hidden_ref, dy_ref, norm_ref, fc_in, proj_in, middle_in,
    block_out, dmid_out, datt_out, gfc_out, gproj_out, gnorm_ref,
    fc_ref, proj_ref, middle_ref, out_ref, datt_ref, gfc_ref, gproj_ref, branch_ref, dhid_ref, act_ref, dpre_ref,
    move_sem, fc_sem, proj_sem, *scratch,
):
    X, Z, H = sizes
    net = Network(sizes)
    part, width = fc_ref.shape[3:]
    rows = hidden_ref.shape[0]
    tile = 256
    tiles = rows // tile
    turns = X * Z

    def place(i):
        off = Z - 1 - lax.rem(i, Z)
        return lax.rem(net.dp + 1 + i // Z, X), net.behind(off), off

    def fetch(i):
        dp, b, _ = place(i)
        at = dp * Z + b
        return (
            pltpu.make_async_copy(fc_in.at[dp, b], fc_ref.at[dp, b], fc_sem.at[at]),
            pltpu.make_async_copy(proj_in.at[dp, b], proj_ref.at[dp, b], proj_sem.at[at]),
        )

    for i in range(turns):
        for copy in fetch(i):
            copy.start()
    mover = Mover(move_sem)
    pull_middle = mover.plan(middle_in, middle_ref)
    pull_middle(0).start()
    net.barrier()
    scatters = [Scatter(net, gfc_ref, *scratch[:3]), Scatter(net, gproj_ref, *scratch[3:])]
    branch_ref[...] = jnp.zeros_like(branch_ref)
    dhid_ref[...] = jnp.zeros_like(dhid_ref)

    slots = {}
    if (X, H) == (2, 4):
        own, first, second, both = scatters[0].early_sets()
        for k in range(Z):
            off = Z - 1 - k
            for scatter in scatters:
                slots.setdefault(k + 1, []).append(functools.partial(scatter.step, both, off))
                for late, chosen in ((1, second), (1, first), (2, own)):
                    slots.setdefault(Z + k + late, []).append(functools.partial(scatter.step, chosen, off))
    else:
        for scatter in scatters:
            for chosen in reversed(scatter.early_sets()):
                for off in reversed(range(Z)):
                    slots.setdefault(turns, []).append(functools.partial(scatter.step, chosen, off))

    def block(i, _):
        dp, b, off = place(i)
        for copy in fetch(i):
            copy.wait()

        def rowed(c, _):
            at = pl.ds(pl.multiple_of(c * tile, tile), tile)
            fc = fc_ref[dp, b].reshape(H * part, width)
            proj = proj_ref[dp, b].reshape(H * part, width)
            pre = dot_nt(hidden_ref[at], fc)
            square = pre * pre
            inner = jnp.tanh(0.7978845608 * pre * (1.0 + 0.044715 * square))
            half = 0.5 * (1.0 + inner)
            act = (pre * half).astype(BF16)
            slope = half + 0.5 * pre * (1.0 - inner * inner) * (0.7978845608 * (1.0 + 3 * 0.044715 * square))
            dpre = (dot_nt(dy_ref[at], proj) * slope).astype(BF16)
            act_ref[at] = act
            dpre_ref[at] = dpre
            branch_ref[at] += dot(act, proj)
            dhid_ref[at] += dot(dpre, fc)
            return 0

        lax.fori_loop(0, tiles, rowed, 0)
        run_at(slots, i, turns)
        gproj_ref[dp, b] = dot_tn(act_ref[...], dy_ref[...]).astype(BF16).reshape(H, part, width)
        gfc_ref[dp, b] = dot_tn(dpre_ref[...], hidden_ref[...]).astype(BF16).reshape(H, part, width)
        for scatter in scatters:
            scatter.begin(lambda dp_at, h_at: dp_at == dp, [off])
        return 0

    lax.fori_loop(0, turns, block, 0)

    gnorm_ref[...] = jnp.zeros_like(gnorm_ref)
    pull_middle(0).wait()
    late = [slots[k] for k in sorted(slots) if k >= turns]
    late_slots = dict(enumerate(late[: tiles - 1]))
    late_slots[tiles - 1] = [item for items in late[tiles - 1 :] for item in items]

    def close(c, _):
        run_at(late_slots, c, tiles)
        at = pl.ds(pl.multiple_of(c * tile, tile), tile)
        middle = middle_ref[at]
        out_ref[at] = (middle + branch_ref[at]).astype(BF16)
        back, gain, shift = norm_backward(middle, norm_ref[2:3].astype(BF16).astype(F32), dhid_ref[at])
        dmid = dy_ref[at].astype(F32) + back
        middle_ref[at] = dmid
        datt_ref[at] = dmid.astype(BF16)
        gnorm_ref[2:3] += gain
        gnorm_ref[3:4] += shift
        return 0

    lax.fori_loop(0, tiles, close, 0)
    pushes = [mover.plan(*pair) for pair in ((out_ref, block_out), (middle_ref, dmid_out), (datt_ref, datt_out))]
    for push in pushes:
        push(0).start()
    gfc_out[...] = scatters[0].result()
    gproj_out[...] = scatters[1].result()
    for push in pushes:
        push(0).wait()
    for scatter in scatters:
        scatter.finish()


def attention_backward(
    sizes, heads, depth, len_ref, norm_ref, gnorm_in, gfc_ref, gproj_ref, x_in, normed_in, qkv_in, fq_in, fk_in,
    state_in, mixed_in, rden_in, wo_in, maps_in, w_in, datt_in, dmid_in,
    dx_out, gattn_out, gfeat_out, sums_out,
    x_ref, normed_ref, qkv_ref, fq_ref, fk_ref, state_ref, mixed_ref, rden_ref, wo_ref, maps_ref, datt_ref, dmid_ref,
    w_ref, gw_ref, gnorm_ref, featsum_ref, featpart_ref,
    dne_ref, back_ref, total_ref, picked_ref, dqkv_ref, dnormed_ref, gsum_ref, cin, cout, chain_send, chain_recv,
    w_sem, move_sem, *scratch,
):
    X, Z, H = sizes
    groups = H
    net = Network(sizes)
    h = net.h
    rows, width = x_ref.shape
    chunks = rows // CHUNK
    part = w_ref.shape[3]
    seq = Rows(len_ref, rows, h)
    low = low_half((CHUNK, 128))

    mover = Mover(move_sem)
    pull_datt, pull_maps, pull_normed, pull_x, pull_dmid, push_dx = (
        mover.plan(*pair)
        for pair in (
            (datt_in, datt_ref), (maps_in, maps_ref), (normed_in, normed_ref), (x_in, x_ref), (dmid_in, dmid_ref),
            (dmid_ref, dx_out),
        )
    )
    ahead_pulls = [
        mover.plan(*pair, groups)
        for pair in ((wo_in, wo_ref), (rden_in, rden_ref), (mixed_in, mixed_ref), (fq_in, fq_ref))
    ]
    group_pulls = [
        mover.plan(*pair, groups) for pair in ((fk_in, fk_ref), (state_in, state_ref), (qkv_in, qkv_ref))
    ]

    def pull_weight(i):
        slot = lax.rem(i, 2)
        return pltpu.make_async_copy(w_in.at[:, :, backwards(i)], w_ref.at[slot], w_sem.at[slot])

    def backwards(i):
        return group_at(h, groups - 1 - i, groups)

    pull_datt(0).start()
    for g in range(groups):
        for pull in ahead_pulls:
            pull(g).start()
    pull_maps(0).start()
    for i in range(groups):
        for pull in group_pulls:
            pull(backwards(i)).start()
    pull_weight(0).start()
    pull_normed(0).start()
    pull_x(0).start()
    pull_dmid(0).start()
    net.barrier(chained=True)
    attn = Scatter(net, gw_ref, *scratch[:3])
    feat = Scatter(net, featpart_ref, *scratch[3:6])

    down = lax.broadcasted_iota(jnp.int32, (256, 256), 0) // HD
    across = lax.broadcasted_iota(jnp.int32, (256, 256), 1) // HD
    other_half = ((down // 2 == across // 2) & (down != across)).astype(BF16)
    first = seq.first()
    pull_datt(0).wait()

    def ahead(g, _):
        for j in range(heads):
            total_ref[j] = jnp.zeros_like(total_ref[j])
        for pull in ahead_pulls:
            pull(g).wait()

        def piece(i, _):
            c = chunks - 1 - i
            at = pl.ds(pl.multiple_of(c * CHUNK, CHUNK), CHUNK)
            second = seq.second_column(c)
            dm = dot(datt_ref[at], wo_ref[g]).astype(BF16).astype(F32)
            rden = rden_ref[g, at].astype(F32)
            sums = dot((dm * mixed_ref[g, at].astype(F32)).astype(BF16), other_half)
            dnum = dm * rden
            dden = sums * swap_halves(rden) * (-1.0 / HD)
            for j in range(heads):
                lanes = slice(128 * (j // 2), 128 * (j // 2) + 128)
                mine, other = dnum[:, lanes], dden[:, lanes]
                dne = (jnp.where(low, mine, other) if j % 2 == 0 else jnp.where(low, other, mine)).astype(BF16)
                dne_ref[g, j, at] = dne
                back_ref[g, j, c] = total_ref[j].astype(BF16)
                total_ref[j] += dot_tn(fq_ref[g, at, 128 * j : 128 * j + 128], by_sequence(dne, second))
            return 0

        lax.fori_loop(0, chunks, piece, 0)
        for j in range(heads):
            picked_ref[g, j] = total_ref[j, :, :128] * (1.0 - first) + total_ref[j, :, 128:] * first
        return 0

    lax.fori_loop(0, groups, ahead, 0)
    after = seq.after()
    chain = Chain(-1, groups, h, equal(after, first), picked_ref, cin, cout, chain_send, chain_recv)
    lowd = low_half((width, 128))
    shape = (X, Z, part, 128)

    def out_grads(g, _):
        chain.step(g)
        for third in range(3):
            beside = dot_tn(datt_ref[...], mixed_ref[g, :, 128 * (third // 2) : 128 * (third // 2) + 128])
            if third != 1:
                beside = swap_halves(beside)
            gw_ref[:, :, g, :, 256 * third + 128 : 256 * third + 256] = beside.astype(BF16).reshape(shape)
        return 0

    lax.fori_loop(0, groups, out_grads, 0)

    dnormed_ref[...] = jnp.zeros_like(dnormed_ref)
    pull_maps(0).wait()
    pull_normed(0).wait()

    def group(i, _):
        g = backwards(i)
        slot = lax.rem(i, 2)
        for pull in group_pulls:
            pull(g).wait()
        pull_weight(i).wait()

        @pl.when(i < groups - 1)
        def _():
            pull_weight(i + 1).start()

        gsum_ref[...] = jnp.zeros_like(gsum_ref)

        def piece(c, _):
            at = pl.ds(pl.multiple_of(c * CHUNK, CHUNK), CHUNK)
            second = seq.second_column(c)
            lower, upper = seq.masks(c)
            dus_q, dus_k, dvs = [], [], []
            for j in range(heads):
                lanes = slice(128 * j, 128 * j + 128)
                fq, fk, dne = fq_ref[g, at, lanes], fk_ref[g, at, lanes], dne_ref[g, j, at]
                carry = cin[g, j].astype(F32)
                later = jnp.concatenate([carry * (1.0 - after), carry * after], axis=1)
                back = (back_ref[g, j, c].astype(F32) + later).astype(BF16)
                state = state_ref[g, j, c]
                block = qkv_ref[g, at, 512 + 128 * (j // 2) : 640 + 128 * (j // 2)]
                values = with_ones(block, j, low)
                scores_t = jnp.where(upper, dot_nt(fk, fq), 0.0).astype(BF16)
                weigh = jnp.where(lower, dot_nt(dne, values), 0.0).astype(BF16)
                weigh_t = jnp.where(upper, dot_nt(values, dne), 0.0).astype(BF16)
                dfq = dot(weigh, fk) + dot_nt(by_sequence(dne, second), state)
                dfk = dot(weigh_t, fq) + dot_nt(by_sequence(values, second), back)
                inter = dot(fk, back)
                dvs.append(dot(scores_t, dne) + jnp.where(second, inter[:, 128:], inter[:, :128]))
                dus_q.append(feature_back(fq.astype(F32), dfq.astype(BF16).astype(F32)).astype(BF16))
                dus_k.append(feature_back(fk.astype(F32), dfk.astype(BF16).astype(F32)).astype(BF16))
            du_q, du_k = jnp.concatenate(dus_q, axis=1), jnp.concatenate(dus_k, axis=1)
            dq = dot_nt(du_q, maps_ref[0, g]).astype(BF16)
            dk = dot_nt(du_k, maps_ref[1, g]).astype(BF16)
            dv = jnp.concatenate([jnp.where(low, dvs[0], dvs[1]), jnp.where(low, dvs[2], 0.0)], axis=1).astype(BF16)
            gsum_ref[0] += dot_tn(qkv_ref[g, at, 0:256], du_q)
            gsum_ref[1] += dot_tn(qkv_ref[g, at, 256:512], du_k)
            dqkv = jnp.concatenate([dq, dk, dv], axis=1)
            dqkv_ref[at] = dqkv
            dnormed_ref[at] += dot_nt(dqkv, w_ref[slot].reshape(width, width))
            return 0

        lax.fori_loop(0, chunks, piece, 0)
        low64 = low_half((HD, 128))
        for j in range(heads):
            sums = [gsum_ref[side, HD * j : HD * j + HD, 128 * j : 128 * j + 128] for side in range(2)]
            sums = [value - pltpu.roll(value, HD, 1) for value in sums]
            pair = jnp.where(low64, sums[0], -sums[1])
            for k in range(X * Z):
                featsum_ref[k // Z, k % Z, g, depth * j : depth * j + depth] = pair[depth * k : depth * k + depth]
        for third in range(3):
            grad = dot_tn(normed_ref[...], dqkv_ref[:, 256 * third : 256 * third + 256])
            at = 256 * third
            gw_ref[:, :, g, :, at : at + 128] = grad[:, 0:128].astype(BF16).reshape(shape)
            beside = gw_ref[:, :, g, :, at + 128 : at + 256].reshape(width, 128)
            gw_ref[:, :, g, :, at + 128 : at + 256] = (
                jnp.where(lowd, grad[:, 128:256], beside.astype(F32)).astype(BF16).reshape(shape)
            )
        attn.begin(lambda dp_at, h_at: h_at == g)

        if (X, H) == (2, 4):

            @pl.when(i == groups - 1)
            def _():
                for off in reversed(range(Z)):
                    attn.step(attn.early_sets()[3], off)

        return 0

    featsum_ref[...] = jnp.zeros_like(featsum_ref)
    lax.fori_loop(0, groups, group, 0)
    for k in range(X * Z):
        for g in range(groups):
            featpart_ref[k // Z, k % Z, g] = featsum_ref[k // Z, k % Z, g].astype(BF16)
    feat.begin()

    gnorm_ref[...] = gnorm_in[...]
    pull_x(0).wait()
    pull_dmid(0).wait()
    slots = {}
    for scatter in (attn, feat):
        early = list(reversed(scatter.early_sets()))
        if scatter is attn and (X, H) == (2, 4):
            early = early[1:]
        for k, chosen in enumerate(early):
            for off in reversed(range(Z)):
                slots.setdefault(min(k, chunks - 1), []).append(functools.partial(scatter.step, chosen, off))

    def close(c, _):
        run_at(slots, c, chunks)
        at = pl.ds(pl.multiple_of(c * CHUNK, CHUNK), CHUNK)
        gain_row = norm_ref[0:1].astype(BF16).astype(F32)
        back, gain, shift = norm_backward(x_ref[at].astype(F32), gain_row, dnormed_ref[at])
        dmid_ref[at] = dmid_ref[at] + back
        gnorm_ref[0:1] += gain
        gnorm_ref[1:2] += shift
        return 0

    lax.fori_loop(0, chunks, close, 0)
    push_dx(0).start()
    square = jnp.zeros((1, 128), F32)
    gattn_out[...] = attn.result()
    gfeat_out[...] = feat.result()
    for ref in (gattn_out, gfeat_out, gfc_ref, gproj_ref):
        column = jnp.sum(ref[...] * ref[...], axis=0, keepdims=True)
        for at in range(0, column.shape[1], 128):
            square = square + column[:, at : at + 128]
    gnorm_ref[4:5, 0:128] = square
    sums_out[...] = total_over_all(net, gnorm_ref[...], *scratch[6:])
    push_dx(0).wait()
    chain.finish(groups)
    for scatter in (attn, feat):
        scatter.finish()


def adamw_update(master, first_mom, second_mom, grad_in, factor, step_rate, decay_rate):
    clipped = grad_in * factor
    first_new = beta_one * first_mom + (1.0 - beta_one) * clipped
    second_new = beta_two * second_mom + (1.0 - beta_two) * clipped * clipped
    direction = (
        first_new
        / (1.0 - beta_one**STEP)
        / (jnp.sqrt(second_new / (1.0 - beta_two**STEP)) + adam_eps)
    )
    master_new = master - step_rate * (direction + decay_rate * master)
    return (master_new, first_new, second_new)


def update_kernel(heads, depth, sums_ref, gattn_ref, gfeat_ref, gfc_ref, gproj_ref, *refs):
    masters, firsts, seconds = refs[0:6], refs[6:12], refs[12:18]
    block_in, dx_in, norm_out = refs[18:21]
    outs, (block_out, dx_out), (feat_grads, block_ref, dx_ref, sems) = refs[21:46], refs[46:48], refs[48:]
    mover = Mover(sems)
    pulls = [mover.plan(block_in, block_ref)(0), mover.plan(dx_in, dx_ref)(0)]
    pushes = [mover.plan(block_ref, block_out)(0), mover.plan(dx_ref, dx_out)(0)]
    for pull in pulls:
        pull.start()
    norm_grads = sums_ref[0:4]
    squares = jnp.sum(sums_ref[4:5, 0:128], keepdims=True) + jnp.sum(norm_grads * norm_grads, keepdims=True)
    grad_norm = jnp.sqrt(squares)
    norm_out[...] = jnp.broadcast_to(grad_norm, norm_out.shape)
    factor = clip_limit / jnp.maximum(grad_norm, clip_limit)
    rates, decays = (0.02, 0.4, 0.15, 0.02, 0.01, 0.3), (0.1, 0.1, 0.1, 0.1, 0.1, 0.0)

    def update(which, at, grads):
        results = adamw_update(
            masters[which][at], firsts[which][at], seconds[which][at], grads, factor, rates[which], decays[which]
        )
        results += (results[0].astype(BF16),)
        if which < 5:
            for kind, value in enumerate(results):
                outs[6 * kind + which][at] = value
        else:
            outs[5][...], outs[11][...] = results[0], results[1]
            outs[17][...], outs[23][...] = results[2][0:2], results[2][2:4]
            outs[24][...] = results[3]

    low = low_half((1, 128))
    for j in range(heads):
        for d in range(0, depth, 2):
            row, other = (gfeat_ref[depth * j + d + k : depth * j + d + k + 1] for k in range(2))
            at = slice(64 * d, 64 * d + 128)
            feat_grads[j, 0:1, at] = jnp.where(low, row, pltpu.roll(other, HD, 1))
            feat_grads[j, 1:2, at] = jnp.where(low, pltpu.roll(row, HD, 1), other)
    for j in range(3):
        update(0, (j,), gattn_ref[:, 256 * j : 256 * j + heads * HD])
        update(1, (slice(HD * j, HD * j + HD),), gattn_ref[:, 256 * j + heads * HD : 256 * j + 256].T)
    update(2, (slice(None),), feat_grads[...])
    update(3, (slice(None),), gfc_ref[...])
    for pull, push in zip(pulls, pushes):
        pull.wait()
        push.start()
    update(4, (slice(None),), gproj_ref[...])
    update(5, (slice(None),), norm_grads)
    for push in pushes:
        push.wait()


def in_vmem(count):
    return [pl.BlockSpec(memory_space=VMEM)] * count


def struct(shape, dtype):
    return jax.ShapeDtypeStruct(shape, dtype)


def call(kernel, outs, smem, operands, scratch, collective_id, name, flops, hbm_in=0, hbm_out=(), limit=63):
    specs = [pl.BlockSpec(memory_space=pltpu.SMEM)] * smem + in_vmem(len(operands) - smem - hbm_in)
    specs += [pl.BlockSpec(memory_space=pl.ANY)] * hbm_in
    out_specs = [pl.BlockSpec(memory_space=pl.ANY if i in hbm_out else VMEM) for i in range(len(outs))]
    traffic = sum(o.size * o.dtype.itemsize for o in outs) + sum(o.size * o.dtype.itemsize for o in operands)
    extra = {} if collective_id is None else {"collective_id": collective_id, "has_side_effects": True}
    return pl.pallas_call(
        kernel,
        out_shape=tuple(outs),
        in_specs=specs,
        out_specs=tuple(out_specs),
        scratch_shapes=scratch,
        compiler_params=pltpu.CompilerParams(vmem_limit_bytes=limit * 2**20, **extra),
        cost_estimate=pl.CostEstimate(flops=flops, bytes_accessed=traffic, transcendentals=0),
        name=name,
    )(*operands)


def on_device(
    sizes,
    block_in,
    cotangent,
    seq_len,
    w_qkv,
    w_out,
    w_feat,
    w_fc,
    w_proj,
    norm_params,
    first_qkv,
    second_qkv,
    first_out,
    second_out,
    first_feat,
    second_feat,
    first_fc,
    second_fc,
    first_proj,
    second_proj,
    first_norms,
    second_norms,
):
    X, Z, H = sizes
    rows, width = block_in.shape
    part, _, head_width = w_qkv.shape
    heads = w_feat.shape[1]
    depth = w_feat.shape[2] // HD
    chunks = rows // CHUNK

    big = (X, Z, H, part, width)
    small = (X, Z, H, FEAT_ROWS, 2 * HD)
    dma = pltpu.SemaphoreType.DMA
    chain_scratch = [
        VMEM((H, heads, 128, 128), F32),
        VMEM((H, heads, 128, 128), BF16),
        VMEM((H, heads, 128, 128), BF16),
        dma((H,)),
        dma((H,)),
    ]
    held = [
        struct((rows, width), BF16),
        struct((H, rows, width), BF16),
        struct((H, rows, 128 * heads), BF16),
        struct((H, rows, 128 * heads), BF16),
        struct((H, heads, chunks, 128, 256), BF16),
        struct((H, rows, 256), BF16),
        struct((H, rows, 256), BF16),
        struct((H, width, 256), BF16),
        struct((2, H, 256, 128 * heads), BF16),
        struct((rows, width), F32),
        struct((rows, width), BF16),
    ]
    normed, qkv, fq, fk, states, mixed, rden, wo, maps, middle, hidden, attn_w, fc_w, proj_w = call(
        functools.partial(attention_forward, sizes, heads, depth),
        held + [struct(big, BF16)] * 3,
        1,
        [seq_len, block_in, w_qkv.transpose(1, 0, 2), w_out, w_feat.transpose(1, 0, 2), w_fc.T, w_proj, norm_params],
        [VMEM(item.shape, item.dtype) for item in held]
        + [
            VMEM((part, width), BF16),
            VMEM((FEAT_ROWS, 128), BF16),
            VMEM((part, width), BF16),
            VMEM((part, width), BF16),
            VMEM((FEAT_ROWS, 128), F32),
            VMEM((4, width), F32),
        ]
        + [VMEM(big, BF16), VMEM(small, BF16), VMEM((H * heads, HD, 128), F32), VMEM((heads, 128, 256), F32)]
        + chain_scratch
        + [dma((6 + 6 * H,))]
        + [sem for _ in range(4) for sem in gather_sems(sizes)],
        0,
        "attention_forward",
        10**10,
        hbm_out=range(14),
    )

    block_out, d_middle, d_att, g_fc, g_proj, g_norm = call(
        functools.partial(feed_forward, sizes),
        [
            struct((rows, width), BF16),
            struct((rows, width), F32),
            struct((rows, width), BF16),
            struct((part, width), F32),
            struct((part, width), F32),
            struct((8, width), F32),
        ],
        0,
        [hidden, cotangent, norm_params, fc_w, proj_w, middle],
        [
            VMEM(big, BF16),
            VMEM(big, BF16),
            VMEM((rows, width), F32),
            VMEM((rows, width), BF16),
            VMEM((rows, width), BF16),
            VMEM(big, BF16),
            VMEM(big, BF16),
            VMEM((rows, width), F32),
            VMEM((rows, width), F32),
            VMEM((rows, H * part), BF16),
            VMEM((rows, H * part), BF16),
            dma((4,)),
            dma((X * Z,)),
            dma((X * Z,)),
        ]
        + scatter_scratch(sizes, (part, width)) * 2,
        1,
        "feed_forward",
        3 * 10**10,
        hbm_in=3,
        hbm_out=range(3),
    )

    pulled = [struct((rows, width), BF16)] + held[:9] + [struct((rows, width), BF16), struct((rows, width), F32)]
    block_in_grad, g_attn, g_feat, sums = call(
        functools.partial(attention_backward, sizes, heads, depth),
        [
            struct((rows, width), F32),
            struct((part, width), F32),
            struct((FEAT_ROWS, 128), F32),
            struct((8, width), F32),
        ],
        1,
        [
            seq_len, norm_params, g_norm, g_fc, g_proj, block_in, normed, qkv, fq, fk, states, mixed, rden, wo, maps,
            attn_w, d_att, d_middle,
        ],
        [VMEM(item.shape, item.dtype) for item in pulled]
        + [
            VMEM((2, X, Z, part, width), BF16),
            VMEM(big, BF16),
            VMEM((8, width), F32),
            VMEM(small, F32),
            VMEM(small, BF16),
            VMEM((H, heads, rows, 128), BF16),
            VMEM((H, heads, chunks, 128, 256), BF16),
            VMEM((heads, 128, 256), F32),
            chain_scratch[0],
            VMEM((rows, width), BF16),
            VMEM((rows, width), F32),
            VMEM((2, 256, 128 * heads), F32),
        ]
        + chain_scratch[1:]
        + [dma((2,)), dma((6 + 7 * H,))]
        + scatter_scratch(sizes, (part, width))
        + scatter_scratch(sizes, (FEAT_ROWS, 128))
        + total_scratch(sizes, (8, width)),
        2,
        "attention_backward",
        2 * 10**10,
        hbm_in=13,
        hbm_out=(0,),
    )

    def turned(qkv, out, feat, fc, proj, *norms):
        return [qkv.transpose(1, 0, 2), out, feat.transpose(1, 0, 2), fc.T, proj, *norms]

    masters = turned(w_qkv, w_out, w_feat, w_fc, w_proj, norm_params)
    firsts = turned(first_qkv, first_out, first_feat, first_fc, first_proj, first_norms)
    seconds = turned(second_qkv, second_out, second_feat, second_fc, second_proj, second_norms)
    shapes = [item.shape for item in masters]
    halves = (2, width)
    norm_filled, *updated, block_out, block_in_grad = call(
        functools.partial(update_kernel, heads, depth),
        [struct((8, 128), F32)]
        + [struct(shape, F32) for shape in shapes * 2 + shapes[:5] + [halves]]
        + [struct(shape, BF16) for shape in shapes[:5]]
        + [struct(halves, F32), struct(shapes[5], BF16)]
        + [struct((rows, width), BF16), struct((rows, width), F32)],
        0,
        [sums, g_attn, g_feat, g_fc, g_proj] + masters + firsts + seconds + [block_out, block_in_grad],
        [VMEM(shapes[2], F32), VMEM((rows, width), BF16), VMEM((rows, width), F32), dma((4,))],
        None,
        "update",
        10**7,
        hbm_in=2,
        hbm_out=(26, 27),
    )
    new, new_first, new_second = (turned(*updated[6 * kind : 6 * kind + 6]) for kind in range(3))
    copies = turned(*updated[18:23], updated[24])
    return (
        norm_filled[0, 0],
        block_out,
        block_in_grad,
        *new,
        *new_first,
        *new_second[:5],
        new_second[5],
        updated[23],
        *copies,
    )


def solution(mesh):
    everything = ("dp", "batch", "head")
    rows = P(everything, None)
    qkv, out, feat = P(("dp", "batch"), None, "head"), P("head", ("dp", "batch")), P(None, "head", ("dp", "batch"))
    fc, proj, whole = P(None, everything), P(everything, None), P()
    weights = (qkv, out, feat, fc, proj, whole)
    in_specs = (rows, rows, P(("dp", "batch"), None)) + weights
    for spec in weights:
        in_specs += (spec, spec)
    out_specs = (whole, rows, rows) + weights + weights + weights[:5] + (whole, whole) + weights
    sizes = (mesh.shape["dp"], mesh.shape["batch"], mesh.shape["head"])
    return jax.shard_map(
        functools.partial(on_device, sizes), mesh=mesh, in_specs=in_specs, out_specs=out_specs, check_vma=False
    )
```

time: 446 us -> 304 us (0.68)
  Pallas kernels: 397 us -> 301 us
  other arithmetic: 22.2 us -> 0 us
  local copies, waits for them, and re-layouts: 21.9 us -> 1.19 us
    pallas_call x5 -> x4, Pallas kernels: 397 us -> 301 us  [call(): pl.pallas_call(kernel, out_shape=tuple(outs), in_specs=specs, out_specs=t...]
    convert_element_type x11 -> x0, other arithmetic: 16.8 us -> none  [the longest x1 2.28 us: on_device(): up_fc[0].astype(BF16)]
    unnamed x22 -> x0, local copies, waits for them, and re-layouts: 12.3 us -> none
where the time goes in v2:
time: 304 us; the launch traced here: 303 us
  Pallas kernels  301 us (99%)
    pallas_call x4, Pallas kernels, call(): pl.pallas_call(kernel, out_shape=tuple(outs), in_specs=specs, out_specs=t...  301 us

profile of v2, /device:TPU:0, one launch (start us, length us, event | category | flops | bytes accessed | tf_op | source)
XLA Modules:
  0.0 303.3 jit_solution(5045255481052313754)
XLA Ops:
  0.7 108.0 %attention_forward.1 = (bf16[1024,768]{1,0:T(8,128)(2,1)}, bf16[4,1024,768]{2,1,0:T(8,128)(2,1)}, bf16[4,1024,384]{2,1,0:T(8,128)(2,1)}, bf16[4,1024,384]{2,1,0:...) custom-call(s32[1,2]{1,0:T(1,128)} %len_ref.3, ...), custom_call_target="tpu_custom_call" | custom-call | flops 10000000000 | bytes 45998088 | tf_op jit(solution)/shard_map/attention_forward/pallas_call | solution.py:1119
  108.7 80.5 %feed_forward.1 = (bf16[1024,768]{1,0:T(8,128)(2,1)}, f32[1024,768]{1,0:T(8,128)}, bf16[1024,768]{1,0:T(8,128)(2,1)}, f32[96,768]{1,0:T(8,128)}, f32[96,768]{1,0:T(8,128)}, /*index=5*/f32[8,768]{1,0:T(8,128)}) custom-call(bf16[1024,768]{1,0:T(8,128)(2,1)} %get-tuple-element.80.hidden_ref, bf16[1024,768]{1,0:T(8,128)(2,1)} %dy_ref.1, f32[4,768]{1,0:T(4,128)} %refs_5_.1, ...), custom_call_target="tpu_custom_call" | custom-call | flops 30000001024 | bytes 22646784 | tf_op jit(solution)/shard_map/feed_forward/pallas_call | solution.py:1119
  189.2 104.8 %attention_backward.1 = (f32[1024,768]{1,0:T(8,128)}, f32[96,768]{1,0:T(8,128)}, f32[32,128]{1,0:T(8,128)}, f32[8,768]{1,0:T(8,128)}) custom-call(s32[1,2]{1,0:T(1,128)} %len_ref.3, f32[4,768]{1,0:T(4,128)} %refs_5_.1, f32[8,768]{1,0:T(8,128)} %get-tuple-element.84.gnorm_in, f32[96,768]{1,0:T(8,128)} %get-tuple-element.85.gfc_ref, ...), custom_call_target="tpu_custom_call" | custom-call | flops 20000000000 | bytes 39759880 | tf_op jit(solution)/shard_map/attention_backward/pallas_call | solution.py:1119
  294.0 8.1 %update.1 = (f32[8,128]{1,0:T(8,128)}, f32[3,96,192]{2,1,0:T(8,128)}, f32[192,96]{1,0:T(8,128)}, f32[3,2,512]{2,1,0:T(2,128)}, f32[96,768]{1,0:T(8,128)}, /*inde...) custom-call(f32[8,768]{1,0:T(8,128)} %get-tuple-element.99.sums_ref,, ...), custom_call_target="tpu_custom_call" | custom-call | flops 10000000 | bytes 16277504 | tf_op jit(solution)/shard_map/update/pallas_call | solution.py:1119
  302.1 1.2 slice.3

commit v3 on v2

--- a/solution.py
+++ b/solution.py
@@ -11,6 +11,9 @@
 STEP = 8
 CHUNK = 256
 FEAT_ROWS = 32
+FC_TURNS = (0, 4, 8, 12, 16)
+PROJ_BEGIN = 0
+PROJ_TURNS = (2, 6, 10, 14, 18)
 MESH = pl.DeviceIdType.MESH
 VMEM = pltpu.VMEM
 F32 = jnp.float32
@@ -89,90 +92,128 @@
     def stages(self, chosen):
         return range(max(chosen) + 1 if chosen else 0, len(self.flips))
 
-    def barrier(self, chained=False):
+    def plane(self):
+        count = self.X * self.H
+        mine = self.dp * self.H + self.h
+        for step in range(1, count):
+            other = lax.rem(mine + step, count)
+            yield step, {"dp": other // self.H, "batch": self.b, "head": lax.rem(other, self.H)}
+
+    def barrier(self, chained=False, whole_plane=False):
+        pl.semaphore_wait(pltpu.get_barrier_semaphore(), self.greet(chained, whole_plane))
+
+    def greet(self, chained=False, whole_plane=False):
         sem = pltpu.get_barrier_semaphore()
         devices = [self.along(self.ahead(off)) for off in range(1, self.Z)]
-        devices += [self.partner(k) for k in range(len(self.flips))]
-        if chained:
-            devices += [{"head": lax.rem(self.h + step, self.H)} for step in (1, self.H - 1)]
+        if whole_plane:
+            devices += [device for _, device in self.plane()]
+        else:
+            devices += [self.partner(k) for k in range(len(self.flips))]
+            if chained:
+                devices += [{"head": lax.rem(self.h + step, self.H)} for step in (1, self.H - 1)]
         for device in devices:
             pl.semaphore_signal(sem, inc=1, device_id=device, device_id_type=MESH)
-        pl.semaphore_wait(sem, len(devices))
+        return len(devices)
 
 
 def gather_sems(sizes):
     X, Z, H = sizes
-    n = X * H - 1
-    return [pltpu.SemaphoreType.DMA((n + 1, Z)), pltpu.SemaphoreType.DMA((n + 1, Z))]
+    return [pltpu.SemaphoreType.DMA((X * H + 1, Z)), pltpu.SemaphoreType.DMA((X * H, Z))]
 
 
 class Gather:
-    def __init__(self, net, shard, buf, send, recv):
-        self.net, self.shard, self.buf, self.send, self.recv = net, shard, buf, send, recv
-
-    def source(self, chosen, off):
-        return self.shard if chosen == () and off == 0 else self.buf.at[self.net.slot(chosen, off)]
-
-    def copy(self, chosen, off, k):
+    def __init__(self, net, shard, buf, send, recv, rows=None):
+        self.net, self.send, self.recv = net, send, recv
+        self.rows = pl.ds(0, shard.shape[0]) if rows is None else rows
+        self.shard, self.buf = shard.at[self.rows], buf
+        self.inner = (net.b == 1) | (net.b == 2)
+        self.ends = send.shape[0] - 1
+
+    def near(self, t):
+        b = self.net.b
+        return (b, flip_bit(b, 0), 2 - b // 2, 3 - 3 * (b // 2))[t]
+
+    def slot(self, chosen, t):
+        dp, h = self.net.coord(chosen)
+        return dp, self.near(t), h, self.rows
+
+    def source(self, chosen, t):
+        return self.shard if chosen == () and t == 0 else self.buf.at[self.slot(chosen, t)]
+
+    def copy(self, chosen, t, k):
         net = self.net
         into = net.index[chosen + (k,)]
         return pltpu.make_async_remote_copy(
-            src_ref=self.source(chosen, off), dst_ref=self.buf.at[net.slot(chosen, off)],
-            send_sem=self.send.at[into, off], recv_sem=self.recv.at[into, off],
+            src_ref=self.source(chosen, t), dst_ref=self.buf.at[self.slot(chosen, t)],
+            send_sem=self.send.at[into, t], recv_sem=self.recv.at[into, t],
             device_id=net.partner(k), device_id_type=MESH,
         )
 
-    def copy_along(self, off):
+    def hop(self, t, outward, arrives, send_sem):
         net = self.net
         return pltpu.make_async_remote_copy(
-            src_ref=self.shard, dst_ref=self.buf.at[net.slot((), 0)],
-            send_sem=self.send.at[0, off], recv_sem=self.recv.at[0, off],
-            device_id=net.along(net.ahead(off)), device_id_type=MESH,
+            src_ref=self.source((), t), dst_ref=self.buf.at[self.slot((), t)],
+            send_sem=send_sem, recv_sem=self.recv.at[0, arrives],
+            device_id=net.along(flip_bit(net.b, 0) if outward else 3 - net.b), device_id_type=MESH,
         )
 
+    def pair_hop(self):
+        return self.hop(0, True, 1, self.send.at[self.ends, 0])
+
+    def inner_hops(self, t):
+        ends = self.send.at[self.ends, 1]
+        return self.hop(t, t > 1, (2, 3, 2, 3)[t], self.send.at[0, t] if t else ends)
+
     def copy_own(self):
-        return pltpu.make_async_copy(self.shard, self.buf.at[self.net.slot((), 0)], self.send.at[0, 0])
-
-    def arrived(self, chosen, off):
+        return pltpu.make_async_copy(self.shard, self.buf.at[self.slot((), 0)], self.send.at[self.ends, 2])
+
+    def arrived(self, chosen, t):
         net = self.net
-        place = self.buf.at[net.slot(chosen, off)]
+        place = self.buf.at[self.slot(chosen, t)]
         into = net.index[chosen]
         pltpu.make_async_remote_copy(
-            src_ref=place, dst_ref=place, send_sem=self.send.at[into, off], recv_sem=self.recv.at[into, off],
+            src_ref=place, dst_ref=place, send_sem=self.send.at[into, t], recv_sem=self.recv.at[into, t],
             device_id=net.partner(0), device_id_type=MESH,
         ).wait_recv()
 
     def begin(self):
-        net = self.net
-        for k in net.stages(()):
+        self.pair_hop().start()
+        pl.when(self.inner)(lambda: self.inner_hops(0).start())
+        for k in self.net.stages(()):
             self.copy((), 0, k).start()
-        for off in range(1, net.Z):
-            self.copy_along(off).start()
         self.copy_own().start()
 
-    def step(self, chosen, off):
-        self.arrived(chosen, off)
+    def step(self, chosen, t):
+        self.arrived(chosen, t)
+        if chosen == ():
+            pl.when(self.inner)(lambda: self.inner_hops(t).start())
         for k in self.net.stages(chosen):
-            self.copy(chosen, off, k).start()
+            self.copy(chosen, t, k).start()
 
     def steps(self):
         net = self.net
-        order = [((), off) for off in range(1, net.Z)]
-        for chosen in net.sets[1:]:
-            order += [(chosen, off) for off in range(net.Z)]
-        half = len(net.sets) // 2 * net.Z - 1
-        return [functools.partial(self.step, *item) for item in order[:half]], [
-            functools.partial(self.step, *item) for item in order[half:]
-        ]
+        early = net.sets[: len(net.sets) // 2]
+        rounds = [[] for _ in range(net.Z + max(len(chosen) for chosen in early))]
+        for t in range(net.Z):
+            for chosen in early:
+                if chosen or t:
+                    rounds[t + len(chosen)].append(functools.partial(self.step, chosen, t))
+        late = [functools.partial(self.step, chosen, t) for chosen in net.sets[len(early) :] for t in range(net.Z)]
+        return rounds[1:], late
 
     def finish(self):
         net = self.net
-        for off in range(1, net.Z):
-            self.copy_along(off).wait_send()
+        self.pair_hop().wait_send()
+
+        @pl.when(self.inner)
+        def _():
+            for t in range(net.Z):
+                self.inner_hops(t).wait_send()
+
         for chosen in net.sets:
             for k in net.stages(chosen):
-                for off in range(net.Z):
-                    self.copy(chosen, off, k).wait_send()
+                for t in range(net.Z):
+                    self.copy(chosen, t, k).wait_send()
 
 
 def scatter_scratch(sizes, shape):
@@ -182,8 +223,8 @@
 
 
 class Scatter:
-    def __init__(self, net, part, inbox, send, recv):
-        self.net, self.part, self.inbox, self.send, self.recv = net, part, inbox, send, recv
+    def __init__(self, net, along, part, inbox, send, recv):
+        self.net, self.along, self.part, self.inbox, self.send, self.recv = net, along, part, inbox, send, recv
         self.last = len(net.flips) - 1
 
     def sum_at(self, chosen, off):
@@ -199,13 +240,6 @@
             recv_sem=self.recv.at[into, off], device_id=net.partner(k), device_id_type=MESH,
         )
 
-    def copy_along(self, off):
-        net = self.net
-        return pltpu.make_async_remote_copy(
-            src_ref=self.sum_at((), off), dst_ref=self.inbox.at[0, off], send_sem=self.send.at[0, off],
-            recv_sem=self.recv.at[0, off], device_id=net.along(net.behind(off)), device_id_type=MESH,
-        )
-
     def early_sets(self):
         return self.net.sets[: len(self.net.sets) // 2]
 
@@ -227,74 +261,97 @@
         for k in reversed(net.stages(chosen)):
             self.copy(chosen, off, k).wait_recv()
             total = total + self.inbox[net.index[chosen + (k,)], off].astype(F32)
-        self.sum_at(chosen, off)[...] = total.astype(BF16)
         if chosen:
+            self.sum_at(chosen, off)[...] = total.astype(BF16)
             self.copy(chosen[:-1], off, chosen[-1]).start()
-        elif off:
-            self.copy_along(off).start()
-
-    def result(self):
-        net = self.net
-        total = self.sum_at((), 0)[...].astype(F32)
-        for off in range(1, net.Z):
-            self.copy_along(off).wait_recv()
-            total = total + self.inbox[0, off].astype(F32)
-        return total
+        else:
+            self.along.give(off, total.astype(BF16))
 
     def finish(self):
         net = self.net
-        for off in range(1, net.Z):
-            self.copy_along(off).wait_send()
         for chosen in net.sets:
             for k in net.stages(chosen):
                 for off in range(net.Z):
                     self.copy(chosen, off, k).wait_send()
 
 
+def along_scratch(sizes, shape):
+    X, Z, H = sizes
+    return [VMEM((Z,) + shape, BF16), pltpu.SemaphoreType.DMA((Z,)), pltpu.SemaphoreType.DMA((Z,))]
+
+
+class Along:
+    def __init__(self, net, sums, inbox, send, recv):
+        self.net, self.sums, self.inbox, self.send, self.recv = net, sums, inbox, send, recv
+
+    def copy(self, off):
+        net = self.net
+        return pltpu.make_async_remote_copy(
+            src_ref=self.sums.at[off], dst_ref=self.inbox.at[off], send_sem=self.send.at[off],
+            recv_sem=self.recv.at[off], device_id=net.along(net.behind(off)), device_id_type=MESH,
+        )
+
+    def give(self, off, value):
+        self.sums[off] = value
+        if off:
+            self.copy(off).start()
+
+    def result(self):
+        total = self.sums[0].astype(F32)
+        for off in range(1, self.net.Z):
+            self.copy(off).wait_recv()
+            total = total + self.inbox[off].astype(F32)
+        return total
+
+    def finish(self):
+        for off in range(1, self.net.Z):
+            self.copy(off).wait_send()
+
+
+class Keep:
+    def __init__(self, sums):
+        self.sums = sums
+
+    def give(self, off, value):
+        self.sums[off] = value
+
+
 def total_scratch(sizes, shape):
     X, Z, H = sizes
-    bits = (X * H).bit_length() - 1
+    count = X * H
     return [
-        VMEM((Z + 2 * bits,) + shape, F32),
-        pltpu.SemaphoreType.DMA((Z + bits,)),
-        pltpu.SemaphoreType.DMA((Z + bits,)),
+        VMEM((count + Z,) + shape, F32),
+        pltpu.SemaphoreType.DMA((count + Z,)),
+        pltpu.SemaphoreType.DMA((count + Z,)),
     ]
 
 
 def total_over_all(net, value, slots, send, recv):
-    Z = net.Z
-    slots[net.b] = value
-    copies = []
-    for off in range(1, Z):
-        copies.append(
+    count, Z = net.X * net.H, net.Z
+
+    def exchange(value, base, mine, size, devices):
+        slots[base + mine] = value
+        for step, device in devices:
+            place = slots.at[base + mine]
             pltpu.make_async_remote_copy(
-                src_ref=slots.at[net.b], dst_ref=slots.at[net.b], send_sem=send.at[off], recv_sem=recv.at[off],
-                device_id=net.along(net.ahead(off)), device_id_type=MESH,
+                src_ref=place, dst_ref=place, send_sem=send.at[base + step], recv_sem=recv.at[base + step],
+                device_id=device, device_id_type=MESH,
+            ).start()
+        for step, device in devices:
+            place = slots.at[base + lax.rem(mine + size - step, size)]
+            copy = pltpu.make_async_remote_copy(
+                src_ref=place, dst_ref=place, send_sem=send.at[base + step], recv_sem=recv.at[base + step],
+                device_id=device, device_id_type=MESH,
             )
-        )
-    for copy in copies:
-        copy.start()
-    for off in range(1, Z):
-        place = slots.at[net.behind(off)]
-        pltpu.make_async_remote_copy(
-            src_ref=place, dst_ref=place, send_sem=send.at[off], recv_sem=recv.at[off],
-            device_id=net.along(net.ahead(off)), device_id_type=MESH,
-        ).wait_recv()
-    for copy in copies:
-        copy.wait_send()
-    value = slots[0]
-    for off in range(1, Z):
-        value = value + slots[off]
-    for k in range(len(net.flips)):
-        slots[Z + 2 * k] = value
-        copy = pltpu.make_async_remote_copy(
-            src_ref=slots.at[Z + 2 * k], dst_ref=slots.at[Z + 2 * k + 1], send_sem=send.at[Z + k],
-            recv_sem=recv.at[Z + k], device_id=net.partner(k), device_id_type=MESH,
-        )
-        copy.start()
-        copy.wait()
-        value = value + slots[Z + 2 * k + 1]
-    return value
+            copy.wait_recv()
+            copy.wait_send()
+        total = slots[base]
+        for i in range(1, size):
+            total = total + slots[base + i]
+        return total
+
+    value = exchange(value, 0, net.dp * net.H + net.h, count, list(net.plane()))
+    return exchange(value, count, net.b, Z, [(off, net.along(net.ahead(off))) for off in range(1, Z)])
 
 
 class Mover:
@@ -339,22 +396,24 @@
     return parts[0] if len(parts) == 1 else jnp.concatenate(parts, axis=1)
 
 
+def half_ones():
+    down = lax.broadcasted_iota(jnp.int32, (128, 128), 0) // HD
+    across = lax.broadcasted_iota(jnp.int32, (128, 128), 1) // HD
+    return (down == across).astype(BF16)
+
+
 def feature_pair(scaled, live):
     low = low_half(scaled.shape)
     top = jnp.max(jnp.where(low, scaled, -jnp.inf), axis=-1, keepdims=True)
     bottom = jnp.max(jnp.where(low, -jnp.inf, scaled), axis=-1, keepdims=True)
     powers = jnp.exp(scaled - jnp.where(low, top, bottom))
-    first = jnp.sum(jnp.where(low, powers, 0.0), axis=-1, keepdims=True)
-    second = jnp.sum(jnp.where(low, 0.0, powers), axis=-1, keepdims=True)
-    return powers * (live / jnp.where(low, first, second))
+    sums = dot(powers.astype(BF16), half_ones())
+    return powers * (live / sums)
 
 
 def feature_back(feature, grads):
-    low = low_half(feature.shape)
     product = feature * grads
-    first = jnp.sum(jnp.where(low, product, 0.0), axis=-1, keepdims=True)
-    second = jnp.sum(jnp.where(low, 0.0, product), axis=-1, keepdims=True)
-    return product - feature * jnp.where(low, first, second)
+    return product - feature * dot(product.astype(BF16), half_ones())
 
 
 class Rows:
@@ -477,10 +536,12 @@
     attn_out, fc_out, proj_out,
     normed_ref, qkv_ref, fq_ref, fk_ref, state_ref, mixed_ref, rden_ref, wo_ref, maps_ref, middle_ref, hidden_ref,
     attn_shard, feat_shard, fc_shard, proj_shard, feat_rows, norm_ref,
-    w_ref, feat_ref, pairs_ref, total_ref, picked_ref, cin, cout, chain_send, chain_recv, move_sem,
+    w_ref, fc_ref, proj_ref, feat_ref, pairs_ref, total_ref, picked_ref, cin, cout, chain_send, chain_recv, move_sem,
     *sems,
 ):
     X, Z, groups = sizes
+    net = Network(sizes)
+    greeted = net.greet(chained=True)
     lanes_here = heads * HD
     for j in range(3):
         attn_shard[:, 256 * j : 256 * j + 128] = wqkv_ref[j, :, 0:128].astype(BF16)
@@ -498,7 +559,6 @@
     fc_shard[...] = wfc_ref[...].astype(BF16)
     proj_shard[...] = wproj_ref[...].astype(BF16)
     norm_ref[...] = norm_in[...].astype(BF16).astype(F32)
-    net = Network(sizes)
     h = net.h
     rows, width = x_ref.shape
     chunks = rows // CHUNK
@@ -517,15 +577,17 @@
         )
     )
     push_middle, push_hidden = mover.plan(middle_ref, middle_out), mover.plan(hidden_ref, hidden_out)
-
-    net.barrier(chained=True)
-    shards = (attn_shard, feat_shard, fc_shard, proj_shard)
-    attn, feat, fc, proj = (
-        Gather(net, shard, buf, sems[2 * i], sems[2 * i + 1])
-        for i, (shard, buf) in enumerate(zip(shards, (w_ref, feat_ref, fc_out, proj_out)))
-    )
+    push_fc, push_proj = mover.plan(fc_ref, fc_out), mover.plan(proj_ref, proj_out)
+
+    pl.semaphore_wait(pltpu.get_barrier_semaphore(), greeted)
+    part = attn_shard.shape[0]
+    cuts = [pl.ds(0, part // 2), pl.ds(part // 2, part // 2)] if part % 32 == 0 else [pl.ds(0, part)]
+    feat = Gather(net, feat_shard, feat_ref, *sems[0:2])
+    fc, proj = Gather(net, fc_shard, fc_ref, *sems[2:4]), Gather(net, proj_shard, proj_ref, *sems[4:6])
+    attns = [Gather(net, attn_shard, w_ref, *sems[6 + 2 * i : 8 + 2 * i], rows) for i, rows in enumerate(cuts)]
     feat.begin()
-    attn.begin()
+    for attn in attns:
+        attn.begin()
 
     def first_norm(c, _):
         at = pl.ds(pl.multiple_of(c * CHUNK, CHUNK), CHUNK)
@@ -533,48 +595,52 @@
         normed_ref[at] = (center * scale * norm_ref[0:1] + norm_ref[1:2]).astype(BF16)
         return 0
 
-    feat.copy_own().wait()
-    attn.copy_own().wait()
+    for gather in (feat, *attns):
+        gather.copy_own().wait()
     feat_on, feat_in = feat.steps()
-    attn_on, attn_in = attn.steps()
-    for step in feat_on[: Z - 1] + attn_on[: Z - 1]:
-        step()
+    attn_rounds, attn_arrivals = zip(*(attn.steps() for attn in attns))
+    attn_on = [sum(steps, []) for steps in zip(*attn_rounds)]
+    attn_in = sum(attn_arrivals, [])
     lax.fori_loop(0, chunks, first_norm, 0)
     push_normed(0).start()
-    late = Z if (X, groups) == (2, 4) else 0
-    now = len(attn_on) - late
-    for step in attn_on[Z - 1 : now] + feat_on[Z - 1 :] + feat_in:
-        step()
-
-    maps_ref[...] = jnp.zeros_like(maps_ref)
-    low64 = low_half((HD, 128))
-    for i in range(X * Z):
-        for g in range(groups):
-            block = feat_ref[i // Z, i % Z, g].astype(F32)
-            for j in range(heads):
-                pairs_ref[g * heads + j, depth * i : depth * i + depth] = block[depth * j : depth * j + depth]
-    for g in range(groups):
-        for j in range(heads):
-            pair = pairs_ref[g * heads + j]
-            swapped = pltpu.roll(pair, HD, 1)
-            at = slice(HD * j, HD * j + HD), slice(128 * j, 128 * j + 128)
-            maps_ref[0, g, at[0], at[1]] = jnp.where(low64, pair, -swapped).astype(BF16)
-            maps_ref[1, g, at[0], at[1]] = jnp.where(low64, swapped, -pair).astype(BF16)
-    push_maps(0).start()
+    ahead = len(attn_on) - (1 if (X, groups) == (2, 4) else 0)
+    for k in range(ahead):
+        for step in feat_on[k] + attn_on[k]:
+            step()
+        if k == Z - 2:
+            fc.begin()
+        if k == len(feat_on) - 2:
+            for step in feat_on[-1] + feat_in:
+                step()
+            maps_ref[...] = jnp.zeros_like(maps_ref)
+            low64 = low_half((HD, 128))
+            for i in range(X * Z):
+                for g in range(groups):
+                    block = feat_ref[i // Z, i % Z, g].astype(F32)
+                    for j in range(heads):
+                        pairs_ref[g * heads + j, depth * i : depth * i + depth] = block[depth * j : depth * j + depth]
+            for g in range(groups):
+                for j in range(heads):
+                    pair = pairs_ref[g * heads + j]
+                    swapped = pltpu.roll(pair, HD, 1)
+                    at = slice(HD * j, HD * j + HD), slice(128 * j, 128 * j + 128)
+                    maps_ref[0, g, at[0], at[1]] = jnp.where(low64, pair, -swapped).astype(BF16)
+                    maps_ref[1, g, at[0], at[1]] = jnp.where(low64, swapped, -pair).astype(BF16)
+            push_maps(0).start()
 
     turns = groups * chunks
     slots = {}
-    if late:
-        for k, step in enumerate(attn_on[now:]):
-            slots.setdefault(k, []).append(step)
-        slots.setdefault(2 * chunks, []).extend(attn_in)
+    if ahead < len(attn_on):
+        slots[2] = list(attn_on[ahead])
+        slots[2 * chunks] = list(attn_in)
     else:
         slots[0] = list(attn_in)
-    slots.setdefault(1, []).extend([fc.begin, proj.begin])
     fc_on, fc_in = fc.steps()
     proj_on, proj_in = proj.steps()
-    for k, pair in enumerate(zip(fc_on, proj_on)):
-        slots.setdefault(4 + k * (2 * turns - 6) // len(fc_on), []).extend(pair)
+    slots.setdefault(PROJ_BEGIN, []).append(proj.begin)
+    for on, turns_at in ((fc_on, FC_TURNS), (proj_on, PROJ_TURNS)):
+        for k, steps in enumerate(on):
+            slots.setdefault(turns_at[min(k, len(turns_at) - 1)], []).extend(steps)
     mix_slots = {k - turns: items for k, items in slots.items() if k >= turns}
     last = seq.last()
 
@@ -676,14 +742,18 @@
     lax.fori_loop(0, chunks, close, 0)
     push_middle(0).start()
     push_hidden(0).start()
-    for step in fc_in + proj_in:
+    for step in fc_in:
         step()
     fc.copy_own().wait()
+    push_fc(0).start()
+    for step in proj_in:
+        step()
     proj.copy_own().wait()
+    push_proj(0).start()
     chain.finish(groups)
-    for gather in (attn, feat, fc, proj):
+    for gather in (*attns, feat, fc, proj):
         gather.finish()
-    for push in (push_normed, push_wo, push_maps, push_attn, push_middle, push_hidden):
+    for push in (push_normed, push_wo, push_maps, push_attn, push_middle, push_hidden, push_fc, push_proj):
         push(0).wait()
     for push in (push_qkv, push_fq, push_fk, push_state, push_mixed, push_rden):
         for g in range(groups):
@@ -692,65 +762,90 @@
 
 def feed_forward(
     sizes, hidden_ref, dy_ref, norm_ref, fc_in, proj_in, middle_in,
-    block_out, dmid_out, datt_out, gfc_out, gproj_out, gnorm_ref,
+    block_out, dmid_out, datt_out, gfc_sums, gproj_sums, gnorm_ref,
     fc_ref, proj_ref, middle_ref, out_ref, datt_ref, gfc_ref, gproj_ref, branch_ref, dhid_ref, act_ref, dpre_ref,
     move_sem, fc_sem, proj_sem, *scratch,
 ):
     X, Z, H = sizes
     net = Network(sizes)
-    part, width = fc_ref.shape[3:]
+    chunks, size, width = fc_ref.shape
+    part = gfc_ref.shape[3]
     rows = hidden_ref.shape[0]
     tile = 256
     tiles = rows // tile
-    turns = X * Z
-
-    def place(i):
-        off = Z - 1 - lax.rem(i, Z)
-        return lax.rem(net.dp + 1 + i // Z, X), net.behind(off), off
-
-    def fetch(i):
-        dp, b, _ = place(i)
-        at = dp * Z + b
+    paired = (X, H) == (2, 4)
+    odd = lax.rem(net.h, 2)
+
+    if paired:
+        far, near = (lax.rem(net.dp + 1, 2), net.dp), (flip_bit(net.h, 1), net.h)
+        kinds = {"both": (far[0], near[0]), "x": (far[0], near[1]), "y": (far[1], near[0]), "own": (far[1], near[1])}
+        plan = [[("both", off) for off in (3, 2, 1, 0)]]
+        plan += [[(kind, off) for off in offs for kind in ("x", "y")] for offs in ((3, 2), (1, 0))]
+        plan += [[("own", off) for off in (3, 2, 1, 0)]]
+        places = []
+        for items in plan:
+            places.append([])
+            for kind, off in items:
+                dp, h = kinds[kind]
+                places[-1] += [(dp, net.behind(off), h), (dp, net.behind(off), flip_bit(h, 0))]
+    else:
+        places = [
+            [(lax.rem(net.dp + 1 + i, X), b, h) for b in range(Z) for h in range(H)] for i in range(X)
+        ]
+
+    def fetch(i, s):
+        at = pl.ds(part * s, part)
         return (
-            pltpu.make_async_copy(fc_in.at[dp, b], fc_ref.at[dp, b], fc_sem.at[at]),
-            pltpu.make_async_copy(proj_in.at[dp, b], proj_ref.at[dp, b], proj_sem.at[at]),
+            pltpu.make_async_copy(fc_in.at[places[i][s]], fc_ref.at[i, at], fc_sem.at[i, s]),
+            pltpu.make_async_copy(proj_in.at[places[i][s]], proj_ref.at[i, at], proj_sem.at[i, s]),
         )
 
-    for i in range(turns):
-        for copy in fetch(i):
-            copy.start()
+    for i in range(chunks):
+        for s in range(size // part):
+            for copy in fetch(i, s):
+                copy.start()
     mover = Mover(move_sem)
     pull_middle = mover.plan(middle_in, middle_ref)
     pull_middle(0).start()
     net.barrier()
-    scatters = [Scatter(net, gfc_ref, *scratch[:3]), Scatter(net, gproj_ref, *scratch[3:])]
+    scatters = [
+        Scatter(net, Keep(gfc_sums), gfc_ref, *scratch[:3]),
+        Scatter(net, Keep(gproj_sums), gproj_ref, *scratch[3:]),
+    ]
     branch_ref[...] = jnp.zeros_like(branch_ref)
     dhid_ref[...] = jnp.zeros_like(dhid_ref)
 
+    turns = chunks * tiles
     slots = {}
-    if (X, H) == (2, 4):
+    if paired:
         own, first, second, both = scatters[0].early_sets()
+
+        def add(slot, chosen, off):
+            for scatter in scatters:
+                slots.setdefault(slot, []).append(functools.partial(scatter.step, chosen, off))
+
         for k in range(Z):
             off = Z - 1 - k
-            for scatter in scatters:
-                slots.setdefault(k + 1, []).append(functools.partial(scatter.step, both, off))
-                for late, chosen in ((1, second), (1, first), (2, own)):
-                    slots.setdefault(Z + k + late, []).append(functools.partial(scatter.step, chosen, off))
+            add(tiles + k, both, off)
+            add((2 + k // 2) * tiles + k % 2, second, off)
+            add((2 + k // 2) * tiles + 2 + k % 2, first, off)
+            add(turns + k, own, off)
     else:
         for scatter in scatters:
             for chosen in reversed(scatter.early_sets()):
                 for off in reversed(range(Z)):
                     slots.setdefault(turns, []).append(functools.partial(scatter.step, chosen, off))
 
-    def block(i, _):
-        dp, b, off = place(i)
-        for copy in fetch(i):
-            copy.wait()
-
-        def rowed(c, _):
+    for i in range(chunks):
+        for s in range(size // part):
+            for copy in fetch(i, s):
+                copy.wait()
+        here = {k - i * tiles: items for k, items in slots.items() if i * tiles <= k < (i + 1) * tiles}
+
+        def rowed(c, _, i=i, here=here):
+            run_at(here, c, tiles)
             at = pl.ds(pl.multiple_of(c * tile, tile), tile)
-            fc = fc_ref[dp, b].reshape(H * part, width)
-            proj = proj_ref[dp, b].reshape(H * part, width)
+            fc, proj = fc_ref[i], proj_ref[i]
             pre = dot_nt(hidden_ref[at], fc)
             square = pre * pre
             inner = jnp.tanh(0.7978845608 * pre * (1.0 + 0.044715 * square))
@@ -765,23 +860,32 @@
             return 0
 
         lax.fori_loop(0, tiles, rowed, 0)
-        run_at(slots, i, turns)
-        gproj_ref[dp, b] = dot_tn(act_ref[...], dy_ref[...]).astype(BF16).reshape(H, part, width)
-        gfc_ref[dp, b] = dot_tn(dpre_ref[...], hidden_ref[...]).astype(BF16).reshape(H, part, width)
+        for grads, left, right in ((gproj_ref, act_ref, dy_ref), (gfc_ref, dpre_ref, hidden_ref)):
+            half = size // 2
+            for at in (0, half):
+                grad = dot_tn(left[:, at : at + half], right[...]).astype(BF16)
+                for s in range(half // part):
+                    grads[places[i][at // part + s]] = grad[part * s : part * s + part]
         for scatter in scatters:
-            scatter.begin(lambda dp_at, h_at: dp_at == dp, [off])
-        return 0
-
-    lax.fori_loop(0, turns, block, 0)
+            if not paired:
+                scatter.begin(lambda dp_at, h_at, i=i: dp_at == places[i][0][0])
+                continue
+            for kind, off in plan[i]:
+                if kind == "both" or kind == "own":
+                    scatter.copy(both if kind == "both" else own, off, scatter.last).start()
+                else:
+                    chosen = (first, second) if kind == "y" else (second, first)
+                    pl.when(odd == 0)(scatter.copy(chosen[0], off, scatter.last).start)
+                    pl.when(odd == 1)(scatter.copy(chosen[1], off, scatter.last).start)
 
     gnorm_ref[...] = jnp.zeros_like(gnorm_ref)
     pull_middle(0).wait()
-    late = [slots[k] for k in sorted(slots) if k >= turns]
-    late_slots = dict(enumerate(late[: tiles - 1]))
-    late_slots[tiles - 1] = [item for items in late[tiles - 1 :] for item in items]
+    late_slots = {min(k - turns, tiles - 1): [] for k in slots if k >= turns}
+    for k in sorted(slots):
+        if k >= turns:
+            late_slots[min(k - turns, tiles - 1)] += slots[k]
 
     def close(c, _):
-        run_at(late_slots, c, tiles)
         at = pl.ds(pl.multiple_of(c * tile, tile), tile)
         middle = middle_ref[at]
         out_ref[at] = (middle + branch_ref[at]).astype(BF16)
@@ -791,14 +895,13 @@
         datt_ref[at] = dmid.astype(BF16)
         gnorm_ref[2:3] += gain
         gnorm_ref[3:4] += shift
+        run_at(late_slots, c, tiles)
         return 0
 
     lax.fori_loop(0, tiles, close, 0)
     pushes = [mover.plan(*pair) for pair in ((out_ref, block_out), (middle_ref, dmid_out), (datt_ref, datt_out))]
     for push in pushes:
         push(0).start()
-    gfc_out[...] = scatters[0].result()
-    gproj_out[...] = scatters[1].result()
     for push in pushes:
         push(0).wait()
     for scatter in scatters:
@@ -806,12 +909,12 @@
 
 
 def attention_backward(
-    sizes, heads, depth, len_ref, norm_ref, gnorm_in, gfc_ref, gproj_ref, x_in, normed_in, qkv_in, fq_in, fk_in,
+    sizes, heads, depth, len_ref, norm_ref, gnorm_in, gfc_sums, gproj_sums, x_in, normed_in, qkv_in, fq_in, fk_in,
     state_in, mixed_in, rden_in, wo_in, maps_in, w_in, datt_in, dmid_in,
-    dx_out, gattn_out, gfeat_out, sums_out,
+    dx_out, gattn_out, gfeat_out, gfc_ref, gproj_ref, sums_out,
     x_ref, normed_ref, qkv_ref, fq_ref, fk_ref, state_ref, mixed_ref, rden_ref, wo_ref, maps_ref, datt_ref, dmid_ref,
     w_ref, gw_ref, gnorm_ref, featsum_ref, featpart_ref,
-    dne_ref, back_ref, total_ref, picked_ref, dqkv_ref, dnormed_ref, gsum_ref, cin, cout, chain_send, chain_recv,
+    dne_ref, back_ref, total_ref, picked_ref, dnormed_ref, gsum_ref, cin, cout, chain_send, chain_recv,
     w_sem, move_sem, *scratch,
 ):
     X, Z, H = sizes
@@ -856,12 +959,19 @@
         for pull in group_pulls:
             pull(backwards(i)).start()
     pull_weight(0).start()
+    pull_weight(1).start()
     pull_normed(0).start()
     pull_x(0).start()
     pull_dmid(0).start()
-    net.barrier(chained=True)
-    attn = Scatter(net, gw_ref, *scratch[:3])
-    feat = Scatter(net, featpart_ref, *scratch[3:6])
+    net.barrier(whole_plane=True)
+    fc_along, proj_along = Along(net, gfc_sums, *scratch[0:3]), Along(net, gproj_sums, *scratch[3:6])
+    for off in reversed(range(1, Z)):
+        fc_along.copy(off).start()
+        proj_along.copy(off).start()
+    attn_along, feat_along = Along(net, *scratch[6:10]), Along(net, *scratch[10:14])
+    attn = Scatter(net, attn_along, gw_ref, *scratch[14:17])
+    feat = Scatter(net, feat_along, featpart_ref, *scratch[17:20])
+    odd = lax.rem(h, 2)
 
     down = lax.broadcasted_iota(jnp.int32, (256, 256), 0) // HD
     across = lax.broadcasted_iota(jnp.int32, (256, 256), 1) // HD
@@ -921,14 +1031,8 @@
 
     def group(i, _):
         g = backwards(i)
-        slot = lax.rem(i, 2)
         for pull in group_pulls:
             pull(g).wait()
-        pull_weight(i).wait()
-
-        @pl.when(i < groups - 1)
-        def _():
-            pull_weight(i + 1).start()
 
         gsum_ref[...] = jnp.zeros_like(gsum_ref)
 
@@ -962,11 +1066,17 @@
             gsum_ref[0] += dot_tn(qkv_ref[g, at, 0:256], du_q)
             gsum_ref[1] += dot_tn(qkv_ref[g, at, 256:512], du_k)
             dqkv = jnp.concatenate([dq, dk, dv], axis=1)
-            dqkv_ref[at] = dqkv
-            dnormed_ref[at] += dot_nt(dqkv, w_ref[slot].reshape(width, width))
+            qkv_ref[g, at] = dqkv
             return 0
 
         lax.fori_loop(0, chunks, piece, 0)
+        if (X, H) == (2, 4):
+
+            @pl.when((i == groups - 1) & (odd == 1))
+            def _():
+                for off in reversed(range(Z)):
+                    attn.step(attn.early_sets()[1], off)
+
         low64 = low_half((HD, 128))
         for j in range(heads):
             sums = [gsum_ref[side, HD * j : HD * j + HD, 128 * j : 128 * j + 128] for side in range(2)]
@@ -975,7 +1085,7 @@
             for k in range(X * Z):
                 featsum_ref[k // Z, k % Z, g, depth * j : depth * j + depth] = pair[depth * k : depth * k + depth]
         for third in range(3):
-            grad = dot_tn(normed_ref[...], dqkv_ref[:, 256 * third : 256 * third + 256])
+            grad = dot_tn(normed_ref[...], qkv_ref[g, :, 256 * third : 256 * third + 256])
             at = 256 * third
             gw_ref[:, :, g, :, at : at + 128] = grad[:, 0:128].astype(BF16).reshape(shape)
             beside = gw_ref[:, :, g, :, at + 128 : at + 256].reshape(width, 128)
@@ -986,10 +1096,15 @@
 
         if (X, H) == (2, 4):
 
-            @pl.when(i == groups - 1)
+            @pl.when(i == groups - 2)
             def _():
                 for off in reversed(range(Z)):
                     attn.step(attn.early_sets()[3], off)
+
+                @pl.when(odd == 0)
+                def _():
+                    for off in reversed(range(Z)):
+                        attn.step(attn.early_sets()[2], off)
 
         return 0
 
@@ -1001,19 +1116,49 @@
     feat.begin()
 
     gnorm_ref[...] = gnorm_in[...]
+    turns = groups * chunks
+    slots = {}
+    for scatter in (attn, feat):
+        own, *others = scatter.early_sets()
+        for off in reversed(range(Z)):
+            late = (Z - 1 - off) * turns // Z
+            turn = {chosen: functools.partial(scatter.step, chosen, off) for chosen in (own, *others)}
+            if scatter is attn and (X, H) == (2, 4):
+
+                def cross(turn=turn):
+                    pl.when(odd == 0)(turn[others[0]])
+                    pl.when(odd == 1)(turn[others[1]])
+
+                slots.setdefault(1 + late // 4, []).append(cross)
+                slots.setdefault(4 + late * 3 // 4, []).append(turn[own])
+            else:
+                for k, chosen in enumerate(reversed(others)):
+                    slots.setdefault(1 + 4 * k if len(others) == 3 else 1, []).append(turn[chosen])
+                slots.setdefault(turns - 2, []).append(turn[own])
+
+    def through(i, _):
+        slot = lax.rem(i, 2)
+        pull_weight(i).wait()
+
+        def piece(c, _):
+            run_at(slots, i * chunks + c, turns)
+            at = pl.ds(pl.multiple_of(c * CHUNK, CHUNK), CHUNK)
+            dnormed_ref[at] += dot_nt(qkv_ref[backwards(i), at], w_ref[slot].reshape(width, width))
+            return 0
+
+        lax.fori_loop(0, chunks, piece, 0)
+
+        @pl.when(i < groups - 2)
+        def _():
+            pull_weight(i + 2).start()
+
+        return 0
+
+    lax.fori_loop(0, groups, through, 0)
     pull_x(0).wait()
     pull_dmid(0).wait()
-    slots = {}
-    for scatter in (attn, feat):
-        early = list(reversed(scatter.early_sets()))
-        if scatter is attn and (X, H) == (2, 4):
-            early = early[1:]
-        for k, chosen in enumerate(early):
-            for off in reversed(range(Z)):
-                slots.setdefault(min(k, chunks - 1), []).append(functools.partial(scatter.step, chosen, off))
 
     def close(c, _):
-        run_at(slots, c, chunks)
         at = pl.ds(pl.multiple_of(c * CHUNK, CHUNK), CHUNK)
         gain_row = norm_ref[0:1].astype(BF16).astype(F32)
         back, gain, shift = norm_backward(x_ref[at].astype(F32), gain_row, dnormed_ref[at])
@@ -1025,18 +1170,20 @@
     lax.fori_loop(0, chunks, close, 0)
     push_dx(0).start()
     square = jnp.zeros((1, 128), F32)
-    gattn_out[...] = attn.result()
-    gfeat_out[...] = feat.result()
+    gfc_ref[...] = fc_along.result()
+    gproj_ref[...] = proj_along.result()
+    gattn_out[...] = attn_along.result()
+    gfeat_out[...] = feat_along.result()
     for ref in (gattn_out, gfeat_out, gfc_ref, gproj_ref):
         column = jnp.sum(ref[...] * ref[...], axis=0, keepdims=True)
         for at in range(0, column.shape[1], 128):
             square = square + column[:, at : at + 128]
     gnorm_ref[4:5, 0:128] = square
-    sums_out[...] = total_over_all(net, gnorm_ref[...], *scratch[6:])
+    sums_out[...] = total_over_all(net, gnorm_ref[...], *scratch[20:])
     push_dx(0).wait()
     chain.finish(groups)
-    for scatter in (attn, feat):
-        scatter.finish()
+    for moving in (attn, feat, fc_along, proj_along, attn_along, feat_along):
+        moving.finish()
 
 
 def adamw_update(master, first_mom, second_mom, grad_in, factor, step_rate, decay_rate):
@@ -1196,31 +1343,33 @@
             VMEM((FEAT_ROWS, 128), F32),
             VMEM((4, width), F32),
         ]
-        + [VMEM(big, BF16), VMEM(small, BF16), VMEM((H * heads, HD, 128), F32), VMEM((heads, 128, 256), F32)]
+        + [VMEM(big, BF16), VMEM(big, BF16), VMEM(big, BF16), VMEM(small, BF16), VMEM((H * heads, HD, 128), F32), VMEM((heads, 128, 256), F32)]
         + chain_scratch
-        + [dma((6 + 6 * H,))]
-        + [sem for _ in range(4) for sem in gather_sems(sizes)],
+        + [dma((8 + 6 * H,))]
+        + [sem for _ in range(5) for sem in gather_sems(sizes)],
         0,
         "attention_forward",
         10**10,
         hbm_out=range(14),
     )
 
-    block_out, d_middle, d_att, g_fc, g_proj, g_norm = call(
+    turns = 4 if (X, H) == (2, 4) else X
+    size = X * Z * H * part // turns
+    block_out, d_middle, d_att, fc_sums, proj_sums, g_norm = call(
         functools.partial(feed_forward, sizes),
         [
             struct((rows, width), BF16),
             struct((rows, width), F32),
             struct((rows, width), BF16),
-            struct((part, width), F32),
-            struct((part, width), F32),
+            struct((Z, part, width), BF16),
+            struct((Z, part, width), BF16),
             struct((8, width), F32),
         ],
         0,
         [hidden, cotangent, norm_params, fc_w, proj_w, middle],
         [
-            VMEM(big, BF16),
-            VMEM(big, BF16),
+            VMEM((turns, size, width), BF16),
+            VMEM((turns, size, width), BF16),
             VMEM((rows, width), F32),
             VMEM((rows, width), BF16),
             VMEM((rows, width), BF16),
@@ -1228,11 +1377,11 @@
             VMEM(big, BF16),
             VMEM((rows, width), F32),
             VMEM((rows, width), F32),
-            VMEM((rows, H * part), BF16),
-            VMEM((rows, H * part), BF16),
+            VMEM((rows, size), BF16),
+            VMEM((rows, size), BF16),
             dma((4,)),
-            dma((X * Z,)),
-            dma((X * Z,)),
+            dma((turns, size // part)),
+            dma((turns, size // part)),
         ]
         + scatter_scratch(sizes, (part, width)) * 2,
         1,
@@ -1243,17 +1392,19 @@
     )
 
     pulled = [struct((rows, width), BF16)] + held[:9] + [struct((rows, width), BF16), struct((rows, width), F32)]
-    block_in_grad, g_attn, g_feat, sums = call(
+    block_in_grad, g_attn, g_feat, g_fc, g_proj, sums = call(
         functools.partial(attention_backward, sizes, heads, depth),
         [
             struct((rows, width), F32),
             struct((part, width), F32),
             struct((FEAT_ROWS, 128), F32),
+            struct((part, width), F32),
+            struct((part, width), F32),
             struct((8, width), F32),
         ],
         1,
         [
-            seq_len, norm_params, g_norm, g_fc, g_proj, block_in, normed, qkv, fq, fk, states, mixed, rden, wo, maps,
+            seq_len, norm_params, g_norm, fc_sums, proj_sums, block_in, normed, qkv, fq, fk, states, mixed, rden, wo, maps,
             attn_w, d_att, d_middle,
         ],
         [VMEM(item.shape, item.dtype) for item in pulled]
@@ -1267,12 +1418,16 @@
             VMEM((H, heads, chunks, 128, 256), BF16),
             VMEM((heads, 128, 256), F32),
             chain_scratch[0],
-            VMEM((rows, width), BF16),
             VMEM((rows, width), F32),
             VMEM((2, 256, 128 * heads), F32),
         ]
         + chain_scratch[1:]
         + [dma((2,)), dma((6 + 7 * H,))]
+        + along_scratch(sizes, (part, width)) * 2
+        + [VMEM((Z, part, width), BF16)]
+        + along_scratch(sizes, (part, width))
+        + [VMEM((Z, FEAT_ROWS, 128), BF16)]
+        + along_scratch(sizes, (FEAT_ROWS, 128))
         + scatter_scratch(sizes, (part, width))
         + scatter_scratch(sizes, (FEAT_ROWS, 128))
         + total_scratch(sizes, (8, width)),

time: 304 us -> 264 us (0.87)
  Pallas kernels: 301 us -> 262 us
    pallas_call x4, Pallas kernels: 301 us -> 262 us  [call(): pl.pallas_call(kernel, out_shape=tuple(outs), in_specs=specs, out_specs=t...]
where the time goes in v3:
time: 264 us; the launch traced here: 263 us
  Pallas kernels  262 us (99%)
    pallas_call x4, Pallas kernels, call(): pl.pallas_call(kernel, out_shape=tuple(outs), in_specs=specs, out_specs=t...  262 us

profile of v3, /device:TPU:0, one launch (start us, length us, event | category | flops | bytes accessed | tf_op | source)
XLA Modules:
  0.0 263.4 jit_solution(11751076370002887475)
XLA Ops:
  0.7 96.5 %attention_forward.1 = (bf16[1024,768]{1,0:T(8,128)(2,1)}, bf16[4,1024,768]{2,1,0:T(8,128)(2,1)}, bf16[4,1024,384]{2,1,0:T(8,128)(2,1)}, bf16[4,1024,384]{2,1,0:...) custom-call(s32[1,2]{1,0:T(1,128)} %len_ref.3, ...), custom_call_target="tpu_custom_call" | custom-call | flops 10000000000 | bytes 45998088 | tf_op jit(solution)/shard_map/attention_forward/pallas_call | solution.py:1266
  97.2 62.6 %feed_forward.1 = (bf16[1024,768]{1,0:T(8,128)(2,1)}, f32[1024,768]{1,0:T(8,128)}, bf16[1024,768]{1,0:T(8,128)(2,1)}, bf16[4,96,768]{2,1,0:T(8,128)(2,1)}, bf16[...) custom-call(bf16[1024,768]{1,0:T(8,128)(2,1)} %get-tuple-element.82.hidden_ref, bf16[1024,768]{1,0:T(8,128)(2,1)} %dy_ref.1, ...), custom_call_target="tpu_custom_call" | custom-call | flops 30000001024 | bytes 23236608 | tf_op jit(solution)/shard_map/feed_forward/pallas_call | solution.py:1266
  159.8 94.3 %attention_backward.1 = (f32[1024,768]{1,0:T(8,128)}, f32[96,768]{1,0:T(8,128)}, f32[32,128]{1,0:T(8,128)}, f32[96,768]{1,0:T(8,128)}, f32[96,768]{1,0:T(8,128)}, /*index=5*/f32[8,768]{1,0:T(8,128)}) custom-call(s32[1,2]{1,0:T(1,128)} %len_ref.3, f32[4,768]{1,0:T(4,128)} %refs_5_.1, f32[8,768]{1,0:T(8,128)} %get-tuple-element.86.gnorm_in, ...), custom_call_target="tpu_custom_call" | custom-call | flops 20000000000 | bytes 40939528 | tf_op jit(solution)/shard_map/attention_backward/pallas_call | solution.py:1266
  254.1 8.1 %update.1 = (f32[8,128]{1,0:T(8,128)}, f32[3,96,192]{2,1,0:T(8,128)}, f32[192,96]{1,0:T(8,128)}, f32[3,2,512]{2,1,0:T(2,128)}, f32[96,768]{1,0:T(8,128)}, /*inde...) custom-call(f32[8,768]{1,0:T(8,128)} %get-tuple-element.101.sums_ref, ...), custom_call_target="tpu_custom_call" | custom-call | flops 10000000 | bytes 16277504 | tf_op jit(solution)/shard_map/update/pallas_call | solution.py:1266
  262.2 1.2 slice.3
